TPU v7x, 32 devices: a whole 2x2x4 slice. The times are simulated.
32 devices in a mesh: blk: 4 (over y, x), inner: 8 (over z, core).
Axes of the slice: x: 2, y: 2, z: 4, core: 2. Of those that a mesh axis runs over, the one named last changes fastest.
Arguments:
- queries: bfloat16 [4096, 768], P(('blk', 'inner')), may hold values from -16 to 16
- keys: bfloat16 [4096, 768], P(('blk', 'inner')), may hold values from -16 to 16
- values: bfloat16 [4096, 768], P(('blk', 'inner')), may hold values from -6 to 6
- valid: int32 [4096], P(('blk', 'inner')), may hold values 0 or 1
- out_weight: bfloat16 [768, 768], replicated, may hold values from -0.21875 to 0.21875
Outputs:
- mixed: bfloat16 [4096, 768], P(('blk', 'inner'))
All inputs are finite; a program needn't handle non-finite values. No bound on the sum of `valid` on one device may be relied on, other than what follows from the above.
Results may differ from a plain program's by a relative error of at most 0.015.
Values may be sent and summed in bfloat16 or wider, within the bound.
No kernel may reach another device: no remote copies, remote signals or barrier semaphores. Data moves between devices by JAX's collectives and lax.ppermute only.
A program may use at most 128 MiB of HBM per device.

v0:
```python
import jax
import jax.numpy as jnp
from jax import lax
from jax.sharding import PartitionSpec as P

HEADS = 12
HEAD_DIM = 64


def make_fold(query_all):
    query_count = query_all.shape[0]
    query_heads = query_all.reshape(query_count, HEADS, HEAD_DIM)
    score_scale = HEAD_DIM ** (-0.5)

    def attend(state_now, piece, start):
        key_piece, value_piece, flag_piece = piece
        piece_rows = key_piece.shape[0]
        block_rows = 128
        count = piece_rows // block_rows
        key_blocks = key_piece.reshape(count, block_rows, HEADS, HEAD_DIM)
        value_blocks = value_piece.reshape(count, block_rows, HEADS, HEAD_DIM)
        flag_blocks = flag_piece.reshape(count, block_rows)

        def one_block(carry, item):
            run_max, row_total, weighted = carry
            key_heads, value_heads, flag_block = item
            scores = (
                jnp.einsum(
                    "qhd,khd->hqk", query_heads, key_heads, preferred_element_type=jnp.float32
                )
                * score_scale
            )
            scores = jnp.where(flag_block[None, None, :] > 0, scores, -1e30)
            new_max = jnp.maximum(run_max, jnp.max(scores, axis=-1))
            shrink = jnp.exp(run_max - new_max)
            chances = jnp.exp(scores - new_max[..., None]).astype(jnp.bfloat16)
            row_total = row_total * shrink + jnp.sum(chances, axis=-1, dtype=jnp.float32)
            weighted = weighted * shrink[..., None] + jnp.einsum(
                "hqk,khd->hqd", chances, value_heads, preferred_element_type=jnp.float32
            )
            return ((new_max, row_total, weighted), None)

        state_end, unused = lax.scan(one_block, state_now, (key_blocks, value_blocks, flag_blocks))
        return state_end

    starting = (
        jnp.zeros((HEADS, query_count), jnp.float32),
        jnp.zeros((HEADS, query_count), jnp.float32),
        jnp.zeros((HEADS, query_count, HEAD_DIM), jnp.float32),
    )
    return (attend, starting)


def settle(top, row_total, weighted):
    return weighted / (jnp.exp(-top) + row_total)[..., None]


def combine_loop(state_end, own_rows):
    run_max, row_total, weighted = state_end
    top = lax.pmax(run_max, "blk")
    shrink = jnp.exp(run_max - top)
    total_own, weighted_own = (
        lax.psum_scatter(row_total * shrink, "blk", scatter_dimension=1, tiled=True),
        lax.psum_scatter(weighted * shrink[..., None], "blk", scatter_dimension=1, tiled=True),
    )
    top_own = lax.dynamic_slice_in_dim(top, lax.axis_index("blk") * own_rows, own_rows, 1)
    return settle(top_own, total_own, weighted_own)


def on_device(queries, keys, values, valid, out_weight):
    own_rows = queries.shape[0]
    width = queries.shape[1]
    flags = valid.astype(jnp.bfloat16)
    query_all = lax.all_gather(queries, "blk", axis=0, tiled=True)
    attend, starting = make_fold(query_all)
    state_end = attend(
        starting,
        (
            lax.all_gather(keys, "inner", axis=0, tiled=True),
            lax.all_gather(values, "inner", axis=0, tiled=True),
            lax.all_gather(flags, "inner", axis=0, tiled=True),
        ),
        jnp.int32(0),
    )
    attended = combine_loop(state_end, own_rows)
    attended = jnp.transpose(attended, (1, 0, 2)).reshape(own_rows, width).astype(jnp.bfloat16)
    return jnp.dot(attended, out_weight, preferred_element_type=jnp.float32).astype(jnp.bfloat16)


def solution(mesh):
    return jax.shard_map(
        on_device,
        mesh=mesh,
        in_specs=(
            P(("blk", "inner"), None),
            P(("blk", "inner"), None),
            P(("blk", "inner"), None),
            P(("blk", "inner")),
            P(),
        ),
        out_specs=P(("blk", "inner"), None),
        check_vma=False,
    )
```

profile of v0, /device:TPU:0, one launch (start us, length us, event | category | flops | bytes accessed | tf_op | source)
XLA Modules:
  0.0 232.7 jit_solution(11879444621232085924)
XLA Ops:
  8.1 15.1 %all_gather.14 = bf16[512,768]{1,0:T(8,128)(2,1)} all-gather(bf16[128,768]{1,0:T(8,128)(2,1)} %param.7), channel_id=1, replica_groups=mesh['blk'=4,'inner'=8] {'blk'}, dimensions={0}, use_global_device_ids=true | all-gather | bytes 983040 | tf_op jit(solution)/shard_map/all_gather | solution.py:74
  24.7 11.9 %all-gather = bf16[8,1,128]{2,1,0:T(2,128)(2,1)S(1)} all-gather(bf16[1,1,128]{2,1,0:T(2,128)(2,1)S(1)} %convert_bitcast_fusion), channel_id=1, replica_groups=mesh['blk'=4,'inner'=8] {'inner'}, dimensions={0}, use_global_device_ids=true | all-gather | bytes 2304 | tf_op jit(solution)/shard_map/all_gather | solution.py:81
  36.8 2.6 %copy.15 = bf16[1024,768]{0,1:T(8,128)(2,1)} copy(bf16[1024,768]{1,0:T(8,128)(2,1)} %all-gather.4.cloned.1.call-done) | data formatting | bytes 3145728 | tf_op jit(solution)/shard_map/all_gather | solution.py:79
  42.8 20.3 %all-gather.6.cloned.1.call-done = bf16[1024,768]{1,0:T(8,128)(2,1)} async-done(((bf16[128,768]{1,0:T(8,128)(2,1)}), bf16[1024,768]{1,0:T(8,128)(2,1)}) %all-gather.6.cloned.1.call-update) | async-done | bytes 1572880 | tf_op jit(solution)/shard_map/all_gather | solution.py:80
  69.1 82.5 %while.15 = (s32[]{:T(128)}, f32[12,512]{1,0:T(8,128)}, f32[12,512]{1,0:T(8,128)}, f32[12,512,64]{1,2,0:T(8,128)S(1)}, bf16[8,128]{1,0:T(8,128)(2,1)S(1)}, /*ind...) while((s32[]{:T(128)}, f32[12,512]{1,0:T(8,128)}, ...), condition=%wide.region_3.4_spmd.clone, body=%wide.region_0.3_spmd.clone.sunk | while | flops 212760960 | bytes 27035620 | solution.py:43
  69.1 3.9 %bitcast_reduce_fusion.2 = (f32[12,512]{1,0:T(8,128)}, f32[12,128,512]{2,1,0:T(8,128)}) fusion(pred[128]{0:T(512)(128)(4,1)S(1)} %compare_bitcast_fusion.2, bf16[512,12,64]{0,2,1:T(8,128)(2,1)S(1)} %get-tuple-element.200, bf16[8,128,12,64]{1,3,2,0:T(8,128)(2,1)} %get-tuple-element.199, s32[]{:T(128)} %get-tuple-element.184), kind=kOutput, calls=%fused_computation.1.clone.1 | convolution fusion | flops 103016448 | bytes 4153984 | tf_op jit(solution)/shard_map/while/body/eval_jaxpr/qhd,khd->hqk/dot_general | solution.py:28
  73.8 2.8 %convert_reduce_fusion.2 = f32[12,512]{1,0:T(8,128)S(1)} fusion(f32[12,512]{1,0:T(8,128)S(1)} %select_maximum_fusion.2, f32[12,128,512]{2,1,0:T(8,128)} %get-tuple-element.171, pred[128]{0:T(512)(128)(4,1)S(1)} %compare_bitcast_fusion.2), kind=kLoop, calls=%fused_computation.4.clone.1 | loop fusion | flops 4712448 | bytes 3195008 | tf_op jit(solution)/shard_map/while/body/eval_jaxpr/reduce_sum | solution.py:37
  79.4 3.9 %bitcast_reduce_fusion.2 = (f32[12,512]{1,0:T(8,128)}, f32[12,128,512]{2,1,0:T(8,128)}) fusion(pred[128]{0:T(512)(128)(4,1)S(1)} %compare_bitcast_fusion.2, bf16[512,12,64]{0,2,1:T(8,128)(2,1)S(1)} %get-tuple-element.200, bf16[8,128,12,64]{1,3,2,0:T(8,128)(2,1)} %get-tuple-element.199, s32[]{:T(128)} %get-tuple-element.184), kind=kOutput, calls=%fused_computation.1.clone.1 | convolution fusion | flops 103016448 | bytes 4153984 | tf_op jit(solution)/shard_map/while/body/eval_jaxpr/qhd,khd->hqk/dot_general | solution.py:28
  84.1 2.8 %convert_reduce_fusion.2 = f32[12,512]{1,0:T(8,128)S(1)} fusion(f32[12,512]{1,0:T(8,128)S(1)} %select_maximum_fusion.2, f32[12,128,512]{2,1,0:T(8,128)} %get-tuple-element.171, pred[128]{0:T(512)(128)(4,1)S(1)} %compare_bitcast_fusion.2), kind=kLoop, calls=%fused_computation.4.clone.1 | loop fusion | flops 4712448 | bytes 3195008 | tf_op jit(solution)/shard_map/while/body/eval_jaxpr/reduce_sum | solution.py:37
  89.7 3.9 %bitcast_reduce_fusion.2 = (f32[12,512]{1,0:T(8,128)}, f32[12,128,512]{2,1,0:T(8,128)}) fusion(pred[128]{0:T(512)(128)(4,1)S(1)} %compare_bitcast_fusion.2, bf16[512,12,64]{0,2,1:T(8,128)(2,1)S(1)} %get-tuple-element.200, bf16[8,128,12,64]{1,3,2,0:T(8,128)(2,1)} %get-tuple-element.199, s32[]{:T(128)} %get-tuple-element.184), kind=kOutput, calls=%fused_computation.1.clone.1 | convolution fusion | flops 103016448 | bytes 4153984 | tf_op jit(solution)/shard_map/while/body/eval_jaxpr/qhd,khd->hqk/dot_general | solution.py:28
  94.4 2.8 %convert_reduce_fusion.2 = f32[12,512]{1,0:T(8,128)S(1)} fusion(f32[12,512]{1,0:T(8,128)S(1)} %select_maximum_fusion.2, f32[12,128,512]{2,1,0:T(8,128)} %get-tuple-element.171, pred[128]{0:T(512)(128)(4,1)S(1)} %compare_bitcast_fusion.2), kind=kLoop, calls=%fused_computation.4.clone.1 | loop fusion | flops 4712448 | bytes 3195008 | tf_op jit(solution)/shard_map/while/body/eval_jaxpr/reduce_sum | solution.py:37
  100.0 3.9 %bitcast_reduce_fusion.2 = (f32[12,512]{1,0:T(8,128)}, f32[12,128,512]{2,1,0:T(8,128)}) fusion(pred[128]{0:T(512)(128)(4,1)S(1)} %compare_bitcast_fusion.2, bf16[512,12,64]{0,2,1:T(8,128)(2,1)S(1)} %get-tuple-element.200, bf16[8,128,12,64]{1,3,2,0:T(8,128)(2,1)} %get-tuple-element.199, s32[]{:T(128)} %get-tuple-element.184), kind=kOutput, calls=%fused_computation.1.clone.1 | convolution fusion | flops 103016448 | bytes 4153984 | tf_op jit(solution)/shard_map/while/body/eval_jaxpr/qhd,khd->hqk/dot_general | solution.py:28
  104.8 2.8 %convert_reduce_fusion.2 = f32[12,512]{1,0:T(8,128)S(1)} fusion(f32[12,512]{1,0:T(8,128)S(1)} %select_maximum_fusion.2, f32[12,128,512]{2,1,0:T(8,128)} %get-tuple-element.171, pred[128]{0:T(512)(128)(4,1)S(1)} %compare_bitcast_fusion.2), kind=kLoop, calls=%fused_computation.4.clone.1 | loop fusion | flops 4712448 | bytes 3195008 | tf_op jit(solution)/shard_map/while/body/eval_jaxpr/reduce_sum | solution.py:37
  110.3 3.9 %bitcast_reduce_fusion.2 = (f32[12,512]{1,0:T(8,128)}, f32[12,128,512]{2,1,0:T(8,128)}) fusion(pred[128]{0:T(512)(128)(4,1)S(1)} %compare_bitcast_fusion.2, bf16[512,12,64]{0,2,1:T(8,128)(2,1)S(1)} %get-tuple-element.200, bf16[8,128,12,64]{1,3,2,0:T(8,128)(2,1)} %get-tuple-element.199, s32[]{:T(128)} %get-tuple-element.184), kind=kOutput, calls=%fused_computation.1.clone.1 | convolution fusion | flops 103016448 | bytes 4153984 | tf_op jit(solution)/shard_map/while/body/eval_jaxpr/qhd,khd->hqk/dot_general | solution.py:28
  115.1 2.8 %convert_reduce_fusion.2 = f32[12,512]{1,0:T(8,128)S(1)} fusion(f32[12,512]{1,0:T(8,128)S(1)} %select_maximum_fusion.2, f32[12,128,512]{2,1,0:T(8,128)} %get-tuple-element.171, pred[128]{0:T(512)(128)(4,1)S(1)} %compare_bitcast_fusion.2), kind=kLoop, calls=%fused_computation.4.clone.1 | loop fusion | flops 4712448 | bytes 3195008 | tf_op jit(solution)/shard_map/while/body/eval_jaxpr/reduce_sum | solution.py:37
  120.7 3.9 %bitcast_reduce_fusion.2 = (f32[12,512]{1,0:T(8,128)}, f32[12,128,512]{2,1,0:T(8,128)}) fusion(pred[128]{0:T(512)(128)(4,1)S(1)} %compare_bitcast_fusion.2, bf16[512,12,64]{0,2,1:T(8,128)(2,1)S(1)} %get-tuple-element.200, bf16[8,128,12,64]{1,3,2,0:T(8,128)(2,1)} %get-tuple-element.199, s32[]{:T(128)} %get-tuple-element.184), kind=kOutput, calls=%fused_computation.1.clone.1 | convolution fusion | flops 103016448 | bytes 4153984 | tf_op jit(solution)/shard_map/while/body/eval_jaxpr/qhd,khd->hqk/dot_general | solution.py:28
  125.4 2.8 %convert_reduce_fusion.2 = f32[12,512]{1,0:T(8,128)S(1)} fusion(f32[12,512]{1,0:T(8,128)S(1)} %select_maximum_fusion.2, f32[12,128,512]{2,1,0:T(8,128)} %get-tuple-element.171, pred[128]{0:T(512)(128)(4,1)S(1)} %compare_bitcast_fusion.2), kind=kLoop, calls=%fused_computation.4.clone.1 | loop fusion | flops 4712448 | bytes 3195008 | tf_op jit(solution)/shard_map/while/body/eval_jaxpr/reduce_sum | solution.py:37
  131.0 3.9 %bitcast_reduce_fusion.2 = (f32[12,512]{1,0:T(8,128)}, f32[12,128,512]{2,1,0:T(8,128)}) fusion(pred[128]{0:T(512)(128)(4,1)S(1)} %compare_bitcast_fusion.2, bf16[512,12,64]{0,2,1:T(8,128)(2,1)S(1)} %get-tuple-element.200, bf16[8,128,12,64]{1,3,2,0:T(8,128)(2,1)} %get-tuple-element.199, s32[]{:T(128)} %get-tuple-element.184), kind=kOutput, calls=%fused_computation.1.clone.1 | convolution fusion | flops 103016448 | bytes 4153984 | tf_op jit(solution)/shard_map/while/body/eval_jaxpr/qhd,khd->hqk/dot_general | solution.py:28
  135.7 2.8 %convert_reduce_fusion.2 = f32[12,512]{1,0:T(8,128)S(1)} fusion(f32[12,512]{1,0:T(8,128)S(1)} %select_maximum_fusion.2, f32[12,128,512]{2,1,0:T(8,128)} %get-tuple-element.171, pred[128]{0:T(512)(128)(4,1)S(1)} %compare_bitcast_fusion.2), kind=kLoop, calls=%fused_computation.4.clone.1 | loop fusion | flops 4712448 | bytes 3195008 | tf_op jit(solution)/shard_map/while/body/eval_jaxpr/reduce_sum | solution.py:37
  141.3 3.9 %bitcast_reduce_fusion.2 = (f32[12,512]{1,0:T(8,128)}, f32[12,128,512]{2,1,0:T(8,128)}) fusion(pred[128]{0:T(512)(128)(4,1)S(1)} %compare_bitcast_fusion.2, bf16[512,12,64]{0,2,1:T(8,128)(2,1)S(1)} %get-tuple-element.200, bf16[8,128,12,64]{1,3,2,0:T(8,128)(2,1)} %get-tuple-element.199, s32[]{:T(128)} %get-tuple-element.184), kind=kOutput, calls=%fused_computation.1.clone.1 | convolution fusion | flops 103016448 | bytes 4153984 | tf_op jit(solution)/shard_map/while/body/eval_jaxpr/qhd,khd->hqk/dot_general | solution.py:28
  146.0 2.8 %convert_reduce_fusion.2 = f32[12,512]{1,0:T(8,128)S(1)} fusion(f32[12,512]{1,0:T(8,128)S(1)} %select_maximum_fusion.2, f32[12,128,512]{2,1,0:T(8,128)} %get-tuple-element.171, pred[128]{0:T(512)(128)(4,1)S(1)} %compare_bitcast_fusion.2), kind=kLoop, calls=%fused_computation.4.clone.1 | loop fusion | flops 4712448 | bytes 3195008 | tf_op jit(solution)/shard_map/while/body/eval_jaxpr/reduce_sum | solution.py:37
  151.6 16.9 %pmax.7 = f32[12,512]{1,0:T(8,128)S(1)} all-reduce(f32[12,512]{1,0:T(8,128)} %get-tuple-element.50), channel_id=1, replica_groups=mesh['blk'=4,'inner'=8] {'blk'}, use_global_device_ids=true, to_apply=%region_4.5 | all-reduce | flops 6144 | bytes 49152 | tf_op jit(solution)/shard_map/pmax | solution.py:60
  171.3 19.0 %reduce-scatter.5.cloned.1.call-done = f32[12,128]{1,0:T(8,128)} async-done(((f32[12,512]{1,0:T(8,128)}), f32[12,128]{1,0:T(8,128)}) %reduce-scatter.5.cloned.1.call-update) | async-done | bytes 6160 | tf_op jit(solution)/shard_map/reduce_scatter | solution.py:63
  190.9 33.1 %reduce-scatter.3.cloned.1.call-done = f32[12,128,64]{1,2,0:T(8,128)} async-done(((f32[12,512,64]{1,2,0:T(8,128)}), f32[12,128,64]{1,2,0:T(8,128)}) %reduce-scatter.3.cloned.1.call-update) | async-done | bytes 393232 | tf_op jit(solution)/shard_map/reduce_scatter | solution.py:64
  (133 shorter events, 46.6 us)
Async XLA Ops:
  6.5 218.6 %copy-start = (bf16[768,768]{1,0:T(8,128)(2,1)S(1)}, bf16[768,768]{1,0:T(8,128)(2,1)}, u32[]{:S(2)}) copy-start(bf16[768,768]{1,0:T(8,128)(2,1)} %param.11) | copy-start | bytes 3538948
  6.5 18.1 %copy-start.5 = (s32[128]{0:T(128)S(1)}, s32[128]{0:T(128)}, u32[]{:S(2)}) copy-start(s32[128]{0:T(128)} %param.10) | copy-start | bytes 1540
  6.5 30.3 %all-gather.4.cloned.1.call-start = ((), (), s32[]{:S(2)}) async-start(), calls=%async_computation.2 | async-start | bytes 1769472 | tf_op jit(solution)/shard_map/all_gather | solution.py:79
  7.3 55.8 %all-gather.6.cloned.1.call-start = ((), (), s32[]{:S(2)}) async-start(), calls=%async_computation.3 | async-start | bytes 1769472 | tf_op jit(solution)/shard_map/all_gather | solution.py:80
  8.0 182.2 %reduce-scatter.5.cloned.1.call-start = ((), (), s32[]{:S(2)}) async-start(), calls=%async_computation.5 | async-start | bytes 40960 | tf_op jit(solution)/shard_map/reduce_scatter | solution.py:63
  73.8 2.8 %copy-start.2 = (f32[12,512]{1,0:T(8,128)S(1)}, f32[12,512]{1,0:T(8,128)}, u32[]{:S(2)}) copy-start(f32[12,512]{1,0:T(8,128)} %get-tuple-element.185) | copy-start | bytes 73732 | tf_op jit(solution)/shard_map/while
  73.8 2.8 %copy-start.3 = (f32[12,512]{1,0:T(8,128)S(1)}, f32[12,512]{1,0:T(8,128)}, u32[]{:S(2)}) copy-start(f32[12,512]{1,0:T(8,128)} %get-tuple-element.186) | copy-start | bytes 73732 | tf_op jit(solution)/shard_map/while
  73.8 2.9 %copy-start.1 = (f32[12,128,512]{2,1,0:T(8,128)S(1)}, f32[12,128,512]{2,1,0:T(8,128)}, u32[]{:S(2)}) copy-start(f32[12,128,512]{2,1,0:T(8,128)} %get-tuple-element.171) | copy-start | bytes 9437188 | tf_op jit(solution)/shard_map/while
  84.1 2.8 %copy-start.3 = (f32[12,512]{1,0:T(8,128)S(1)}, f32[12,512]{1,0:T(8,128)}, u32[]{:S(2)}) copy-start(f32[12,512]{1,0:T(8,128)} %get-tuple-element.186) | copy-start | bytes 73732 | tf_op jit(solution)/shard_map/while
  84.1 2.9 %copy-start.1 = (f32[12,128,512]{2,1,0:T(8,128)S(1)}, f32[12,128,512]{2,1,0:T(8,128)}, u32[]{:S(2)}) copy-start(f32[12,128,512]{2,1,0:T(8,128)} %get-tuple-element.171) | copy-start | bytes 9437188 | tf_op jit(solution)/shard_map/while
  94.4 2.8 %copy-start.2 = (f32[12,512]{1,0:T(8,128)S(1)}, f32[12,512]{1,0:T(8,128)}, u32[]{:S(2)}) copy-start(f32[12,512]{1,0:T(8,128)} %get-tuple-element.185) | copy-start | bytes 73732 | tf_op jit(solution)/shard_map/while
  94.4 2.8 %copy-start.3 = (f32[12,512]{1,0:T(8,128)S(1)}, f32[12,512]{1,0:T(8,128)}, u32[]{:S(2)}) copy-start(f32[12,512]{1,0:T(8,128)} %get-tuple-element.186) | copy-start | bytes 73732 | tf_op jit(solution)/shard_map/while
  94.4 2.9 %copy-start.1 = (f32[12,128,512]{2,1,0:T(8,128)S(1)}, f32[12,128,512]{2,1,0:T(8,128)}, u32[]{:S(2)}) copy-start(f32[12,128,512]{2,1,0:T(8,128)} %get-tuple-element.171) | copy-start | bytes 9437188 | tf_op jit(solution)/shard_map/while
  104.7 2.8 %copy-start.3 = (f32[12,512]{1,0:T(8,128)S(1)}, f32[12,512]{1,0:T(8,128)}, u32[]{:S(2)}) copy-start(f32[12,512]{1,0:T(8,128)} %get-tuple-element.186) | copy-start | bytes 73732 | tf_op jit(solution)/shard_map/while
  104.7 2.9 %copy-start.1 = (f32[12,128,512]{2,1,0:T(8,128)S(1)}, f32[12,128,512]{2,1,0:T(8,128)}, u32[]{:S(2)}) copy-start(f32[12,128,512]{2,1,0:T(8,128)} %get-tuple-element.171) | copy-start | bytes 9437188 | tf_op jit(solution)/shard_map/while
  115.0 2.8 %copy-start.3 = (f32[12,512]{1,0:T(8,128)S(1)}, f32[12,512]{1,0:T(8,128)}, u32[]{:S(2)}) copy-start(f32[12,512]{1,0:T(8,128)} %get-tuple-element.186) | copy-start | bytes 73732 | tf_op jit(solution)/shard_map/while
  115.1 2.9 %copy-start.1 = (f32[12,128,512]{2,1,0:T(8,128)S(1)}, f32[12,128,512]{2,1,0:T(8,128)}, u32[]{:S(2)}) copy-start(f32[12,128,512]{2,1,0:T(8,128)} %get-tuple-element.171) | copy-start | bytes 9437188 | tf_op jit(solution)/shard_map/while
  125.4 2.8 %copy-start.3 = (f32[12,512]{1,0:T(8,128)S(1)}, f32[12,512]{1,0:T(8,128)}, u32[]{:S(2)}) copy-start(f32[12,512]{1,0:T(8,128)} %get-tuple-element.186) | copy-start | bytes 73732 | tf_op jit(solution)/shard_map/while
  125.4 2.9 %copy-start.1 = (f32[12,128,512]{2,1,0:T(8,128)S(1)}, f32[12,128,512]{2,1,0:T(8,128)}, u32[]{:S(2)}) copy-start(f32[12,128,512]{2,1,0:T(8,128)} %get-tuple-element.171) | copy-start | bytes 9437188 | tf_op jit(solution)/shard_map/while
  135.7 2.8 %copy-start.3 = (f32[12,512]{1,0:T(8,128)S(1)}, f32[12,512]{1,0:T(8,128)}, u32[]{:S(2)}) copy-start(f32[12,512]{1,0:T(8,128)} %get-tuple-element.186) | copy-start | bytes 73732 | tf_op jit(solution)/shard_map/while
  135.7 2.9 %copy-start.1 = (f32[12,128,512]{2,1,0:T(8,128)S(1)}, f32[12,128,512]{2,1,0:T(8,128)}, u32[]{:S(2)}) copy-start(f32[12,128,512]{2,1,0:T(8,128)} %get-tuple-element.171) | copy-start | bytes 9437188 | tf_op jit(solution)/shard_map/while
  146.0 2.8 %copy-start.3 = (f32[12,512]{1,0:T(8,128)S(1)}, f32[12,512]{1,0:T(8,128)}, u32[]{:S(2)}) copy-start(f32[12,512]{1,0:T(8,128)} %get-tuple-element.186) | copy-start | bytes 73732 | tf_op jit(solution)/shard_map/while
  146.0 2.9 %copy-start.1 = (f32[12,128,512]{2,1,0:T(8,128)S(1)}, f32[12,128,512]{2,1,0:T(8,128)}, u32[]{:S(2)}) copy-start(f32[12,128,512]{2,1,0:T(8,128)} %get-tuple-element.171) | copy-start | bytes 9437188 | tf_op jit(solution)/shard_map/while
  169.9 54.2 %reduce-scatter.3.cloned.1.call-start = ((), (), s32[]{:S(2)}) async-start(), calls=%async_computation.4 | async-start | bytes 1966080 | tf_op jit(solution)/shard_map/reduce_scatter | solution.py:64
  (14 other events, 33.9 us)
Sparse Core Ops, SparseCore 0:
  9.0 27.7 all-gather.3
  38.5 24.5 all-gather.5
  170.0 20.1 reduce-scatter.4
  193.1 30.9 reduce-scatter.2
where the time goes:
time: 234 us; the launch traced here: 233 us
  waiting for transfers between devices  74 us (32%)
  matrix products  49.1 us (21%)
  blocking collectives  43.9 us (19%)
  other arithmetic  33 us (14%)
  local copies, waits for them, and re-layouts  18.7 us (8%)
  between operations  13.2 us (6%)
    reduce_scatter x1, waiting for transfers between devices, combine_loop(): lax.psum_scatter(weighted * shrink[..., None], 'blk', scatter_dimension=1...  33.1 us
    dot_general x8, matrix products, one_block(): jnp.einsum('qhd,khd->hqk', query_heads, key_heads, preferred_element_type...  31.3 us
    reduce_sum x8, other arithmetic, one_block(): jnp.sum(chances, axis=-1, dtype=jnp.float32)  22.1 us
    all_gather x1, waiting for transfers between devices, on_device(): lax.all_gather(values, 'inner', axis=0, tiled=True)  20.3 us
    reduce_scatter x1, waiting for transfers between devices, combine_loop(): lax.psum_scatter(row_total * shrink, 'blk', scatter_dimension=1, tiled=True)  19 us
    pmax x1, blocking collectives, combine_loop(): top = lax.pmax(run_max, 'blk')  16.9 us
    dot_general x8, matrix products, one_block(): jnp.einsum('hqk,khd->hqd', chances, value_heads, preferred_element_type=j...  16.8 us
    all_gather x1, blocking collectives, on_device(): query_all = lax.all_gather(queries, 'blk', axis=0, tiled=True)  15.1 us
  transfers between devices with their start and end apart: 4, of which 4 were waited for; matrix products, arithmetic and copies ran while one was open for 4% of the time, Pallas kernels for 0%

commit v1 on v0

v1 whole, which is shorter than its diff:
```python
import functools

import jax
import jax.numpy as jnp
from jax import lax
from jax.experimental import pallas as pl
from jax.experimental.pallas import tpu as pltpu
from jax.sharding import PartitionSpec as P

HEAD_DIM = 64
GROUPS = 4
LANES = 128
MARK = 100.0
MARK_TEST = 64.0
SAFE = 64.0
LOW = -1e30
BF16 = jnp.bfloat16
F32 = jnp.float32
VMEM = pl.BlockSpec(memory_space=pltpu.VMEM)
NT = (((1,), (1,)), ((), ()))


def params():
    return pltpu.CompilerParams(vmem_limit_bytes=48 * 1024 * 1024)


def lower_lanes(shape):
    return lax.broadcasted_iota(jnp.int32, shape, 1) < HEAD_DIM


def swap_halves(x):
    return pltpu.roll(x, HEAD_DIM, 1)


def pack_kernel(rest, per_group, q_ref, k_ref, v_ref, valid_ref, *outs):
    mine = lax.axis_index("inner") // rest
    rows = q_ref.shape[0]
    half = rows // 2
    square = (rows, rows)
    on_diagonal = lax.broadcasted_iota(jnp.int32, square, 0) == lax.broadcasted_iota(
        jnp.int32, square, 1
    )
    flag_row = jnp.broadcast_to(valid_ref[...].astype(F32), square)
    picked = jnp.where(on_diagonal, flag_row, 0.0).astype(BF16)
    flags = jnp.dot(picked, jnp.ones((rows, LANES), BF16), preferred_element_type=F32) > 0.5
    low = lower_lanes((rows, LANES))
    low_half = lower_lanes((half, LANES))
    kv_groups, q_groups = [], []
    for g in range(GROUPS):
        kv_slots, q_slots = [], []
        for j in range(per_group):
            h = g * per_group + j
            tile = pl.ds((h // 2) * LANES, LANES)
            k = k_ref[:, tile].astype(F32)
            v = v_ref[:, tile].astype(F32)
            q = q_ref[:, tile].astype(F32) * (HEAD_DIM**-0.5)
            if h % 2 == 0:
                kv = jnp.where(low, k, swap_halves(v))
                qq = jnp.where(low_half, q[:half], swap_halves(q[half:]))
            else:
                kv = jnp.where(low, swap_halves(k), v)
                qq = jnp.where(low_half, swap_halves(q[:half]), q[half:])
            kv_slots.append(jnp.where(flags, kv, MARK))
            q_slots.append(qq)
        kv_groups.append(kv_slots)
        q_groups.append(q_slots)
    for s in range(GROUPS):
        want = lax.rem(mine + s, GROUPS)
        for j in range(per_group):
            lanes = pl.ds(j * LANES, LANES)
            for groups, out in ((kv_groups, outs[s]), (q_groups, outs[GROUPS + s])):
                x = groups[0][j]
                for g in range(1, GROUPS):
                    x = jnp.where(want == g, groups[g][j], x)
                out[:, lanes] = x.astype(BF16)


def pack(q, k, v, valid, rest):
    rows, width = q.shape
    per_group = width // HEAD_DIM // GROUPS
    slots = per_group * LANES
    return pl.pallas_call(
        functools.partial(pack_kernel, rest, per_group),
        out_shape=[jax.ShapeDtypeStruct((rows, slots), BF16)] * GROUPS
        + [jax.ShapeDtypeStruct((rows // 2, slots), BF16)] * GROUPS,
        in_specs=[VMEM] * 4,
        out_specs=[VMEM] * (2 * GROUPS),
        compiler_params=params(),
    )(q, k, v, valid.reshape(1, rows))


def attend_kernel(n_q, n_kv, half, first, *refs):
    q_refs, refs = refs[:n_q], refs[n_q:]
    kv_refs, refs = refs[:n_kv], refs[n_kv:]
    if not first:
        acc_in, top_in = refs[:2]
        refs = refs[2:]
    acc, top, qs, ks, vs = refs
    slots = qs.shape[1] // LANES
    rows_q = qs.shape[0]
    rows_k = ks.shape[0]
    start = 0
    for ref in q_refs:
        for piece in range(ref.shape[0] // half):
            for j in range(slots):
                lanes = pl.ds(j * LANES, LANES)
                x = ref[pl.ds(piece * half, half), lanes].astype(F32)
                low = lower_lanes(x.shape)
                qs[pl.ds(start, half), lanes] = jnp.where(low, x, 0.0).astype(BF16)
                qs[pl.ds(start + half, half), lanes] = jnp.where(low, swap_halves(x), 0.0).astype(BF16)
            start += 2 * half
    start = 0
    for ref in kv_refs:
        n = ref.shape[0]
        for j in range(slots):
            lanes = pl.ds(j * LANES, LANES)
            x = ref[:, lanes].astype(F32)
            hole = x > MARK_TEST
            low = lower_lanes(x.shape)
            x = jnp.where(hole, 0.0, x)
            ks[pl.ds(start, n), lanes] = x.astype(BF16)
            vs[pl.ds(start, n), lanes] = jnp.where(low, jnp.where(hole, 0.0, 1.0), x).astype(BF16)
        start += n
    pick = (lax.broadcasted_iota(jnp.int32, (LANES, LANES), 0) < HEAD_DIM).astype(BF16)

    def largest(ref):
        best = None
        for j in range(slots):
            x = ref[:, pl.ds(j * LANES, LANES)].astype(F32)
            norms = jnp.dot((x * x).astype(BF16), pick, preferred_element_type=F32)
            best = norms if best is None else jnp.maximum(best, norms)
        return jnp.max(best)

    bound = largest(qs) * largest(ks) * 1.05
    safe = bound <= SAFE * SAFE
    if first:
        top[...] = jnp.zeros_like(top)
        acc[...] = jnp.zeros_like(acc)
    else:
        safe = jnp.logical_and(safe, jnp.max(top_in[...]) == 0.0)
        top[...] = top_in[...]
        acc[...] = acc_in[...]
    block = min(256, rows_q)

    @pl.when(safe)
    def _():
        for j in range(slots):
            lanes = pl.ds(j * LANES, LANES)
            for r in range(0, rows_q, block):
                at = pl.ds(r, block)
                s = lax.dot_general(qs[at, lanes], ks[:, lanes], NT, preferred_element_type=F32)
                p = jnp.exp(s).astype(BF16)
                acc[at, lanes] = acc[at, lanes] + jnp.dot(p, vs[:, lanes], preferred_element_type=F32)

    @pl.when(jnp.logical_not(safe))
    def _():
        step_q, step_k = 128, 256

        def over_queries(i, unused):
            at = pl.ds(pl.multiple_of(i * step_q, step_q), step_q)
            lane = lax.broadcasted_iota(jnp.int32, (step_q, LANES), 1)
            tops = top[at, :]
            for j in range(slots):
                lanes = pl.ds(j * LANES, LANES)
                own = jnp.sum(jnp.where(lane == j, tops, 0.0), axis=1, keepdims=True)

                def over_keys(c, carry):
                    high, total = carry
                    ka = pl.ds(pl.multiple_of(c * step_k, step_k), step_k)
                    s = lax.dot_general(qs[at, lanes], ks[ka, lanes], NT, preferred_element_type=F32)
                    ones = lax.dot_general(
                        jnp.ones((step_q, LANES), BF16),
                        jnp.where(lower_lanes((step_k, LANES)), vs[ka, lanes].astype(F32), 0.0).astype(BF16),
                        NT,
                        preferred_element_type=F32,
                    )
                    s = jnp.where(ones > 0.5, s, LOW)
                    new = jnp.maximum(high, jnp.max(s, axis=1, keepdims=True))
                    p = jnp.exp(s - new).astype(BF16)
                    total = total * jnp.exp(high - new) + jnp.dot(p, vs[ka, lanes], preferred_element_type=F32)
                    return new, total

                high, total = lax.fori_loop(0, rows_k // step_k, over_keys, (own, acc[at, lanes]))
                acc[at, lanes] = total
                tops = jnp.where(lane == j, high, tops)
            top[at, :] = tops
            return unused

        lax.fori_loop(0, rows_q // step_q, over_queries, 0)


def attend(q_list, kv_list, half, state):
    slots = q_list[0].shape[1]
    rows_q = 2 * sum(q.shape[0] for q in q_list)
    rows_k = sum(k.shape[0] for k in kv_list)
    first = state is None
    args = list(q_list) + list(kv_list) + ([] if first else list(state))
    return pl.pallas_call(
        functools.partial(attend_kernel, len(q_list), len(kv_list), half, first),
        out_shape=[
            jax.ShapeDtypeStruct((rows_q, slots), F32),
            jax.ShapeDtypeStruct((rows_q, LANES), F32),
        ],
        in_specs=[VMEM] * len(args),
        out_specs=[VMEM] * 2,
        scratch_shapes=[
            pltpu.VMEM((rows_q, slots), BF16),
            pltpu.VMEM((rows_k, slots), BF16),
            pltpu.VMEM((rows_k, slots), BF16),
        ],
        compiler_params=params(),
        cost_estimate=pl.CostEstimate(
            flops=4 * rows_q * rows_k * slots, bytes_accessed=4 * rows_q * slots, transcendentals=rows_q * rows_k * slots // LANES
        ),
    )(*args)


def settle_kernel(n, *refs):
    accs, tops, outs = refs[:n], refs[n : 2 * n], refs[2 * n :]
    rows, width = accs[0].shape
    slots = width // LANES
    lane = lax.broadcasted_iota(jnp.int32, (rows, LANES), 1)
    piece = rows // len(outs)
    half = piece // 2
    low_half = lower_lanes((half, LANES))
    for j in range(slots):
        lanes = pl.ds(j * LANES, LANES)
        own = [jnp.sum(jnp.where(lane == j, t[...], 0.0), axis=1, keepdims=True) for t in tops]
        high = functools.reduce(jnp.maximum, own)
        total = functools.reduce(lambda a, b: a + b, [a[:, lanes] * jnp.exp(t - high) for a, t in zip(accs, own)])
        result = total / (swap_halves(total) + jnp.exp(-high))
        for i, out in enumerate(outs):
            first = result[i * piece : i * piece + half]
            second = result[i * piece + half : (i + 1) * piece]
            out[:, lanes] = jnp.where(low_half, swap_halves(first), second).astype(BF16)


def settle(accs, tops, n_out):
    rows, width = accs[0].shape
    return pl.pallas_call(
        functools.partial(settle_kernel, len(accs)),
        out_shape=[jax.ShapeDtypeStruct((rows // n_out // 2, width), BF16)] * n_out,
        in_specs=[VMEM] * (2 * len(accs)),
        out_specs=[VMEM] * n_out,
        compiler_params=params(),
    )(*accs, *tops)


def project_kernel(rest, *refs):
    parts, w_ref, out, joined = refs[:GROUPS], refs[GROUPS], refs[GROUPS + 1], refs[GROUPS + 2]
    mine = lax.axis_index("inner") // rest
    half, width = parts[0].shape
    slots = width // LANES
    group_rows = slots * HEAD_DIM
    total = None
    for s, part in enumerate(parts):
        for j in range(slots):
            x = part[:, pl.ds(j * LANES, LANES)]
            joined[:half, pl.ds(j * HEAD_DIM, HEAD_DIM)] = x[:, :HEAD_DIM]
            joined[half:, pl.ds(j * HEAD_DIM, HEAD_DIM)] = x[:, HEAD_DIM:]
        g = lax.rem(mine + s, GROUPS)
        w = w_ref[pl.ds(pl.multiple_of(g * group_rows, 16), group_rows), :]
        term = jnp.dot(joined[...], w, preferred_element_type=F32)
        total = term if total is None else total + term
    out[...] = total.astype(BF16)


def project(parts, w, rest):
    half, width = parts[0].shape
    return pl.pallas_call(
        functools.partial(project_kernel, rest),
        out_shape=jax.ShapeDtypeStruct((2 * half, w.shape[1]), BF16),
        in_specs=[VMEM] * (GROUPS + 1),
        out_specs=VMEM,
        scratch_shapes=[pltpu.VMEM((2 * half, width // 2), BF16)],
        compiler_params=params(),
    )(*parts, w)


def on_device(n_blk, n_inner, q, k, v, valid, w):
    rest = n_inner // GROUPS

    def over_groups(x, s):
        return lax.ppermute(x, "inner", [(i, (i + s * rest) % n_inner) for i in range(n_inner)])

    def over_rest(x, t):
        return lax.ppermute(x, "inner", [(i, i // rest * rest + (i + t) % rest) for i in range(n_inner)])

    def over_blk(x, move):
        return lax.ppermute(x, "blk", [(i, move(i)) for i in range(n_blk)])

    def spread(chunk, which):
        if n_blk == 4:
            from_x = over_blk(chunk, lambda i: i ^ 1)
            from_y = over_blk(chunk, lambda i: i ^ 2)
            if which == 0:
                far = over_blk(from_y, lambda i: i ^ 1)
            else:
                far = over_blk(from_x, lambda i: i ^ 2)
            return [chunk, from_x, from_y, far]
        return [chunk] + [over_blk(chunk, lambda i, t=t: (i + t) % n_blk) for t in range(1, n_blk)]

    packed = pack(q, k, v, valid, rest)
    kv, qs = packed[:GROUPS], packed[GROUPS:]
    kv = [kv[0]] + [over_groups(kv[s], s) for s in range(1, GROUPS)]
    qs = [qs[0]] + [over_groups(qs[s], s) for s in range(1, GROUPS)]
    blocks = spread(jnp.concatenate(kv[:2], axis=0), 0) + spread(jnp.concatenate(kv[2:], axis=0), 1)
    q_own = jnp.concatenate(qs, axis=0)
    q_list = [q_own] + [over_rest(q_own, t) for t in range(1, rest)]
    acc, top = attend(q_list, blocks, q.shape[0] // 2, None)
    rows = 2 * q_own.shape[0]
    accs, tops = [acc[:rows]], [top[:rows]]
    for t in range(1, rest):
        accs.append(over_rest(acc[t * rows : (t + 1) * rows], rest - t))
        tops.append(over_rest(top[t * rows : (t + 1) * rows], rest - t))
    parts = settle(accs, tops, GROUPS)
    parts = [parts[0]] + [over_groups(parts[s], GROUPS - s) for s in range(1, GROUPS)]
    return project(parts, w, rest)


def solution(mesh):
    rows = P(("blk", "inner"), None)
    return jax.shard_map(
        functools.partial(on_device, mesh.shape["blk"], mesh.shape["inner"]),
        mesh=mesh,
        in_specs=(rows, rows, rows, P(("blk", "inner")), P()),
        out_specs=rows,
        check_vma=False,
    )
```

time: 234 us -> 133 us (0.57)
  Pallas kernels: 0 us -> 84.6 us
  waiting for transfers between devices: 74 us -> 19 us
  matrix products: 49.1 us -> 0 us
  blocking collectives: 43.9 us -> 0 us
  other arithmetic: 33 us -> 0 us
  starting transfers between devices: 0.12 us -> 25 us
  local copies, waits for them, and re-layouts: 18.7 us -> 3.68 us
  between operations: 13.2 us -> 0.13 us
    pallas_call x0 -> x4, Pallas kernels: none -> 84.6 us  [the longest x1 82 us: attend(): pl.pallas_call(functools.partial(attend_kernel, len(q_list), len(kv_list)...]
    reduce_scatter x2 -> x0, waiting for transfers between devices: 52.1 us -> none  [the longest x1 33.1 us: combine_loop(): lax.psum_scatter(weighted * shrink[..., None], 'blk', scatter_dimension=1...]
    dot_general x17 -> x0, matrix products: 49.1 us -> none  [the longest x8 31.3 us: one_block(): jnp.einsum('qhd,khd->hqk', query_heads, key_heads, preferred_element_type...]
    all_gather x2 -> x0, blocking collectives: 27.1 us -> none  [the longest x1 15.1 us: on_device(): query_all = lax.all_gather(queries, 'blk', axis=0, tiled=True)]
    ppermute x0 -> x18, starting transfers between devices: none -> 25 us  [the longest x9 16 us: over_groups(): lax.ppermute(x, 'inner', [(i, (i + s * rest) % n_inner) for i in range(n_...]
    reduce_sum x8 -> x0, other arithmetic: 22.1 us -> none  [one_block(): jnp.sum(chances, axis=-1, dtype=jnp.float32)]
    all_gather x2 -> x0, waiting for transfers between devices: 20.5 us -> none  [the longest x1 20.3 us: on_device(): lax.all_gather(values, 'inner', axis=0, tiled=True)]
    ppermute x0 -> x18, waiting for transfers between devices: none -> 19 us  [the longest x9 9.59 us: over_groups(): lax.ppermute(x, 'inner', [(i, (i + s * rest) % n_inner) for i in range(n_...]
  transfers between devices with their start and end apart: 4 -> 18, of which waited for: 4 -> 9; matrix products, arithmetic and copies ran while one was open for 4% -> 0% of each run, Pallas kernels for 0% -> 0%
where the time goes in v1:
time: 133 us
  Pallas kernels  84.6 us (64%)
  starting transfers between devices  25 us (19%)
  waiting for transfers between devices  19 us (14%)
  local copies, waits for them, and re-layouts  3.68 us (3%)
    pallas_call x1, Pallas kernels, attend(): pl.pallas_call(functools.partial(attend_kernel, len(q_list), len(kv_list)...  82 us
    ppermute x9, starting transfers between devices, over_groups(): lax.ppermute(x, 'inner', [(i, (i + s * rest) % n_inner) for i in range(n_...  16 us
    ppermute x9, waiting for transfers between devices, over_groups(): lax.ppermute(x, 'inner', [(i, (i + s * rest) % n_inner) for i in range(n_...  9.59 us
    ppermute x6, starting transfers between devices, over_blk(): return lax.ppermute(x, 'blk', [(i, move(i)) for i in range(n_blk)])  8.34 us
    ppermute x6, waiting for transfers between devices, over_blk(): return lax.ppermute(x, 'blk', [(i, move(i)) for i in range(n_blk)])  7.4 us
    unnamed x15, local copies, waits for them, and re-layouts  3.49 us
  transfers between devices with their start and end apart: 18, of which 9 were waited for; matrix products, arithmetic and copies ran while one was open for 0% of the time, Pallas kernels for 0%

profile of v1, /device:TPU:0, one launch (start us, length us, event | category | flops | bytes accessed | tf_op | source)
XLA Modules:
  0.0 132.5 jit_solution(6478122608321247283)
XLA Ops:
  0.0 0.9 copy-done.1
  0.9 0.9 copy-done.2
  1.9 0.9 copy-done.3
  3.9 3.1 %collective-permute-start = (bf16[64,384]{1,0:T(8,128)(2,1)S(1)}, bf16[64,384]{1,0:T(8,128)(2,1)S(1)}, u32[]{:S(2)}, u32[]{:S(2)}) collective-permute-start(bf16[64,384]{1,0:T(8,128)(2,1)S(1)} %get-tuple-element.20), channel_id=1, source_target_pairs={{0,2},{1,3},{2,4},{3,5},{4,6},{5,7},{6,0},{7,1},{8,10},{9,11},{10,... | collective-permute-start | bytes 147464 | tf_op jit(solution)/shard_map/ppermute | solution.py:284
  7.0 2.6 %collective-permute-start.1 = (bf16[64,384]{1,0:T(8,128)(2,1)S(1)}, bf16[64,384]{1,0:T(8,128)(2,1)S(1)}, u32[]{:S(2)}, u32[]{:S(2)}) collective-permute-start(bf16[64,384]{1,0:T(8,128)(2,1)S(1)} %get-tuple-element.21), channel_id=1, source_target_pairs={{0,4},{1,5},{2,6},{3,7},{4,0},{5,1},{6,2},{7,3},{8,12},{9,13},{10,... | collective-permute-start | bytes 147464 | tf_op jit(solution)/shard_map/ppermute | solution.py:284
  9.6 1.3 %collective-permute-start.2 = (bf16[64,384]{1,0:T(8,128)(2,1)S(1)}, bf16[64,384]{1,0:T(8,128)(2,1)S(1)}, u32[]{:S(2)}, u32[]{:S(2)}) collective-permute-start(bf16[64,384]{1,0:T(8,128)(2,1)S(1)} %get-tuple-element.22), channel_id=1, source_target_pairs={{0,6},{1,7},{2,0},{3,1},{4,2},{5,3},{6,4},{7,5},{8,14},{9,15},{10,... | collective-permute-start | bytes 147464 | tf_op jit(solution)/shard_map/ppermute | solution.py:284
  10.9 0.7 collective-permute-start.4
  12.0 2.9 %collective-permute-start.9 = (bf16[128,384]{1,0:T(8,128)(2,1)S(1)}, bf16[128,384]{1,0:T(8,128)(2,1)S(1)}, u32[]{:S(2)}, u32[]{:S(2)}) collective-permute-start(bf16[128,384]{1,0:T(8,128)(2,1)S(1)} %get-tuple-element.26), channel_id=1, source_target_pairs={{0,6},{1,7},{2,0},{3,1},{4,2},{5,3},{6,4},{7,5},{8,14},{9,15},{10,... | collective-permute-start | bytes 294920 | tf_op jit(solution)/shard_map/ppermute | solution.py:284
  14.8 3.7 %collective-permute-done.4 = bf16[128,384]{1,0:T(8,128)(2,1)S(1)} collective-permute-done((bf16[128,384]{1,0:T(8,128)(2,1)S(1)}, bf16[128,384]{1,0:T(8,128)(2,1)S(1)}, u32[]{:S(2)}, u32[]{:S(2)}) %collective-permute-start.4) | collective-permute-done | bytes 98336 | tf_op jit(solution)/shard_map/ppermute | solution.py:284
  18.6 1.6 %collective-permute-start.6 = (bf16[256,384]{1,0:T(8,128)(2,1)S(1)}, bf16[256,384]{1,0:T(8,128)(2,1)S(1)}, u32[]{:S(2)}, u32[]{:S(2)}) collective-permute-start(bf16[256,384]{1,0:T(8,128)(2,1)S(1)} %constant_dynamic-update-slice_fusion.4.refs_2_), channel_id=1, source_target_pairs={{0,16},{8,24},{16,0},{24,8},{1,17},{9,25},{17,1},{25,9},{2,18},{10... | collective-permute-start | bytes 589832 | tf_op jit(solution)/shard_map/ppermute | solution.py:290
  20.8 1.6 %collective-permute-start.10 = (bf16[256,384]{1,0:T(8,128)(2,1)S(1)}, bf16[256,384]{1,0:T(8,128)(2,1)S(1)}, u32[]{:S(2)}, u32[]{:S(2)}) collective-permute-start(bf16[256,384]{1,0:T(8,128)(2,1)S(1)} %constant_dynamic-update-slice_fusion.6.refs_6_), channel_id=1, source_target_pairs={{0,8},{8,0},{16,24},{24,16},{1,9},{9,1},{17,25},{25,17},{2,10},{10... | collective-permute-start | bytes 589832 | tf_op jit(solution)/shard_map/ppermute | solution.py:290
  23.1 1.5 %collective-permute-start.11 = (bf16[256,384]{1,0:T(8,128)(2,1)S(1)}, bf16[256,384]{1,0:T(8,128)(2,1)S(1)}, u32[]{:S(2)}, u32[]{:S(2)}) collective-permute-start(bf16[256,384]{1,0:T(8,128)(2,1)S(1)} %constant_dynamic-update-slice_fusion.6.refs_6_), channel_id=1, source_target_pairs={{0,16},{8,24},{16,0},{24,8},{1,17},{9,25},{17,1},{25,9},{2,18},{10... | collective-permute-start | bytes 589832 | tf_op jit(solution)/shard_map/ppermute | solution.py:290
  24.6 1.5 %collective-permute-start.7 = (bf16[256,384]{1,0:T(8,128)(2,1)S(1)}, bf16[256,384]{1,0:T(8,128)(2,1)S(1)}, u32[]{:S(2)}, u32[]{:S(2)}) collective-permute-start(bf16[256,384]{1,0:T(8,128)(2,1)S(1)} %collective-permute-done.6.refs_4_), channel_id=1, source_target_pairs={{0,8},{8,0},{16,24},{24,16},{1,9},{9,1},{17,25},{25,17},{2,10},{10... | collective-permute-start | bytes 589832 | tf_op jit(solution)/shard_map/ppermute | solution.py:290
  26.1 1.6 %collective-permute-done.10.refs_7_ = bf16[256,384]{1,0:T(8,128)(2,1)S(1)} collective-permute-done((bf16[256,384]{1,0:T(8,128)(2,1)S(1)}, bf16[256,384]{1,0:T(8,128)(2,1)S(1)}, u32[]{:S(2)}, u32[]{:S(2)}) %collective-permute-start.10) | collective-permute-done | bytes 196640 | tf_op jit(solution)/shard_map/ppermute | solution.py:290
  27.7 1.6 %collective-permute-start.12 = (bf16[256,384]{1,0:T(8,128)(2,1)S(1)}, bf16[256,384]{1,0:T(8,128)(2,1)S(1)}, u32[]{:S(2)}, u32[]{:S(2)}) collective-permute-start(bf16[256,384]{1,0:T(8,128)(2,1)S(1)} %collective-permute-done.10.refs_7_), channel_id=1, source_target_pairs={{0,16},{8,24},{16,0},{24,8},{1,17},{9,25},{17,1},{25,9},{2,18},{10... | collective-permute-start | bytes 589832 | tf_op jit(solution)/shard_map/ppermute | solution.py:290
  29.3 2.6 %collective-permute-done.5.refs_3_ = bf16[256,384]{1,0:T(8,128)(2,1)S(1)} collective-permute-done((bf16[256,384]{1,0:T(8,128)(2,1)S(1)}, bf16[256,384]{1,0:T(8,128)(2,1)S(1)}, u32[]{:S(2)}, u32[]{:S(2)}) %collective-permute-start.5) | collective-permute-done | bytes 196640 | tf_op jit(solution)/shard_map/ppermute | solution.py:290
  32.0 3.2 %collective-permute-done.7.refs_5_ = bf16[256,384]{1,0:T(8,128)(2,1)S(1)} collective-permute-done((bf16[256,384]{1,0:T(8,128)(2,1)S(1)}, bf16[256,384]{1,0:T(8,128)(2,1)S(1)}, u32[]{:S(2)}, u32[]{:S(2)}) %collective-permute-start.7) | collective-permute-done | bytes 196640 | tf_op jit(solution)/shard_map/ppermute | solution.py:290
  35.1 82.0 %shard_map.56 = (f32[1024,384]{1,0:T(8,128)S(1)}, f32[1024,128]{1,0:T(8,128)S(1)}) custom-call(bf16[256,384]{1,0:T(8,128)(2,1)S(1)} %constant_dynamic-update-slice_fusion.refs_0_, bf16[256,384]{1,0:T(8,128)(2,1)S(1)} %collective-permute-done.3.refs_1_, bf16[256,384]{1,0:T(8,128)(2,1)S(1)} %constant_dynamic-update-slice_fusion.4.refs_2_, ...), custom_call_target="tpu_custom_call" | custom-call | flops 3221225472 | bytes 1572864 | tf_op jit(solution)/shard_map/pallas_call | solution.py:198
  118.0 2.0 %collective-permute-done.14.refs_3_ = f32[512,128]{1,0:T(8,128)S(1)} collective-permute-done((f32[512,128]{1,0:T(8,128)S(1)}, f32[512,128]{1,0:T(8,128)S(1)}, u32[]{:S(2)}, u32[]{:S(2)}) %collective-permute-start.14) | collective-permute-done | bytes 262176 | tf_op jit(solution)/shard_map/ppermute | solution.py:287
  120.0 1.0 shard_map.57
  121.0 4.5 %collective-permute-start.15 = (bf16[64,384]{1,0:T(8,128)(2,1)S(1)}, bf16[64,384]{1,0:T(8,128)(2,1)S(1)}, u32[]{:S(2)}, u32[]{:S(2)}) collective-permute-start(bf16[64,384]{1,0:T(8,128)(2,1)S(1)} %get-tuple-element.30), channel_id=1, source_target_pairs={{0,6},{1,7},{2,0},{3,1},{4,2},{5,3},{6,4},{7,5},{8,14},{9,15},{10,... | collective-permute-start | bytes 147464 | tf_op jit(solution)/shard_map/ppermute | solution.py:284
  126.1 1.5 %collective-permute-done.15.refs_1_ = bf16[64,384]{1,0:T(8,128)(2,1)S(1)} collective-permute-done((bf16[64,384]{1,0:T(8,128)(2,1)S(1)}, bf16[64,384]{1,0:T(8,128)(2,1)S(1)}, u32[]{:S(2)}, u32[]{:S(2)}) %collective-permute-start.15) | collective-permute-done | bytes 49184 | tf_op jit(solution)/shard_map/ppermute | solution.py:284
  127.6 3.2 %collective-permute-done.16.refs_2_ = bf16[64,384]{1,0:T(8,128)(2,1)S(1)} collective-permute-done((bf16[64,384]{1,0:T(8,128)(2,1)S(1)}, bf16[64,384]{1,0:T(8,128)(2,1)S(1)}, u32[]{:S(2)}, u32[]{:S(2)}) %collective-permute-start.16) | collective-permute-done | bytes 49184 | tf_op jit(solution)/shard_map/ppermute | solution.py:284
  131.4 1.1 shard_map.58
  (36 shorter events, 4.9 us)
Async XLA Ops:
  0.0 0.9 copy-start.1
  0.9 0.9 copy-start.2
  1.9 0.9 copy-start.3
  2.8 0.7 copy-start.4
  3.9 8.1 %collective-permute-start = (bf16[64,384]{1,0:T(8,128)(2,1)S(1)}, bf16[64,384]{1,0:T(8,128)(2,1)S(1)}, u32[]{:S(2)}, u32[]{:S(2)}) collective-permute-start(bf16[64,384]{1,0:T(8,128)(2,1)S(1)} %get-tuple-element.20), channel_id=1, source_target_pairs={{0,2},{1,3},{2,4},{3,5},{4,6},{5,7},{6,0},{7,1},{8,10},{9,11},{10,... | collective-permute-start | bytes 147464 | tf_op jit(solution)/shard_map/ppermute | solution.py:284
  7.0 15.4 %collective-permute-start.1 = (bf16[64,384]{1,0:T(8,128)(2,1)S(1)}, bf16[64,384]{1,0:T(8,128)(2,1)S(1)}, u32[]{:S(2)}, u32[]{:S(2)}) collective-permute-start(bf16[64,384]{1,0:T(8,128)(2,1)S(1)} %get-tuple-element.21), channel_id=1, source_target_pairs={{0,4},{1,5},{2,6},{3,7},{4,0},{5,1},{6,2},{7,3},{8,12},{9,13},{10,... | collective-permute-start | bytes 147464 | tf_op jit(solution)/shard_map/ppermute | solution.py:284
  9.6 12.8 %collective-permute-start.2 = (bf16[64,384]{1,0:T(8,128)(2,1)S(1)}, bf16[64,384]{1,0:T(8,128)(2,1)S(1)}, u32[]{:S(2)}, u32[]{:S(2)}) collective-permute-start(bf16[64,384]{1,0:T(8,128)(2,1)S(1)} %get-tuple-element.22), channel_id=1, source_target_pairs={{0,6},{1,7},{2,0},{3,1},{4,2},{5,3},{6,4},{7,5},{8,14},{9,15},{10,... | collective-permute-start | bytes 147464 | tf_op jit(solution)/shard_map/ppermute | solution.py:284
  10.9 7.6 %collective-permute-start.4 = (bf16[128,384]{1,0:T(8,128)(2,1)S(1)}, bf16[128,384]{1,0:T(8,128)(2,1)S(1)}, u32[]{:S(2)}, u32[]{:S(2)}) collective-permute-start(bf16[128,384]{1,0:T(8,128)(2,1)S(1)} %get-tuple-element.24), channel_id=1, source_target_pairs={{0,2},{1,3},{2,4},{3,5},{4,6},{5,7},{6,0},{7,1},{8,10},{9,11},{10,... | collective-permute-start | bytes 294920 | tf_op jit(solution)/shard_map/ppermute | solution.py:284
  11.6 9.2 %collective-permute-start.8 = (bf16[128,384]{1,0:T(8,128)(2,1)S(1)}, bf16[128,384]{1,0:T(8,128)(2,1)S(1)}, u32[]{:S(2)}, u32[]{:S(2)}) collective-permute-start(bf16[128,384]{1,0:T(8,128)(2,1)S(1)} %get-tuple-element.25), channel_id=1, source_target_pairs={{0,4},{1,5},{2,6},{3,7},{4,0},{5,1},{6,2},{7,3},{8,12},{9,13},{10,... | collective-permute-start | bytes 294920 | tf_op jit(solution)/shard_map/ppermute | solution.py:284
  12.0 8.8 %collective-permute-start.9 = (bf16[128,384]{1,0:T(8,128)(2,1)S(1)}, bf16[128,384]{1,0:T(8,128)(2,1)S(1)}, u32[]{:S(2)}, u32[]{:S(2)}) collective-permute-start(bf16[128,384]{1,0:T(8,128)(2,1)S(1)} %get-tuple-element.26), channel_id=1, source_target_pairs={{0,6},{1,7},{2,0},{3,1},{4,2},{5,3},{6,4},{7,5},{8,14},{9,15},{10,... | collective-permute-start | bytes 294920 | tf_op jit(solution)/shard_map/ppermute | solution.py:284
  18.6 6.1 %collective-permute-start.6 = (bf16[256,384]{1,0:T(8,128)(2,1)S(1)}, bf16[256,384]{1,0:T(8,128)(2,1)S(1)}, u32[]{:S(2)}, u32[]{:S(2)}) collective-permute-start(bf16[256,384]{1,0:T(8,128)(2,1)S(1)} %constant_dynamic-update-slice_fusion.4.refs_2_), channel_id=1, source_target_pairs={{0,16},{8,24},{16,0},{24,8},{1,17},{9,25},{17,1},{25,9},{2,18},{10... | collective-permute-start | bytes 589832 | tf_op jit(solution)/shard_map/ppermute | solution.py:290
  20.8 6.9 %collective-permute-start.10 = (bf16[256,384]{1,0:T(8,128)(2,1)S(1)}, bf16[256,384]{1,0:T(8,128)(2,1)S(1)}, u32[]{:S(2)}, u32[]{:S(2)}) collective-permute-start(bf16[256,384]{1,0:T(8,128)(2,1)S(1)} %constant_dynamic-update-slice_fusion.6.refs_6_), channel_id=1, source_target_pairs={{0,8},{8,0},{16,24},{24,16},{1,9},{9,1},{17,25},{25,17},{2,10},{10... | collective-permute-start | bytes 589832 | tf_op jit(solution)/shard_map/ppermute | solution.py:290
  22.4 6.9 %collective-permute-start.3 = (bf16[256,384]{1,0:T(8,128)(2,1)S(1)}, bf16[256,384]{1,0:T(8,128)(2,1)S(1)}, u32[]{:S(2)}, u32[]{:S(2)}) collective-permute-start(bf16[256,384]{1,0:T(8,128)(2,1)S(1)} %constant_dynamic-update-slice_fusion.refs_0_), channel_id=1, source_target_pairs={{0,1},{1,0},{2,3},{3,2},{4,5},{5,4},{6,7},{7,6},{8,9},{9,8},{10,11... | collective-permute-start | bytes 589832 | tf_op jit(solution)/shard_map/ppermute | solution.py:287
  22.5 9.4 %collective-permute-start.5 = (bf16[256,384]{1,0:T(8,128)(2,1)S(1)}, bf16[256,384]{1,0:T(8,128)(2,1)S(1)}, u32[]{:S(2)}, u32[]{:S(2)}) collective-permute-start(bf16[256,384]{1,0:T(8,128)(2,1)S(1)} %constant_dynamic-update-slice_fusion.4.refs_2_), channel_id=1, source_target_pairs={{0,8},{8,0},{16,24},{24,16},{1,9},{9,1},{17,25},{25,17},{2,10},{10... | collective-permute-start | bytes 589832 | tf_op jit(solution)/shard_map/ppermute | solution.py:290
  23.1 8.9 %collective-permute-start.11 = (bf16[256,384]{1,0:T(8,128)(2,1)S(1)}, bf16[256,384]{1,0:T(8,128)(2,1)S(1)}, u32[]{:S(2)}, u32[]{:S(2)}) collective-permute-start(bf16[256,384]{1,0:T(8,128)(2,1)S(1)} %constant_dynamic-update-slice_fusion.6.refs_6_), channel_id=1, source_target_pairs={{0,16},{8,24},{16,0},{24,8},{1,17},{9,25},{17,1},{25,9},{2,18},{10... | collective-permute-start | bytes 589832 | tf_op jit(solution)/shard_map/ppermute | solution.py:290
  24.6 10.5 %collective-permute-start.7 = (bf16[256,384]{1,0:T(8,128)(2,1)S(1)}, bf16[256,384]{1,0:T(8,128)(2,1)S(1)}, u32[]{:S(2)}, u32[]{:S(2)}) collective-permute-start(bf16[256,384]{1,0:T(8,128)(2,1)S(1)} %collective-permute-done.6.refs_4_), channel_id=1, source_target_pairs={{0,8},{8,0},{16,24},{24,16},{1,9},{9,1},{17,25},{25,17},{2,10},{10... | collective-permute-start | bytes 589832 | tf_op jit(solution)/shard_map/ppermute | solution.py:290
  27.7 7.4 %collective-permute-start.12 = (bf16[256,384]{1,0:T(8,128)(2,1)S(1)}, bf16[256,384]{1,0:T(8,128)(2,1)S(1)}, u32[]{:S(2)}, u32[]{:S(2)}) collective-permute-start(bf16[256,384]{1,0:T(8,128)(2,1)S(1)} %collective-permute-done.10.refs_7_), channel_id=1, source_target_pairs={{0,16},{8,24},{16,0},{24,8},{1,17},{9,25},{17,1},{25,9},{2,18},{10... | collective-permute-start | bytes 589832 | tf_op jit(solution)/shard_map/ppermute | solution.py:290
  117.3 2.7 %collective-permute-start.13 = (f32[512,384]{1,0:T(8,128)S(1)}, f32[512,384]{1,0:T(8,128)S(1)}, u32[]{:S(2)}, u32[]{:S(2)}) collective-permute-start(f32[512,384]{1,0:T(8,128)S(1)} %get-tuple-element.33), channel_id=1, source_target_pairs={{0,1},{1,0},{2,3},{3,2},{4,5},{5,4},{6,7},{7,6},{8,9},{9,8},{10,11... | collective-permute-start | bytes 2359304 | tf_op jit(solution)/shard_map/ppermute | solution.py:287
  117.4 14.0 %copy-start = (bf16[768,768]{1,0:T(8,128)(2,1)S(1)}, bf16[768,768]{1,0:T(8,128)(2,1)}, u32[]{:S(2)}) copy-start(bf16[768,768]{1,0:T(8,128)(2,1)} %refs_4_.1) | copy-start | bytes 3538948
  117.4 2.6 %collective-permute-start.14 = (f32[512,128]{1,0:T(8,128)S(1)}, f32[512,128]{1,0:T(8,128)S(1)}, u32[]{:S(2)}, u32[]{:S(2)}) collective-permute-start(f32[512,128]{1,0:T(8,128)S(1)} %get-tuple-element.35), channel_id=1, source_target_pairs={{0,1},{1,0},{2,3},{3,2},{4,5},{5,4},{6,7},{7,6},{8,9},{9,8},{10,11... | collective-permute-start | bytes 786440 | tf_op jit(solution)/shard_map/ppermute | solution.py:287
  121.0 6.6 %collective-permute-start.15 = (bf16[64,384]{1,0:T(8,128)(2,1)S(1)}, bf16[64,384]{1,0:T(8,128)(2,1)S(1)}, u32[]{:S(2)}, u32[]{:S(2)}) collective-permute-start(bf16[64,384]{1,0:T(8,128)(2,1)S(1)} %get-tuple-element.30), channel_id=1, source_target_pairs={{0,6},{1,7},{2,0},{3,1},{4,2},{5,3},{6,4},{7,5},{8,14},{9,15},{10,... | collective-permute-start | bytes 147464 | tf_op jit(solution)/shard_map/ppermute | solution.py:284
  125.5 5.3 %collective-permute-start.16 = (bf16[64,384]{1,0:T(8,128)(2,1)S(1)}, bf16[64,384]{1,0:T(8,128)(2,1)S(1)}, u32[]{:S(2)}, u32[]{:S(2)}) collective-permute-start(bf16[64,384]{1,0:T(8,128)(2,1)S(1)} %get-tuple-element.31), channel_id=1, source_target_pairs={{0,4},{1,5},{2,6},{3,7},{4,0},{5,1},{6,2},{7,3},{8,12},{9,13},{10,... | collective-permute-start | bytes 147464 | tf_op jit(solution)/shard_map/ppermute | solution.py:284
  125.5 5.9 %collective-permute-start.17 = (bf16[64,384]{1,0:T(8,128)(2,1)S(1)}, bf16[64,384]{1,0:T(8,128)(2,1)S(1)}, u32[]{:S(2)}, u32[]{:S(2)}) collective-permute-start(bf16[64,384]{1,0:T(8,128)(2,1)S(1)} %get-tuple-element.32), channel_id=1, source_target_pairs={{0,2},{1,3},{2,4},{3,5},{4,6},{5,7},{6,0},{7,1},{8,10},{9,11},{10,... | collective-permute-start | bytes 147464 | tf_op jit(solution)/shard_map/ppermute | solution.py:284

commit v2 on v1

v2 whole, which is shorter than its diff:
```python
import functools

import jax
import jax.numpy as jnp
from jax import lax
from jax.experimental import pallas as pl
from jax.experimental.pallas import tpu as pltpu
from jax.sharding import PartitionSpec as P

HEAD_DIM = 64
GROUPS = 4
LANES = 128
MARK = 100.0
MARK_TEST = 64.0
SAFE = 64.0
LOW = -1e30
ONES = 16
MOST_QUERIES = 1024
MOST_KEYS = 2048
LIMIT = 1e30
BF16 = jnp.bfloat16
F32 = jnp.float32
VMEM = pl.BlockSpec(memory_space=pltpu.VMEM)
NT = (((1,), (1,)), ((), ()))
TN = (((0,), (0,)), ((), ()))


MIB = 1024 * 1024


def params(mib=32):
    return pltpu.CompilerParams(vmem_limit_bytes=mib * MIB)


def lower_lanes(shape):
    return lax.broadcasted_iota(jnp.int32, shape, 1) < HEAD_DIM


def swap_halves(x):
    return pltpu.roll(x, HEAD_DIM, 1)


def pack_kernel(rest, per_group, q_hbm, k_hbm, v_hbm, valid_hbm, *refs):
    outs, (q_ref, k_ref, v_ref, valid_ref, sems) = refs[:GROUPS], refs[GROUPS:]
    copies = [
        pltpu.make_async_copy(src, dst, sems.at[i])
        for i, (src, dst) in enumerate(
            ((valid_hbm, valid_ref), (k_hbm, k_ref), (v_hbm, v_ref), (q_hbm, q_ref))
        )
    ]
    for copy in copies:
        copy.start()
    mine = lax.axis_index("inner") // rest
    rows = q_ref.shape[0]
    half = rows // 2
    for copy in copies:
        copy.wait()
    square = (rows, rows)
    on_diagonal = lax.broadcasted_iota(jnp.int32, square, 0) == lax.broadcasted_iota(
        jnp.int32, square, 1
    )
    flag_row = jnp.broadcast_to(valid_ref[...].astype(F32), square)
    picked = jnp.where(on_diagonal, flag_row, 0.0).astype(BF16)
    flags = jnp.dot(picked, jnp.ones((rows, LANES), BF16), preferred_element_type=F32) > 0.5
    low = lower_lanes((rows, LANES))
    low_half = lower_lanes((half, LANES))
    kv_groups, q_groups = [], []
    for g in range(GROUPS):
        kv_slots, q_slots = [], []
        for j in range(per_group):
            h = g * per_group + j
            tile = pl.ds((h // 2) * LANES, LANES)
            k = k_ref[:, tile].astype(F32)
            v = v_ref[:, tile].astype(F32)
            q = q_ref[:, tile].astype(F32) * (HEAD_DIM**-0.5)
            if h % 2 == 0:
                kv = jnp.where(low, k, swap_halves(v))
                qq = jnp.where(low_half, q[:half], swap_halves(q[half:]))
            else:
                kv = jnp.where(low, swap_halves(k), v)
                qq = jnp.where(low_half, swap_halves(q[:half]), q[half:])
            kv_slots.append(jnp.where(flags, kv, MARK))
            q_slots.append(qq)
        kv_groups.append(kv_slots)
        q_groups.append(q_slots)
    for s in range(GROUPS):
        want = lax.rem(mine + s, GROUPS)
        for j in range(per_group):
            lanes = pl.ds(j * LANES, LANES)
            for groups, start, n in ((kv_groups, 0, rows), (q_groups, rows, half)):
                x = groups[0][j]
                for g in range(1, GROUPS):
                    x = jnp.where(want == g, groups[g][j], x)
                outs[s][pl.ds(start, n), lanes] = x.astype(BF16)


def pack(q, k, v, valid, rest):
    rows, width = q.shape
    per_group = width // HEAD_DIM // GROUPS
    slots = per_group * LANES
    return pl.pallas_call(
        functools.partial(pack_kernel, rest, per_group),
        out_shape=[jax.ShapeDtypeStruct((rows + rows // 2, slots), BF16)] * GROUPS,
        in_specs=[pl.BlockSpec(memory_space=pltpu.HBM)] * 4,
        out_specs=[VMEM] * GROUPS,
        scratch_shapes=[pltpu.VMEM((rows, width), BF16)] * 3
        + [pltpu.VMEM((1, rows), jnp.int32), pltpu.SemaphoreType.DMA((4,))],
        compiler_params=params(24),
    )(*[pltpu.with_memory_space_constraint(x, pltpu.HBM) for x in (q, k, v, valid.reshape(1, rows))])


def spread_queries(refs, half, qs):
    start = 0
    for ref in refs:
        for piece in range(ref.shape[0] // half):
            for j in range(qs.shape[1] // LANES):
                lanes = pl.ds(j * LANES, LANES)
                x = ref[pl.ds(piece * half, half), lanes].astype(F32)
                low = lower_lanes(x.shape)
                qs[pl.ds(start, half), lanes] = jnp.where(low, x, 0.0).astype(BF16)
                qs[pl.ds(start + half, half), lanes] = jnp.where(low, swap_halves(x), 0.0).astype(BF16)
            start += 2 * half


def spread_keys(refs, ks, vs):
    start = 0
    for ref in refs:
        n = ref.shape[0]
        for j in range(ks.shape[1] // LANES):
            lanes = pl.ds(j * LANES, LANES)
            x = ref[:, lanes]
            hole = x > jnp.asarray(MARK_TEST, BF16)
            low = lower_lanes(x.shape)
            zero = jnp.zeros_like(x)
            x = jnp.where(hole, zero, x)
            ks[pl.ds(start, n), lanes] = x
            vs[pl.ds(start, n), lanes] = jnp.where(low, jnp.where(hole, zero, jnp.ones_like(x)), x)
        start += n


def largest_norm(ref):
    pick = (lax.broadcasted_iota(jnp.int32, (LANES, LANES), 0) < HEAD_DIM).astype(BF16)
    best = None
    for j in range(ref.shape[1] // LANES):
        x = ref[:, pl.ds(j * LANES, LANES)]
        norms = jnp.dot(x * x, pick, preferred_element_type=F32)
        best = norms if best is None else jnp.maximum(best, norms)
    return jnp.max(best, axis=0, keepdims=True)[0, 0]


def add_keys(cols, qs, ks, vs, acc, top, safe, fresh):
    slots = ks.shape[1] // LANES
    rows_k = ks.shape[0]

    @pl.when(safe)
    def _():
        for j in range(slots):
            lanes = pl.ds(j * LANES, LANES)
            for col in range(0, cols, MOST_QUERIES):
                at = pl.ds(col, min(MOST_QUERIES, cols - col))
                total = None if fresh else acc[lanes, at]
                for row in range(0, rows_k, MOST_KEYS):
                    ka = pl.ds(row, min(MOST_KEYS, rows_k - row))
                    s = lax.dot_general(ks[ka, lanes], qs[at, lanes], NT, preferred_element_type=F32)
                    p = jnp.exp(s).astype(BF16)
                    term = lax.dot_general(vs[ka, lanes], p, TN, preferred_element_type=F32)
                    total = term if total is None else total + term
                acc[lanes, at] = total

    @pl.when(jnp.logical_not(safe))
    def _():
        step_q, step_k = 128, 128
        if fresh:
            acc[...] = jnp.zeros_like(acc)

        def over_queries(i, unused):
            at = pl.ds(pl.multiple_of(i * step_q, step_q), step_q)
            for j in range(slots):
                lanes = pl.ds(j * LANES, LANES)

                def over_keys(c, carry):
                    high, total = carry
                    ka = pl.ds(pl.multiple_of(c * step_k, step_k), step_k)
                    v = vs[ka, lanes]
                    s = lax.dot_general(ks[ka, lanes], qs[at, lanes], NT, preferred_element_type=F32)
                    s = jnp.where(v[:, :1].astype(F32) > 0.5, s, LOW)
                    best = jnp.max(s, axis=0, keepdims=True)
                    best = (best + jnp.abs(best) * (1.0 / 128)).astype(BF16).astype(F32)
                    new = jnp.maximum(high, best)
                    p = jnp.exp(s - new).astype(BF16)
                    total = total * jnp.exp(high - new) + lax.dot_general(v, p, TN, preferred_element_type=F32)
                    return new, total

                high, total = lax.fori_loop(0, rows_k // step_k, over_keys, (top[pl.ds(j, 1), at], acc[lanes, at]))
                acc[lanes, at] = total
                top[pl.ds(j, 1), at] = high
            return unused

        lax.fori_loop(0, cols // step_q, over_queries, 0)


def attend_kernel(n_q, n_kv, half, first, n_export, *refs):
    q_refs, refs = refs[:n_q], refs[n_q:]
    kv_refs, refs = refs[:n_kv], refs[n_kv:]
    if first:
        qs, acc, top, info = refs[:4]
        exports, (ks, vs) = refs[4 : 4 + n_export], refs[4 + n_export :]
        spread_queries(q_refs, half, qs)
        top[...] = jnp.zeros_like(top)
        length = largest_norm(qs)
    else:
        qs = q_refs[0]
        unused_acc, unused_top, info_in, acc, top, info = refs[:6]
        exports, (ks, vs) = refs[6 : 6 + n_export], refs[6 + n_export :]
        length = info_in[...][0, 0]
    spread_keys(kv_refs, ks, vs)
    safe = length * largest_norm(ks) * 1.05 <= SAFE * SAFE
    info[...] = jnp.full(info.shape, jnp.where(safe, length, LIMIT), F32)
    add_keys(qs.shape[0], qs, ks, vs, acc, top, safe, first)
    cols = qs.shape[0] // (n_export + 1)
    for i, out in enumerate(exports):
        at = pl.ds((i + 1) * cols, cols)
        for j in range(qs.shape[1] // LANES):
            start = j * (HEAD_DIM + 2 * ONES)
            out[pl.ds(start, HEAD_DIM), :] = acc[pl.ds(j * LANES + HEAD_DIM, HEAD_DIM), at].astype(BF16)
            out[pl.ds(start + HEAD_DIM, ONES), :] = acc[pl.ds(j * LANES, ONES), at].astype(BF16)
            shift = jnp.broadcast_to(top[pl.ds(j, 1), at], (ONES, cols))
            out[pl.ds(start + HEAD_DIM + ONES, ONES), :] = shift.astype(BF16)


def attend(q_list, kv_list, half, state, n_export=0):
    width = q_list[0].shape[1]
    slots = width // LANES
    first = state is None
    rows_q = sum(q.shape[0] for q in q_list) * (2 if first else 1)
    rows_k = sum(k.shape[0] for k in kv_list)
    args = list(q_list) + list(kv_list) + ([] if first else list(state))
    out_shape = [jax.ShapeDtypeStruct((rows_q, width), BF16)] if first else []
    out_shape += [
        jax.ShapeDtypeStruct((width, rows_q), F32),
        jax.ShapeDtypeStruct((8, rows_q), F32),
        jax.ShapeDtypeStruct((8, LANES), F32),
    ]
    sent = (slots * (HEAD_DIM + 2 * ONES), rows_q // (n_export + 1))
    out_shape += [jax.ShapeDtypeStruct(sent, BF16)] * n_export
    out = pl.pallas_call(
        functools.partial(attend_kernel, len(q_list), len(kv_list), half, first, n_export),
        out_shape=out_shape,
        in_specs=[VMEM] * len(args),
        out_specs=[VMEM] * len(out_shape),
        scratch_shapes=[pltpu.VMEM((rows_k, width), BF16)] * 2,
        input_output_aliases={} if first else {len(args) - 3: 0, len(args) - 2: 1},
        compiler_params=params(),
        cost_estimate=pl.CostEstimate(
            flops=16 * rows_q * rows_k * width,
            bytes_accessed=4 * rows_q * width,
            transcendentals=rows_q * rows_k * slots,
        ),
    )(*args)
    out = list(out) if first else [q_list[0]] + list(out)
    return out[0], out[1:4], out[4:]


def finish_kernel(n_import, slots, acc, top, *refs):
    imports, outs = refs[:n_import], refs[n_import:]
    piece = outs[0].shape[1]
    step = HEAD_DIM + 2 * ONES
    for i, out in enumerate(outs):
        at = pl.ds(i * piece, piece)
        for j in range(slots):
            total = acc[pl.ds(j * LANES + HEAD_DIM, HEAD_DIM), at]
            count = acc[pl.ds(j * LANES, 1), at]
            high = top[pl.ds(j, 1), at]
            for ref in imports:
                values = ref[pl.ds(j * step, HEAD_DIM), at].astype(F32)
                sums = ref[pl.ds(j * step + HEAD_DIM, ONES), at].astype(F32)[:1]
                shift = ref[pl.ds(j * step + HEAD_DIM + ONES, ONES), at].astype(F32)[:1]
                new = jnp.maximum(high, shift)
                mine, theirs = jnp.exp(high - new), jnp.exp(shift - new)
                total = total * mine + values * theirs
                count = count * mine + sums * theirs
                high = new
            share = 1.0 / (count + jnp.exp(-high))
            out[pl.ds(j * HEAD_DIM, HEAD_DIM), :] = (total * share).astype(BF16)


def finish(state, imports, n_out):
    acc, top, unused = state
    slots = acc.shape[0] // LANES
    piece = acc.shape[1] // (len(imports) + 1) // n_out
    return pl.pallas_call(
        functools.partial(finish_kernel, len(imports), slots),
        out_shape=[jax.ShapeDtypeStruct((slots * HEAD_DIM, piece), BF16)] * n_out,
        in_specs=[VMEM] * (2 + len(imports)),
        out_specs=[VMEM] * n_out,
        compiler_params=params(),
    )(acc, top, *imports)


def project_kernel(rest, *refs):
    parts, w_ref, out = refs[:GROUPS], refs[GROUPS], refs[GROUPS + 1]
    mine = lax.axis_index("inner") // rest
    rows = parts[0].shape[0]
    total = None
    for s, part in enumerate(parts):
        g = lax.rem(mine + s, GROUPS)
        w = w_ref[pl.ds(pl.multiple_of(g * rows, 16), rows), :]
        term = lax.dot_general(part[...], w, TN, preferred_element_type=F32)
        total = term if total is None else total + term
    out[...] = total.astype(BF16)


def project(parts, w, rest):
    return pl.pallas_call(
        functools.partial(project_kernel, rest),
        out_shape=jax.ShapeDtypeStruct((parts[0].shape[1], w.shape[1]), BF16),
        in_specs=[VMEM] * (GROUPS + 1),
        out_specs=VMEM,
        compiler_params=params(),
    )(*parts, w)


def on_device(n_blk, n_inner, q, k, v, valid, w):
    rest = n_inner // GROUPS
    half = q.shape[0] // 2

    def over_groups(x, s):
        return lax.ppermute(x, "inner", [(i, (i + s * rest) % n_inner) for i in range(n_inner)])

    def over_rest(x, t):
        return lax.ppermute(x, "inner", [(i, i // rest * rest + (i + t) % rest) for i in range(n_inner)])

    def over_blk(x, t):
        return lax.ppermute(x, "blk", [(i, (i + t) % n_blk) for i in range(n_blk)])

    def along(first, second):
        return [
            (b * n_inner + i, (b ^ (second if i % 2 else first)) * n_inner + i)
            for b in range(n_blk)
            for i in range(n_inner)
        ]

    def near(chunk):
        return [lax.ppermute(chunk, ("blk", "inner"), along(d, d)) for d in (1, 2)]

    def passed(blocks):
        return jnp.where(lax.axis_index("inner") % 2 == 0, *blocks)

    def far(block):
        return lax.ppermute(block, ("blk", "inner"), along(2, 1))

    def after(x, *done):
        return lax.optimization_barrier((x, *done))[0]

    def diagonal(chunk):
        return lax.ppermute(chunk, ("blk", "inner"), along(3, 3))

    pieces = list(pack(q, k, v, valid, rest))
    rows = q.shape[0]

    def gathered_queries(pieces):
        own = jnp.concatenate([x[rows:] for x in pieces], axis=0)
        return [own] + [over_rest(own, t) for t in range(1, rest)]

    if n_blk == 4 and rest == 2:
        near0 = near(pieces[0][:rows])
        pieces[1], pieces[3] = over_groups(pieces[1], 1), over_groups(pieces[3], 3)
        pieces[2] = over_groups(after(pieces[2], pieces[1], pieces[3]), 2)
        chunk1 = jnp.concatenate([pieces[1][:rows], pieces[3][:rows]], axis=0)
        near1 = near(chunk1)
        far0 = far(passed(near0))
        near1 = after(tuple(near1), far0)
        far1 = far(passed(near1))
        chunk2 = after(pieces[2], *near1)[:rows]
        blocks2 = [*near(chunk2), diagonal(chunk2)]
        q_list = gathered_queries(pieces)
        chunks = [pieces[0][:rows], chunk1, chunk2]
        queries, state, unused = attend(q_list, [*chunks, *near0, far0, *near1], half, None)
        queries, state, exports = attend([queries], [far1, *blocks2], half, state, rest - 1)
    else:
        pieces = [pieces[0]] + [over_groups(pieces[s], s) for s in range(1, GROUPS)]
        kv = [x[:rows] for x in pieces]
        q_list = gathered_queries(pieces)
        chunk = jnp.concatenate(kv, axis=0)
        blocks = [chunk] + [over_blk(chunk, t) for t in range(1, n_blk)]
        queries, state, exports = attend(q_list, blocks, half, None, rest - 1)
    imports = [over_rest(x, rest - 1 - t) for t, x in enumerate(exports)]
    parts = list(finish(state, imports, GROUPS))
    parts = [parts[0]] + [over_groups(parts[s], GROUPS - s) for s in range(1, GROUPS)]
    return project(parts, w, rest)


def solution(mesh):
    rows = P(("blk", "inner"), None)
    return jax.shard_map(
        functools.partial(on_device, mesh.shape["blk"], mesh.shape["inner"]),
        mesh=mesh,
        in_specs=(rows, rows, rows, P(("blk", "inner")), P()),
        out_specs=rows,
        check_vma=False,
    )
```

time: 133 us -> 171 us (1.29)
  Pallas kernels: 84.6 us -> 134 us
  starting transfers between devices: 25 us -> 19.9 us
  local copies, waits for them, and re-layouts: 3.68 us -> 0.07 us
  waiting for transfers between devices: 19 us -> 17.1 us
    pallas_call x1 -> x2, Pallas kernels: 82 us -> 131 us  [attend(): pl.pallas_call(functools.partial(attend_kernel, len(q_list), len(kv_list)...]
    ppermute x6 -> x9, waiting for transfers between devices: 7.4 us -> 0.02 us  [the longest x6 0.02 us: near(): return [lax.ppermute(chunk, ('blk', 'inner'), along(d, d)) for d in (1, 2)]]
    ppermute x9 -> x6, starting transfers between devices: 16 us -> 8.86 us  [over_groups(): lax.ppermute(x, 'inner', [(i, (i + s * rest) % n_inner) for i in range(n_...]
    ppermute x9 -> x6, waiting for transfers between devices: 9.59 us -> 15.5 us  [over_groups(): lax.ppermute(x, 'inner', [(i, (i + s * rest) % n_inner) for i in range(n_...]
    unnamed x15 -> x2, local copies, waits for them, and re-layouts: 3.49 us -> 0.01 us
    ppermute x6 -> x9, starting transfers between devices: 8.34 us -> 11 us  [the longest x6 9.33 us: near(): return [lax.ppermute(chunk, ('blk', 'inner'), along(d, d)) for d in (1, 2)]]
  transfers between devices with their start and end apart: 18 -> 17, of which waited for: 9 -> 6; matrix products, arithmetic and copies ran while one was open for 0% -> 0% of each run, Pallas kernels for 0% -> 52%
where the time goes in v2:
time: 171 us
  Pallas kernels  134 us (78%)
  starting transfers between devices  19.9 us (12%)
  waiting for transfers between devices  17.1 us (10%)
    pallas_call x2, Pallas kernels, attend(): pl.pallas_call(functools.partial(attend_kernel, len(q_list), len(kv_list)...  131 us
    ppermute x6, waiting for transfers between devices, over_groups(): lax.ppermute(x, 'inner', [(i, (i + s * rest) % n_inner) for i in range(n_...  15.5 us
    ppermute x6, starting transfers between devices, near(): return [lax.ppermute(chunk, ('blk', 'inner'), along(d, d)) for d in (1, 2)]  9.33 us
    ppermute x6, starting transfers between devices, over_groups(): lax.ppermute(x, 'inner', [(i, (i + s * rest) % n_inner) for i in range(n_...  8.86 us
  transfers between devices with their start and end apart: 17, of which 6 were waited for; matrix products, arithmetic and copies ran while one was open for 0% of the time, Pallas kernels for 52%

profile of v2, /device:TPU:0, one launch (start us, length us, event | category | flops | bytes accessed | tf_op | source)
XLA Modules:
  0.0 171.3 jit_solution(14299307664998476814)
XLA Ops:
  0.0 1.6 shard_map.55
  1.6 3.1 %collective-permute-start = (bf16[192,384]{1,0:T(8,128)(2,1)S(1)}, bf16[192,384]{1,0:T(8,128)(2,1)S(1)}, u32[]{:S(2)}, u32[]{:S(2)}) collective-permute-start(bf16[192,384]{1,0:T(8,128)(2,1)S(1)} %get-tuple-element.25), channel_id=1, source_target_pairs={{0,2},{1,3},{2,4},{3,5},{4,6},{5,7},{6,0},{7,1},{8,10},{9,11},{10,... | collective-permute-start | bytes 442376 | tf_op jit(solution)/shard_map/ppermute | solution.py:328
  4.7 2.1 %collective-permute-start.1 = (bf16[192,384]{1,0:T(8,128)(2,1)S(1)}, bf16[192,384]{1,0:T(8,128)(2,1)S(1)}, u32[]{:S(2)}, u32[]{:S(2)}) collective-permute-start(bf16[192,384]{1,0:T(8,128)(2,1)S(1)} %get-tuple-element.27), channel_id=1, source_target_pairs={{0,6},{1,7},{2,0},{3,1},{4,2},{5,3},{6,4},{7,5},{8,14},{9,15},{10,... | collective-permute-start | bytes 442376 | tf_op jit(solution)/shard_map/ppermute | solution.py:328
  6.8 1.7 %collective-permute-start.7 = (bf16[128,384]{1,0:T(8,128)(2,1)S(1)}, bf16[128,384]{1,0:T(8,128)(2,1)S(1)}, u32[]{:S(2)}, u32[]{:S(2)}) collective-permute-start(bf16[128,384]{1,0:T(8,128)(2,1)S(1)} %slice.29.refs_2_), channel_id=1, source_target_pairs={{0,16},{1,17},{2,18},{3,19},{4,20},{5,21},{6,22},{7,23},{8,24},{9,... | collective-permute-start | bytes 294920 | tf_op jit(solution)/shard_map/ppermute | solution.py:344
  8.5 1.5 collective-permute-start.6
  10.0 1.4 collective-permute-done
  11.4 1.7 collective-permute-done.1
  13.2 1.6 collective-permute-start.5
  14.8 1.5 collective-permute-start.4
  16.3 1.3 collective-permute-start.2
  17.6 0.6 collective-permute-start.8
  18.2 6.7 %collective-permute-done.2 = bf16[192,384]{1,0:T(8,128)(2,1)S(1)} collective-permute-done((bf16[192,384]{1,0:T(8,128)(2,1)S(1)}, bf16[192,384]{1,0:T(8,128)(2,1)S(1)}, u32[]{:S(2)}, u32[]{:S(2)}) %collective-permute-start.2) | collective-permute-done | bytes 147488 | tf_op jit(solution)/shard_map/ppermute | solution.py:328
  25.1 0.5 collective-permute-start.12
  25.6 1.5 collective-permute-start.11
  27.1 1.5 collective-permute-start.10
  28.7 0.6 collective-permute-start.9
  29.2 89.7 %shard_map.56 = (bf16[1024,384]{1,0:T(8,128)(2,1)S(1)}, f32[384,1024]{1,0:T(8,128)S(1)}, f32[8,1024]{1,0:T(8,128)S(1)}, f32[8,128]{1,0:T(8,128)S(1)}) custom-call(bf16[256,384]{1,0:T(8,128)(2,1)S(1)} %pad_maximum_fusion.refs_0_, bf16[256,384]{1,0:T(8,128)(2,1)S(1)} %collective-permute-done.3.refs_1_, bf16[128,384]{1,0:T(8,128)(2,1)S(1)} %slice.29.refs_2_, ...), custom_call_target="tpu_custom_call" | custom-call | flops 8858370048 | bytes 1572864 | tf_op jit(solution)/shard_map/pallas_call | solution.py:246
  119.0 41.4 %shard_map.57 = (f32[384,1024]{1,0:T(8,128)S(1)}, f32[8,1024]{1,0:T(8,128)S(1)}, f32[8,128]{1,0:T(8,128)}, bf16[288,512]{1,0:T(8,128)(2,1)S(1)}) custom-call(bf16[1024,384]{1,0:T(8,128)(2,1)S(1)} %get-tuple-element.32.refs_0_, bf16[256,384]{1,0:T(8,128)(2,1)S(1)} %collective-permute-done.9.refs_1_, ...), custom_call_target="tpu_custom_call", output_to_operand_aliasing={{0}: (5, {}), {1}: (6, {})} | custom-call | flops 4026531840 | bytes 1572864 | tf_op jit(solution)/shard_map/pallas_call | solution.py:246
  160.4 1.6 collective-permute-done.13.refs_0_
  162.1 1.7 %collective-permute-start.14 = (bf16[192,128]{1,0:T(8,128)(2,1)S(1)}, bf16[192,128]{1,0:T(8,128)(2,1)S(1)}, u32[]{:S(2)}, u32[]{:S(2)}) collective-permute-start(bf16[192,128]{1,0:T(8,128)(2,1)S(1)} %get-tuple-element.40), channel_id=1, source_target_pairs={{0,6},{1,7},{2,0},{3,1},{4,2},{5,3},{6,4},{7,5},{8,14},{9,15},{10,... | collective-permute-start | bytes 147464 | tf_op jit(solution)/shard_map/ppermute | solution.py:328
  163.8 0.6 collective-permute-start.16
  164.5 1.8 %collective-permute-done.14.refs_1_ = bf16[192,128]{1,0:T(8,128)(2,1)S(1)} collective-permute-done((bf16[192,128]{1,0:T(8,128)(2,1)S(1)}, bf16[192,128]{1,0:T(8,128)(2,1)S(1)}, u32[]{:S(2)}, u32[]{:S(2)}) %collective-permute-start.14) | collective-permute-done | bytes 49184 | tf_op jit(solution)/shard_map/ppermute | solution.py:328
  166.2 3.9 %collective-permute-done.15.refs_2_ = bf16[192,128]{1,0:T(8,128)(2,1)S(1)} collective-permute-done((bf16[192,128]{1,0:T(8,128)(2,1)S(1)}, bf16[192,128]{1,0:T(8,128)(2,1)S(1)}, u32[]{:S(2)}, u32[]{:S(2)}) %collective-permute-start.15) | collective-permute-done | bytes 49184 | tf_op jit(solution)/shard_map/ppermute | solution.py:328
  170.2 1.1 shard_map.59
  (29 shorter events, 0.4 us)
Async XLA Ops:
  1.6 9.8 %collective-permute-start = (bf16[192,384]{1,0:T(8,128)(2,1)S(1)}, bf16[192,384]{1,0:T(8,128)(2,1)S(1)}, u32[]{:S(2)}, u32[]{:S(2)}) collective-permute-start(bf16[192,384]{1,0:T(8,128)(2,1)S(1)} %get-tuple-element.25), channel_id=1, source_target_pairs={{0,2},{1,3},{2,4},{3,5},{4,6},{5,7},{6,0},{7,1},{8,10},{9,11},{10,... | collective-permute-start | bytes 442376 | tf_op jit(solution)/shard_map/ppermute | solution.py:328
  4.7 8.5 %collective-permute-start.1 = (bf16[192,384]{1,0:T(8,128)(2,1)S(1)}, bf16[192,384]{1,0:T(8,128)(2,1)S(1)}, u32[]{:S(2)}, u32[]{:S(2)}) collective-permute-start(bf16[192,384]{1,0:T(8,128)(2,1)S(1)} %get-tuple-element.27), channel_id=1, source_target_pairs={{0,6},{1,7},{2,0},{3,1},{4,2},{5,3},{6,4},{7,5},{8,14},{9,15},{10,... | collective-permute-start | bytes 442376 | tf_op jit(solution)/shard_map/ppermute | solution.py:328
  6.8 10.8 %collective-permute-start.7 = (bf16[128,384]{1,0:T(8,128)(2,1)S(1)}, bf16[128,384]{1,0:T(8,128)(2,1)S(1)}, u32[]{:S(2)}, u32[]{:S(2)}) collective-permute-start(bf16[128,384]{1,0:T(8,128)(2,1)S(1)} %slice.29.refs_2_), channel_id=1, source_target_pairs={{0,16},{1,17},{2,18},{3,19},{4,20},{5,21},{6,22},{7,23},{8,24},{9,... | collective-permute-start | bytes 294920 | tf_op jit(solution)/shard_map/ppermute | solution.py:344
  8.5 9.1 %collective-permute-start.6 = (bf16[128,384]{1,0:T(8,128)(2,1)S(1)}, bf16[128,384]{1,0:T(8,128)(2,1)S(1)}, u32[]{:S(2)}, u32[]{:S(2)}) collective-permute-start(bf16[128,384]{1,0:T(8,128)(2,1)S(1)} %slice.29.refs_2_), channel_id=1, source_target_pairs={{0,8},{1,9},{2,10},{3,11},{4,12},{5,13},{6,14},{7,15},{8,0},{9,1},... | collective-permute-start | bytes 294920 | tf_op jit(solution)/shard_map/ppermute | solution.py:344
  13.2 11.8 %collective-permute-start.5 = (bf16[256,384]{1,0:T(8,128)(2,1)S(1)}, bf16[256,384]{1,0:T(8,128)(2,1)S(1)}, u32[]{:S(2)}, u32[]{:S(2)}) collective-permute-start(bf16[256,384]{1,0:T(8,128)(2,1)S(1)} %pad_maximum_fusion.1.refs_3_), channel_id=1, source_target_pairs={{0,16},{1,17},{2,18},{3,19},{4,20},{5,21},{6,22},{7,23},{8,24},{9,... | collective-permute-start | bytes 589832 | tf_op jit(solution)/shard_map/ppermute | solution.py:344
  14.8 10.3 %collective-permute-start.4 = (bf16[256,384]{1,0:T(8,128)(2,1)S(1)}, bf16[256,384]{1,0:T(8,128)(2,1)S(1)}, u32[]{:S(2)}, u32[]{:S(2)}) collective-permute-start(bf16[256,384]{1,0:T(8,128)(2,1)S(1)} %pad_maximum_fusion.1.refs_3_), channel_id=1, source_target_pairs={{0,8},{1,9},{2,10},{3,11},{4,12},{5,13},{6,14},{7,15},{8,0},{9,1},... | collective-permute-start | bytes 589832 | tf_op jit(solution)/shard_map/ppermute | solution.py:344
  16.3 8.6 %collective-permute-start.2 = (bf16[192,384]{1,0:T(8,128)(2,1)S(1)}, bf16[192,384]{1,0:T(8,128)(2,1)S(1)}, u32[]{:S(2)}, u32[]{:S(2)}) collective-permute-start(bf16[192,384]{1,0:T(8,128)(2,1)S(1)} %get-tuple-element.28), channel_id=1, source_target_pairs={{0,4},{1,5},{2,6},{3,7},{4,0},{5,1},{6,2},{7,3},{8,12},{9,13},{10,... | collective-permute-start | bytes 442376 | tf_op jit(solution)/shard_map/ppermute | solution.py:328
  17.6 7.4 %collective-permute-start.8 = (bf16[128,384]{1,0:T(8,128)(2,1)S(1)}, bf16[128,384]{1,0:T(8,128)(2,1)S(1)}, u32[]{:S(2)}, u32[]{:S(2)}) collective-permute-start(bf16[128,384]{1,0:T(8,128)(2,1)S(1)} %broadcast_select_fusion.1), channel_id=1, source_target_pairs={{0,16},{1,9},{2,18},{3,11},{4,20},{5,13},{6,22},{7,15},{8,24},{9,1... | collective-permute-start | bytes 294920 | tf_op jit(solution)/shard_map/ppermute | solution.py:350
  25.0 4.3 %collective-permute-start.3 = (bf16[256,384]{1,0:T(8,128)(2,1)S(1)}, bf16[256,384]{1,0:T(8,128)(2,1)S(1)}, u32[]{:S(2)}, u32[]{:S(2)}) collective-permute-start(bf16[256,384]{1,0:T(8,128)(2,1)S(1)} %pad_maximum_fusion.refs_0_), channel_id=1, source_target_pairs={{0,1},{1,0},{2,3},{3,2},{4,5},{5,4},{6,7},{7,6},{8,9},{9,8},{10,11... | collective-permute-start | bytes 589832 | tf_op jit(solution)/shard_map/ppermute | solution.py:331
  25.1 93.9 %collective-permute-start.12 = (bf16[128,384]{1,0:T(8,128)(2,1)S(1)}, bf16[128,384]{1,0:T(8,128)(2,1)S(1)}, u32[]{:S(2)}, u32[]{:S(2)}) collective-permute-start(bf16[128,384]{1,0:T(8,128)(2,1)S(1)} %slice.32.refs_4_), channel_id=1, source_target_pairs={{0,24},{1,25},{2,26},{3,27},{4,28},{5,29},{6,30},{7,31},{8,16},{9,... | collective-permute-start | bytes 294920 | tf_op jit(solution)/shard_map/ppermute | solution.py:356
  25.6 93.4 %collective-permute-start.11 = (bf16[128,384]{1,0:T(8,128)(2,1)S(1)}, bf16[128,384]{1,0:T(8,128)(2,1)S(1)}, u32[]{:S(2)}, u32[]{:S(2)}) collective-permute-start(bf16[128,384]{1,0:T(8,128)(2,1)S(1)} %slice.32.refs_4_), channel_id=1, source_target_pairs={{0,16},{1,17},{2,18},{3,19},{4,20},{5,21},{6,22},{7,23},{8,24},{9,... | collective-permute-start | bytes 294920 | tf_op jit(solution)/shard_map/ppermute | solution.py:344
  27.1 91.9 %collective-permute-start.10 = (bf16[128,384]{1,0:T(8,128)(2,1)S(1)}, bf16[128,384]{1,0:T(8,128)(2,1)S(1)}, u32[]{:S(2)}, u32[]{:S(2)}) collective-permute-start(bf16[128,384]{1,0:T(8,128)(2,1)S(1)} %slice.32.refs_4_), channel_id=1, source_target_pairs={{0,8},{1,9},{2,10},{3,11},{4,12},{5,13},{6,14},{7,15},{8,0},{9,1},... | collective-permute-start | bytes 294920 | tf_op jit(solution)/shard_map/ppermute | solution.py:344
  28.7 90.4 %collective-permute-start.9 = (bf16[256,384]{1,0:T(8,128)(2,1)S(1)}, bf16[256,384]{1,0:T(8,128)(2,1)S(1)}, u32[]{:S(2)}, u32[]{:S(2)}) collective-permute-start(bf16[256,384]{1,0:T(8,128)(2,1)S(1)} %broadcast_select_fusion), channel_id=1, source_target_pairs={{0,16},{1,9},{2,18},{3,11},{4,20},{5,13},{6,22},{7,15},{8,24},{9,1... | collective-permute-start | bytes 589832 | tf_op jit(solution)/shard_map/ppermute | solution.py:350
  160.4 9.8 %copy-start = (bf16[768,768]{1,0:T(8,128)(2,1)S(1)}, bf16[768,768]{1,0:T(8,128)(2,1)}, u32[]{:S(2)}) copy-start(bf16[768,768]{1,0:T(8,128)(2,1)} %refs_4_.1) | copy-start | bytes 3538948
  160.4 1.6 collective-permute-start.13
  162.1 4.1 %collective-permute-start.14 = (bf16[192,128]{1,0:T(8,128)(2,1)S(1)}, bf16[192,128]{1,0:T(8,128)(2,1)S(1)}, u32[]{:S(2)}, u32[]{:S(2)}) collective-permute-start(bf16[192,128]{1,0:T(8,128)(2,1)S(1)} %get-tuple-element.40), channel_id=1, source_target_pairs={{0,6},{1,7},{2,0},{3,1},{4,2},{5,3},{6,4},{7,5},{8,14},{9,15},{10,... | collective-permute-start | bytes 147464 | tf_op jit(solution)/shard_map/ppermute | solution.py:328
  163.8 6.3 %collective-permute-start.15 = (bf16[192,128]{1,0:T(8,128)(2,1)S(1)}, bf16[192,128]{1,0:T(8,128)(2,1)S(1)}, u32[]{:S(2)}, u32[]{:S(2)}) collective-permute-start(bf16[192,128]{1,0:T(8,128)(2,1)S(1)} %get-tuple-element.41), channel_id=1, source_target_pairs={{0,4},{1,5},{2,6},{3,7},{4,0},{5,1},{6,2},{7,3},{8,12},{9,13},{10,... | collective-permute-start | bytes 147464 | tf_op jit(solution)/shard_map/ppermute | solution.py:328
  163.8 6.3 %collective-permute-start.16 = (bf16[192,128]{1,0:T(8,128)(2,1)S(1)}, bf16[192,128]{1,0:T(8,128)(2,1)S(1)}, u32[]{:S(2)}, u32[]{:S(2)}) collective-permute-start(bf16[192,128]{1,0:T(8,128)(2,1)S(1)} %get-tuple-element.42), channel_id=1, source_target_pairs={{0,2},{1,3},{2,4},{3,5},{4,6},{5,7},{6,0},{7,1},{8,10},{9,11},{10,... | collective-permute-start | bytes 147464 | tf_op jit(solution)/shard_map/ppermute | solution.py:328

commit v3 on v2

v3 whole, which is shorter than its diff:
```python
import functools

import jax
import jax.numpy as jnp
from jax import lax
from jax.experimental import pallas as pl
from jax.experimental.pallas import tpu as pltpu
from jax.sharding import PartitionSpec as P

HEAD_DIM = 64
GROUPS = 4
LANES = 128
MARK = 100.0
MARK_TEST = 64.0
SAFE = 64.0
LOW = -1e30
ONES = 16
MOST_QUERIES = 1024
MOST_KEYS = 2048
LIMIT = 1e30
BF16 = jnp.bfloat16
F32 = jnp.float32
VMEM = pl.BlockSpec(memory_space=pltpu.VMEM)
NT = (((1,), (1,)), ((), ()))
TN = (((0,), (0,)), ((), ()))


MIB = 1024 * 1024


def params(mib=32):
    return pltpu.CompilerParams(vmem_limit_bytes=mib * MIB)


def lower_lanes(shape):
    return lax.broadcasted_iota(jnp.int32, shape, 1) < HEAD_DIM


def swap_halves(x):
    return pltpu.roll(x, HEAD_DIM, 1)


def pack_kernel(rest, per_group, q_hbm, k_hbm, v_hbm, valid_hbm, *refs):
    outs, (q_ref, k_ref, v_ref, valid_ref, sems) = refs[:GROUPS], refs[GROUPS:]
    copies = [
        pltpu.make_async_copy(src, dst, sems.at[i])
        for i, (src, dst) in enumerate(
            ((valid_hbm, valid_ref), (k_hbm, k_ref), (v_hbm, v_ref), (q_hbm, q_ref))
        )
    ]
    for copy in copies:
        copy.start()
    mine = lax.axis_index("inner") // rest
    rows = q_ref.shape[0]
    half = rows // 2
    for copy in copies:
        copy.wait()
    square = (rows, rows)
    on_diagonal = lax.broadcasted_iota(jnp.int32, square, 0) == lax.broadcasted_iota(
        jnp.int32, square, 1
    )
    flag_row = jnp.broadcast_to(valid_ref[...].astype(F32), square)
    picked = jnp.where(on_diagonal, flag_row, 0.0).astype(BF16)
    flags = jnp.dot(picked, jnp.ones((rows, LANES), BF16), preferred_element_type=F32) > 0.5
    low = lower_lanes((rows, LANES))
    low_half = lower_lanes((half, LANES))
    kv_groups, q_groups = [], []
    for g in range(GROUPS):
        kv_slots, q_slots = [], []
        for j in range(per_group):
            h = g * per_group + j
            tile = pl.ds((h // 2) * LANES, LANES)
            k = k_ref[:, tile].astype(F32)
            v = v_ref[:, tile].astype(F32)
            q = q_ref[:, tile].astype(F32) * (HEAD_DIM**-0.5)
            if h % 2 == 0:
                kv = jnp.where(low, k, swap_halves(v))
                qq = jnp.where(low_half, q[:half], swap_halves(q[half:]))
            else:
                kv = jnp.where(low, swap_halves(k), v)
                qq = jnp.where(low_half, swap_halves(q[:half]), q[half:])
            kv_slots.append(jnp.where(flags, kv, MARK))
            q_slots.append(qq)
        kv_groups.append(kv_slots)
        q_groups.append(q_slots)
    for s in range(GROUPS):
        want = jnp.bitwise_xor(mine, s)
        for j in range(per_group):
            lanes = pl.ds(j * LANES, LANES)
            for groups, start, n in ((kv_groups, 0, rows), (q_groups, rows, half)):
                x = groups[0][j]
                for g in range(1, GROUPS):
                    x = jnp.where(want == g, groups[g][j], x)
                outs[s][pl.ds(start, n), lanes] = x.astype(BF16)


def pack(q, k, v, valid, rest):
    rows, width = q.shape
    per_group = width // HEAD_DIM // GROUPS
    slots = per_group * LANES
    return pl.pallas_call(
        functools.partial(pack_kernel, rest, per_group),
        out_shape=[jax.ShapeDtypeStruct((rows + rows // 2, slots), BF16)] * GROUPS,
        in_specs=[pl.BlockSpec(memory_space=pltpu.HBM)] * 4,
        out_specs=[VMEM] * GROUPS,
        scratch_shapes=[pltpu.VMEM((rows, width), BF16)] * 3
        + [pltpu.VMEM((1, rows), jnp.int32), pltpu.SemaphoreType.DMA((4,))],
        compiler_params=params(24),
    )(*[pltpu.with_memory_space_constraint(x, pltpu.HBM) for x in (q, k, v, valid.reshape(1, rows))])


def spread_queries(refs, half, qs):
    start = 0
    for ref in refs:
        for piece in range(ref.shape[0] // half):
            for j in range(qs.shape[1] // LANES):
                lanes = pl.ds(j * LANES, LANES)
                x = ref[pl.ds(piece * half, half), lanes].astype(F32)
                low = lower_lanes(x.shape)
                qs[pl.ds(start, half), lanes] = jnp.where(low, x, 0.0).astype(BF16)
                qs[pl.ds(start + half, half), lanes] = jnp.where(low, swap_halves(x), 0.0).astype(BF16)
            start += 2 * half


def spread_keys(refs, ks, vs):
    start = 0
    for ref in refs:
        n = ref.shape[0]
        for j in range(ks.shape[1] // LANES):
            lanes = pl.ds(j * LANES, LANES)
            x = ref[:, lanes]
            hole = x > jnp.asarray(MARK_TEST, BF16)
            low = lower_lanes(x.shape)
            zero = jnp.zeros_like(x)
            x = jnp.where(hole, zero, x)
            ks[pl.ds(start, n), lanes] = x
            vs[pl.ds(start, n), lanes] = jnp.where(low, jnp.where(hole, zero, jnp.ones_like(x)), x)
        start += n


def largest_norm(ref):
    pick = lower_lanes((16, LANES)).astype(BF16)
    best = None
    for j in range(ref.shape[1] // LANES):
        x = ref[:, pl.ds(j * LANES, LANES)]
        norms = lax.dot_general(pick, x * x, NT, preferred_element_type=F32)
        best = norms if best is None else jnp.maximum(best, norms)
    return jnp.max(best[:8])


def add_keys(work, ks, vs, safe):
    slots = ks.shape[1] // LANES
    rows_k = ks.shape[0]

    @pl.when(safe)
    def _():
        steps = []
        for first_key, fresh, qs, acc, unused in work:
            for j in range(slots):
                for col in range(0, qs.shape[0], MOST_QUERIES):
                    at = pl.ds(col, min(MOST_QUERIES, qs.shape[0] - col))
                    for row in range(first_key, rows_k, MOST_KEYS):
                        ka = pl.ds(row, min(MOST_KEYS, rows_k - row))
                        steps.append((qs, acc, pl.ds(j * LANES, LANES), at, ka, fresh and row == first_key))

        def scores(step):
            qs, unused, lanes, at, ka, unused = step
            return lax.dot_general(ks[ka, lanes], qs[at, lanes], NT, preferred_element_type=F32)

        ahead = scores(steps[0])
        for i, (qs, acc, lanes, at, ka, zero) in enumerate(steps):
            p = jnp.exp(ahead).astype(BF16)
            if i + 1 < len(steps):
                ahead = scores(steps[i + 1])
            term = lax.dot_general(vs[ka, lanes], p, TN, preferred_element_type=F32)
            acc[lanes, at] = term if zero else acc[lanes, at] + term

    @pl.when(jnp.logical_not(safe))
    def _():
        for first_key, fresh, qs, acc, top in work:
            if fresh:
                acc[...] = jnp.zeros_like(acc)
            add_keys_shifted(first_key, qs, ks, vs, acc, top)


def add_keys_shifted(first_key, qs, ks, vs, acc, top):
    slots = ks.shape[1] // LANES
    rows_k = ks.shape[0]
    cols = qs.shape[0]
    step_q, step_k = 128, 128

    def over_queries(i, unused):
        at = pl.ds(pl.multiple_of(i * step_q, step_q), step_q)
        for j in range(slots):
            lanes = pl.ds(j * LANES, LANES)

            def over_keys(c, carry):
                high, total = carry
                ka = pl.ds(pl.multiple_of(c * step_k, step_k), step_k)
                v = vs[ka, lanes]
                s = lax.dot_general(ks[ka, lanes], qs[at, lanes], NT, preferred_element_type=F32)
                s = jnp.where(v[:, :1].astype(F32) > 0.5, s, LOW)
                best = jnp.max(s, axis=0, keepdims=True)
                best = (best + jnp.abs(best) * (1.0 / 128)).astype(BF16).astype(F32)
                new = jnp.maximum(high, best)
                p = jnp.exp(s - new).astype(BF16)
                total = total * jnp.exp(high - new) + lax.dot_general(v, p, TN, preferred_element_type=F32)
                return new, total

            high, total = lax.fori_loop(first_key // step_k, rows_k // step_k, over_keys, (top[pl.ds(j, 1), at], acc[lanes, at]))
            acc[lanes, at] = total
            top[pl.ds(j, 1), at] = high
        return unused

    lax.fori_loop(0, cols // step_q, over_queries, 0)


def attend_kernel(sets, n_kv, half, first, n_export, *refs):
    given = []
    for n_q, unused in sets:
        count = n_q or 3
        given.append(refs[:count])
        refs = refs[count:]
    kv_refs, refs = refs[:n_kv], refs[n_kv:]
    if not first:
        info_in, refs = refs[0], refs[1:]
    held = []
    for (n_q, unused), mine in zip(sets, given):
        count = 3 if n_q else 2
        held.append(refs[:3] if n_q else (mine[0], *refs[:2]))
        refs = refs[count:]
    info, exports, (ks, vs) = refs[0], refs[1 : 1 + n_export], refs[1 + n_export :]
    length = None if first else info_in[...][0, 0]
    for (n_q, unused), mine, (qs, acc, top) in zip(sets, given, held):
        if n_q:
            spread_queries(mine, half, qs)
            top[...] = jnp.zeros_like(top)
            own = largest_norm(qs)
            length = own if length is None else jnp.maximum(length, own)
    spread_keys(kv_refs, ks, vs)
    safe = length * largest_norm(ks) * 1.05 <= SAFE * SAFE
    info[...] = jnp.full(info.shape, jnp.where(safe, length, LIMIT), F32)
    add_keys([(first_key, n_q > 0, *mine) for (n_q, first_key), mine in zip(sets, held)], ks, vs, safe)
    for i, out in enumerate(exports):
        place = 0
        for qs, acc, top in held:
            cols = qs.shape[0] // (n_export + 1)
            at, to = pl.ds((i + 1) * cols, cols), pl.ds(place, cols)
            for j in range(qs.shape[1] // LANES):
                start = j * (HEAD_DIM + 2 * ONES)
                out[pl.ds(start, HEAD_DIM), to] = acc[pl.ds(j * LANES + HEAD_DIM, HEAD_DIM), at].astype(BF16)
                out[pl.ds(start + HEAD_DIM, ONES), to] = acc[pl.ds(j * LANES, ONES), at].astype(BF16)
                shift = jnp.broadcast_to(top[pl.ds(j, 1), at], (ONES, cols))
                out[pl.ds(start + HEAD_DIM + ONES, ONES), to] = shift.astype(BF16)
            place += cols


def attend(sets, kv_list, half, info, n_export=0):
    width = kv_list[0].shape[1]
    slots = width // LANES
    first = info is None
    rows_k = sum(k.shape[0] for k in kv_list)
    args, meta, out_shape, aliases, work, own_cols = [], [], [], {}, 0, 0
    for items, first_key in sets:
        new = items[0].dtype == items[1].dtype
        cols = sum(q.shape[0] for q in items) * 2 if new else items[0].shape[0]
        meta.append((len(items) if new else 0, first_key))
        if new:
            out_shape.append(jax.ShapeDtypeStruct((cols, width), BF16))
        else:
            aliases[len(args) + 1], aliases[len(args) + 2] = len(out_shape), len(out_shape) + 1
        out_shape += [jax.ShapeDtypeStruct((width, cols), F32), jax.ShapeDtypeStruct((8, cols), F32)]
        args += items
        work += cols * (rows_k - first_key)
        own_cols += cols // (n_export + 1)
    args += kv_list
    if not first:
        args.append(info)
    out_shape.append(jax.ShapeDtypeStruct((8, LANES), F32))
    out_shape += [jax.ShapeDtypeStruct((slots * (HEAD_DIM + 2 * ONES), own_cols), BF16)] * n_export
    out = list(
        pl.pallas_call(
            functools.partial(attend_kernel, meta, len(kv_list), half, first, n_export),
            out_shape=out_shape,
            in_specs=[VMEM] * len(args),
            out_specs=[VMEM] * len(out_shape),
            scratch_shapes=[pltpu.VMEM((rows_k, width), BF16)] * 2,
            input_output_aliases=aliases,
            compiler_params=params(),
            cost_estimate=pl.CostEstimate(
                flops=16 * work * width, bytes_accessed=4 * rows_k * width, transcendentals=work * slots
            ),
        )(*args)
    )
    states = []
    for (items, unused), (n_q, unused) in zip(sets, meta):
        states.append([out.pop(0) if n_q else items[0], out.pop(0), out.pop(0)])
    return states, out[0], out[1:]


def finish_kernel(n_sets, n_import, wanted, *refs):
    held = [refs[2 * i : 2 * i + 2] for i in range(n_sets)]
    imports, outs = refs[2 * n_sets : 2 * n_sets + n_import], list(refs[2 * n_sets + n_import :])
    piece = outs[0].shape[1]
    step = HEAD_DIM + 2 * ONES
    place = 0
    for acc, top in held:
        cols = acc.shape[1] // (n_import + 1)
        for col in range(0, cols, piece):
            if (place + col) // piece not in wanted:
                continue
            out = outs.pop(0)
            at, there = pl.ds(col, piece), pl.ds(place + col, piece)
            for j in range(acc.shape[0] // LANES):
                total = acc[pl.ds(j * LANES + HEAD_DIM, HEAD_DIM), at]
                count = acc[pl.ds(j * LANES, 1), at]
                high = top[pl.ds(j, 1), at]
                for ref in imports:
                    values = ref[pl.ds(j * step, HEAD_DIM), there].astype(F32)
                    sums = ref[pl.ds(j * step + HEAD_DIM, ONES), there].astype(F32)[:1]
                    shift = ref[pl.ds(j * step + HEAD_DIM + ONES, ONES), there].astype(F32)[:1]
                    new = jnp.maximum(high, shift)
                    mine, theirs = jnp.exp(high - new), jnp.exp(shift - new)
                    total = total * mine + values * theirs
                    count = count * mine + sums * theirs
                    high = new
                share = 1.0 / (count + jnp.exp(-high))
                out[pl.ds(j * HEAD_DIM, HEAD_DIM), :] = (total * share).astype(BF16)
        place += cols


def finish(states, imports, n_pieces, wanted):
    sums = [x for state in states for x in state[1:]]
    slots = sums[0].shape[0] // LANES
    piece = sum(state[1].shape[1] for state in states) // (len(imports) + 1) // n_pieces
    return pl.pallas_call(
        functools.partial(finish_kernel, len(states), len(imports), wanted),
        out_shape=[jax.ShapeDtypeStruct((slots * HEAD_DIM, piece), BF16)] * len(wanted),
        in_specs=[VMEM] * (len(sums) + len(imports)),
        out_specs=[VMEM] * len(wanted),
        compiler_params=params(),
    )(*sums, *imports)


def project_kernel(rest, *refs):
    parts, w_ref, out = refs[:GROUPS], refs[GROUPS], refs[GROUPS + 1]
    mine = lax.axis_index("inner") // rest
    rows = parts[0].shape[0]
    total = None
    for s, part in enumerate(parts):
        g = jnp.bitwise_xor(mine, s)
        w = w_ref[pl.ds(pl.multiple_of(g * rows, 16), rows), :]
        term = lax.dot_general(part[...], w, TN, preferred_element_type=F32)
        total = term if total is None else total + term
    out[...] = total.astype(BF16)


def project(parts, w, rest):
    return pl.pallas_call(
        functools.partial(project_kernel, rest),
        out_shape=jax.ShapeDtypeStruct((parts[0].shape[1], w.shape[1]), BF16),
        in_specs=[VMEM] * (GROUPS + 1),
        out_specs=VMEM,
        compiler_params=params(),
    )(*parts, w)


def on_device(n_blk, n_inner, q, k, v, valid, w):
    rest = n_inner // GROUPS
    half = q.shape[0] // 2

    def over_groups(x, s):
        return lax.ppermute(x, "inner", [(i, (i // rest ^ s) * rest + i % rest) for i in range(n_inner)])

    def over_rest(x, t):
        return lax.ppermute(x, "inner", [(i, i // rest * rest + (i + t) % rest) for i in range(n_inner)])

    def over_blk(x, t):
        return lax.ppermute(x, "blk", [(i, (i + t) % n_blk) for i in range(n_blk)])

    def along(first, second):
        return [
            (b * n_inner + i, (b ^ (second if i % 2 else first)) * n_inner + i)
            for b in range(n_blk)
            for i in range(n_inner)
        ]

    def near(chunk):
        return [lax.ppermute(chunk, ("blk", "inner"), along(d, d)) for d in (1, 2)]

    def passed(blocks):
        return jnp.where(lax.axis_index("inner") % 2 == 0, *blocks)

    def far(block):
        return lax.ppermute(block, ("blk", "inner"), along(2, 1))

    def after(x, *done):
        return lax.optimization_barrier((x, *done))[0]

    def diagonal(chunk):
        return lax.ppermute(chunk, ("blk", "inner"), along(3, 3))

    pieces = list(pack(q, k, v, valid, rest))
    rows = q.shape[0]

    def gathered_queries(pieces):
        own = jnp.concatenate([x[rows:] for x in pieces], axis=0)
        return [own] + [over_rest(own, t) for t in range(1, rest)]

    if n_blk == 4 and rest == 2:
        own0 = pieces[0][:rows]
        near0 = near(own0)
        pieces[1], pieces[2] = over_groups(pieces[1], 1), over_groups(pieces[2], 2)
        pieces[3] = over_groups(after(pieces[3], pieces[1], pieces[2]), 3)
        pieces[1], pieces[2] = after((pieces[1], pieces[2]), *near0)
        q_early = gathered_queries(pieces[:3])
        near0 = after(tuple(near0), *q_early)
        own1 = after(jnp.concatenate([x[:rows] for x in pieces[1:3]], axis=0), *q_early)
        near1 = near(own1)
        far0 = far(passed(near0))
        early = [own0, own1, *near0, far0]
        (early_set,), info, unused = attend([(q_early, 0)], early, half, None)
        near1 = after(tuple(near1), early_set[1])
        pass1 = passed(near1)
        far1 = far(pass1)
        last = after(pieces[3], early_set[1])
        own2 = last[:rows]
        block2 = [*near(own2), diagonal(own2)]
        q_late = gathered_queries([last])
        met = sum(x.shape[0] for x in early)
        states, info, unused = attend([(early_set, met), (q_late, 0)], [*early, *near1, own2], half, info)
        states, info, exports = attend([(x, 0) for x in states], [far1, *block2], half, info, rest - 1)
    else:
        pieces = [pieces[0]] + [over_groups(pieces[s], s) for s in range(1, GROUPS)]
        chunk = jnp.concatenate([x[:rows] for x in pieces], axis=0)
        blocks = [chunk] + [over_blk(chunk, t) for t in range(1, n_blk)]
        states, info, exports = attend([(gathered_queries(pieces), 0)], blocks, half, None, rest - 1)
    imports = [over_rest(x, rest - 1 - t) for t, x in enumerate(exports)]
    there = [over_groups(x, s) for s, x in zip((2, 3), finish(states, imports, GROUPS, (2, 3)))]
    own, beside = finish(states, imports, GROUPS, (0, 1))
    parts = [own, over_groups(beside, 1), *there]
    return project(parts, w, rest)


def solution(mesh):
    rows = P(("blk", "inner"), None)
    return jax.shard_map(
        functools.partial(on_device, mesh.shape["blk"], mesh.shape["inner"]),
        mesh=mesh,
        in_specs=(rows, rows, rows, P(("blk", "inner")), P()),
        out_specs=rows,
        check_vma=False,
    )
```

time: 171 us -> 169 us (0.988)
  waiting for transfers between devices: 17.1 us -> 11.7 us
  starting transfers between devices: 19.9 us -> 22.2 us
    ppermute x6, waiting for transfers between devices: 15.5 us -> 4.26 us  [over_groups(): lax.ppermute(x, 'inner', [(i, (i // rest ^ s) * rest + i % rest) for i in...]
    ppermute x6, waiting for transfers between devices: 0.02 us -> 3.13 us  [near(): return [lax.ppermute(chunk, ('blk', 'inner'), along(d, d)) for d in (1, 2)]]
    ppermute x6, starting transfers between devices: 8.86 us -> 11.8 us  [over_groups(): lax.ppermute(x, 'inner', [(i, (i // rest ^ s) * rest + i % rest) for i in...]
    pallas_call x3 -> x5, Pallas kernels: 131 us -> 132 us  [the longest x3 132 us: attend(): pl.pallas_call(functools.partial(attend_kernel, meta, len(kv_list), half,...]
  transfers between devices with their start and end apart: 17 -> 18, of which waited for: 6 -> 8; matrix products, arithmetic and copies ran while one was open for 0% -> 0% of each run, Pallas kernels for 52% -> 54%
where the time goes in v3:
time: 169 us
  Pallas kernels  134 us (79%)
  starting transfers between devices  22.2 us (13%)
  waiting for transfers between devices  11.7 us (7%)
    pallas_call x3, Pallas kernels, attend(): pl.pallas_call(functools.partial(attend_kernel, meta, len(kv_list), half,...  132 us
    ppermute x6, starting transfers between devices, over_groups(): lax.ppermute(x, 'inner', [(i, (i // rest ^ s) * rest + i % rest) for i in...  11.8 us
    ppermute x6, starting transfers between devices, near(): return [lax.ppermute(chunk, ('blk', 'inner'), along(d, d)) for d in (1, 2)]  8.61 us
    ppermute x6, waiting for transfers between devices, over_groups(): lax.ppermute(x, 'inner', [(i, (i // rest ^ s) * rest + i % rest) for i in...  4.26 us
  transfers between devices with their start and end apart: 18, of which 8 were waited for; matrix products, arithmetic and copies ran while one was open for 0% of the time, Pallas kernels for 54%

profile of v3, /device:TPU:0, one launch (start us, length us, event | category | flops | bytes accessed | tf_op | source)
XLA Modules:
  0.0 168.6 jit_solution(842696060454902795)
XLA Ops:
  0.0 1.6 shard_map.55
  1.6 3.1 %collective-permute-start = (bf16[192,384]{1,0:T(8,128)(2,1)S(1)}, bf16[192,384]{1,0:T(8,128)(2,1)S(1)}, u32[]{:S(2)}, u32[]{:S(2)}) collective-permute-start(bf16[192,384]{1,0:T(8,128)(2,1)S(1)} %get-tuple-element.38), channel_id=1, source_target_pairs={{0,2},{1,3},{2,0},{3,1},{4,6},{5,7},{6,4},{7,5},{8,10},{9,11},{10,... | collective-permute-start | bytes 442376 | tf_op jit(solution)/shard_map/ppermute | solution.py:373
  4.7 2.6 %collective-permute-start.1 = (bf16[192,384]{1,0:T(8,128)(2,1)S(1)}, bf16[192,384]{1,0:T(8,128)(2,1)S(1)}, u32[]{:S(2)}, u32[]{:S(2)}) collective-permute-start(bf16[192,384]{1,0:T(8,128)(2,1)S(1)} %get-tuple-element.39), channel_id=1, source_target_pairs={{0,4},{1,5},{2,6},{3,7},{4,0},{5,1},{6,2},{7,3},{8,12},{9,13},{10,... | collective-permute-start | bytes 442376 | tf_op jit(solution)/shard_map/ppermute | solution.py:373
  7.3 1.6 collective-permute-start.3
  8.9 1.5 collective-permute-start.2
  10.4 1.6 collective-permute-done.3.refs_5_.refs_8_
  12.0 1.5 collective-permute-done.2.refs_4_.refs_7_
  13.5 0.6 collective-permute-done.1
  14.3 2.5 %collective-permute-start.6 = (bf16[192,384]{1,0:T(8,128)(2,1)S(1)}, bf16[192,384]{1,0:T(8,128)(2,1)S(1)}, u32[]{:S(2)}, u32[]{:S(2)}) collective-permute-start(bf16[192,384]{1,0:T(8,128)(2,1)S(1)} %get-tuple-element.49), channel_id=1, source_target_pairs={{0,6},{1,7},{2,4},{3,5},{4,2},{5,3},{6,0},{7,1},{8,14},{9,15},{10,... | collective-permute-start | bytes 442376 | tf_op jit(solution)/shard_map/ppermute | solution.py:373
  16.8 1.6 collective-permute-start.5
  18.4 0.6 collective-permute-start.9
  19.0 1.5 collective-permute-start.8
  20.5 1.6 collective-permute-done.5.refs_6_.refs_9_
  22.1 37.0 %shard_map.56 = (bf16[768,384]{1,0:T(8,128)(2,1)S(1)}, f32[384,768]{1,0:T(8,128)S(1)}, f32[8,768]{1,0:T(8,128)S(1)}, f32[8,128]{1,0:T(8,128)S(1)}) custom-call(bf16[192,384]{1,0:T(8,128)(2,1)S(1)} %pad_maximum_fusion.1.refs_0_, bf16[192,384]{1,0:T(8,128)(2,1)S(1)} %collective-permute-done.4.refs_1_, bf16[128,384]{1,0:T(8,128)(2,1)S(1)} %slice.25.refs_2_.refs_5_, ...), custom_call_target="tpu_custom_call" | custom-call | flops 3623878656 | bytes 1179648 | tf_op jit(solution)/shard_map/pallas_call | solution.py:282
  59.3 3.4 %collective-permute-start.11 = (bf16[128,384]{1,0:T(8,128)(2,1)S(1)}, bf16[128,384]{1,0:T(8,128)(2,1)S(1)}, u32[]{:S(2)}, u32[]{:S(2)}) collective-permute-start(bf16[128,384]{1,0:T(8,128)(2,1)S(1)} %slice.31.refs_12_), channel_id=1, source_target_pairs={{0,8},{1,9},{2,10},{3,11},{4,12},{5,13},{6,14},{7,15},{8,0},{9,1},... | collective-permute-start | bytes 294920 | tf_op jit(solution)/shard_map/ppermute | solution.py:389
  62.8 1.1 collective-permute-done.7.refs_4_
  63.9 53.2 %shard_map.57 = (f32[384,768]{1,0:T(8,128)S(1)}, f32[8,768]{1,0:T(8,128)S(1)}, bf16[256,384]{1,0:T(8,128)(2,1)S(1)}, f32[384,256]{1,0:T(8,128)S(1)}, f32[8,256]{1,0:T(8,128)S(1)}, /*index=5*/f32[8,128]{1,0:T(8,128)S(1)}) custom-call(bf16[768,384]{1,0:T(8,128)(2,1)S(1)} %get-tuple-element.45.refs_0_, ...), custom_call_target="tpu_custom_call", output_to_operand_aliasing={{0}: (1, {}), {1}: (2, {})} | custom-call | flops 5234491392 | bytes 2162688 | tf_op jit(solution)/shard_map/pallas_call | solution.py:282
  117.2 41.3 %shard_map.58 = (f32[384,768]{1,0:T(8,128)S(1)}, f32[8,768]{1,0:T(8,128)S(1)}, f32[384,256]{1,0:T(8,128)S(1)}, f32[8,256]{1,0:T(8,128)S(1)}, f32[8,128]{1,0:T(8,128)}, /*index=5*/bf16[288,512]{1,0:T(8,128)(2,1)S(1)}) custom-call(bf16[768,384]{1,0:T(8,128)(2,1)S(1)} %get-tuple-element.45.refs_, ...), custom_call_target="tpu_custom_call", output_to_operand_aliasing={{0}: (1, {}), {1}: (2, {}), {2}: (4, {}), {3}: (5, {})} | custom-call | flops 4026531840 | bytes 983040 | tf_op jit(solution)/shard_map/pallas_call | solution.py:282
  158.5 1.6 collective-permute-done.14.refs_4_
  160.3 2.0 %collective-permute-start.17 = (bf16[192,128]{1,0:T(8,128)(2,1)S(1)}, bf16[192,128]{1,0:T(8,128)(2,1)S(1)}, u32[]{:S(2)}, u32[]{:S(2)}) collective-permute-start(bf16[192,128]{1,0:T(8,128)(2,1)S(1)} %get-tuple-element.68), channel_id=1, source_target_pairs={{0,6},{1,7},{2,4},{3,5},{4,2},{5,3},{6,0},{7,1},{8,14},{9,15},{10,... | collective-permute-start | bytes 147464 | tf_op jit(solution)/shard_map/ppermute | solution.py:373
  162.3 1.5 collective-permute-start.15
  163.9 2.9 %collective-permute-done.16.refs_2_ = bf16[192,128]{1,0:T(8,128)(2,1)S(1)} collective-permute-done((bf16[192,128]{1,0:T(8,128)(2,1)S(1)}, bf16[192,128]{1,0:T(8,128)(2,1)S(1)}, u32[]{:S(2)}, u32[]{:S(2)}) %collective-permute-start.16) | collective-permute-done | bytes 49184 | tf_op jit(solution)/shard_map/ppermute | solution.py:373
  166.8 0.7 collective-permute-done.15.refs_1_
  167.5 1.1 shard_map.61
  (33 shorter events, 0.7 us)
Async XLA Ops:
  1.6 11.9 %collective-permute-start = (bf16[192,384]{1,0:T(8,128)(2,1)S(1)}, bf16[192,384]{1,0:T(8,128)(2,1)S(1)}, u32[]{:S(2)}, u32[]{:S(2)}) collective-permute-start(bf16[192,384]{1,0:T(8,128)(2,1)S(1)} %get-tuple-element.38), channel_id=1, source_target_pairs={{0,2},{1,3},{2,0},{3,1},{4,6},{5,7},{6,4},{7,5},{8,10},{9,11},{10,... | collective-permute-start | bytes 442376 | tf_op jit(solution)/shard_map/ppermute | solution.py:373
  4.7 9.4 %collective-permute-start.1 = (bf16[192,384]{1,0:T(8,128)(2,1)S(1)}, bf16[192,384]{1,0:T(8,128)(2,1)S(1)}, u32[]{:S(2)}, u32[]{:S(2)}) collective-permute-start(bf16[192,384]{1,0:T(8,128)(2,1)S(1)} %get-tuple-element.39), channel_id=1, source_target_pairs={{0,4},{1,5},{2,6},{3,7},{4,0},{5,1},{6,2},{7,3},{8,12},{9,13},{10,... | collective-permute-start | bytes 442376 | tf_op jit(solution)/shard_map/ppermute | solution.py:373
  7.3 4.7 %collective-permute-start.3 = (bf16[128,384]{1,0:T(8,128)(2,1)S(1)}, bf16[128,384]{1,0:T(8,128)(2,1)S(1)}, u32[]{:S(2)}, u32[]{:S(2)}) collective-permute-start(bf16[128,384]{1,0:T(8,128)(2,1)S(1)} %slice.25.refs_2_.refs_5_), channel_id=1, source_target_pairs={{0,16},{1,17},{2,18},{3,19},{4,20},{5,21},{6,22},{7,23},{8,24},{9,... | collective-permute-start | bytes 294920 | tf_op jit(solution)/shard_map/ppermute | solution.py:389
  8.9 4.6 %collective-permute-start.2 = (bf16[128,384]{1,0:T(8,128)(2,1)S(1)}, bf16[128,384]{1,0:T(8,128)(2,1)S(1)}, u32[]{:S(2)}, u32[]{:S(2)}) collective-permute-start(bf16[128,384]{1,0:T(8,128)(2,1)S(1)} %slice.25.refs_2_.refs_5_), channel_id=1, source_target_pairs={{0,8},{1,9},{2,10},{3,11},{4,12},{5,13},{6,14},{7,15},{8,0},{9,1},... | collective-permute-start | bytes 294920 | tf_op jit(solution)/shard_map/ppermute | solution.py:389
  14.2 2.7 %collective-permute-start.4 = (bf16[192,384]{1,0:T(8,128)(2,1)S(1)}, bf16[192,384]{1,0:T(8,128)(2,1)S(1)}, u32[]{:S(2)}, u32[]{:S(2)}) collective-permute-start(bf16[192,384]{1,0:T(8,128)(2,1)S(1)} %pad_maximum_fusion.1.refs_0_), channel_id=1, source_target_pairs={{0,1},{1,0},{2,3},{3,2},{4,5},{5,4},{6,7},{7,6},{8,9},{9,8},{10,11... | collective-permute-start | bytes 442376 | tf_op jit(solution)/shard_map/ppermute | solution.py:376
  14.3 44.8 %collective-permute-start.6 = (bf16[192,384]{1,0:T(8,128)(2,1)S(1)}, bf16[192,384]{1,0:T(8,128)(2,1)S(1)}, u32[]{:S(2)}, u32[]{:S(2)}) collective-permute-start(bf16[192,384]{1,0:T(8,128)(2,1)S(1)} %get-tuple-element.49), channel_id=1, source_target_pairs={{0,6},{1,7},{2,4},{3,5},{4,2},{5,3},{6,0},{7,1},{8,14},{9,15},{10,... | collective-permute-start | bytes 442376 | tf_op jit(solution)/shard_map/ppermute | solution.py:373
  16.8 5.3 %collective-permute-start.5 = (bf16[128,384]{1,0:T(8,128)(2,1)S(1)}, bf16[128,384]{1,0:T(8,128)(2,1)S(1)}, u32[]{:S(2)}, u32[]{:S(2)}) collective-permute-start(bf16[128,384]{1,0:T(8,128)(2,1)S(1)} %broadcast_select_fusion.1), channel_id=1, source_target_pairs={{0,16},{1,9},{2,18},{3,11},{4,20},{5,13},{6,22},{7,15},{8,24},{9,1... | collective-permute-start | bytes 294920 | tf_op jit(solution)/shard_map/ppermute | solution.py:395
  18.4 44.3 %collective-permute-start.9 = (bf16[256,384]{1,0:T(8,128)(2,1)S(1)}, bf16[256,384]{1,0:T(8,128)(2,1)S(1)}, u32[]{:S(2)}, u32[]{:S(2)}) collective-permute-start(bf16[256,384]{1,0:T(8,128)(2,1)S(1)} %pad_maximum_fusion.refs_3_.refs_6_), channel_id=1, source_target_pairs={{0,16},{1,17},{2,18},{3,19},{4,20},{5,21},{6,22},{7,23},{8,24},{9,... | collective-permute-start | bytes 589832 | tf_op jit(solution)/shard_map/ppermute | solution.py:389
  19.0 43.7 %collective-permute-start.8 = (bf16[256,384]{1,0:T(8,128)(2,1)S(1)}, bf16[256,384]{1,0:T(8,128)(2,1)S(1)}, u32[]{:S(2)}, u32[]{:S(2)}) collective-permute-start(bf16[256,384]{1,0:T(8,128)(2,1)S(1)} %pad_maximum_fusion.refs_3_.refs_6_), channel_id=1, source_target_pairs={{0,8},{1,9},{2,10},{3,11},{4,12},{5,13},{6,14},{7,15},{8,0},{9,1},... | collective-permute-start | bytes 589832 | tf_op jit(solution)/shard_map/ppermute | solution.py:389
  59.1 58.0 %collective-permute-start.13 = (bf16[128,384]{1,0:T(8,128)(2,1)S(1)}, bf16[128,384]{1,0:T(8,128)(2,1)S(1)}, u32[]{:S(2)}, u32[]{:S(2)}) collective-permute-start(bf16[128,384]{1,0:T(8,128)(2,1)S(1)} %slice.31.refs_12_), channel_id=1, source_target_pairs={{0,24},{1,25},{2,26},{3,27},{4,28},{5,29},{6,30},{7,31},{8,16},{9,... | collective-permute-start | bytes 294920 | tf_op jit(solution)/shard_map/ppermute | solution.py:401
  59.2 57.9 %collective-permute-start.12 = (bf16[128,384]{1,0:T(8,128)(2,1)S(1)}, bf16[128,384]{1,0:T(8,128)(2,1)S(1)}, u32[]{:S(2)}, u32[]{:S(2)}) collective-permute-start(bf16[128,384]{1,0:T(8,128)(2,1)S(1)} %slice.31.refs_12_), channel_id=1, source_target_pairs={{0,16},{1,17},{2,18},{3,19},{4,20},{5,21},{6,22},{7,23},{8,24},{9,... | collective-permute-start | bytes 294920 | tf_op jit(solution)/shard_map/ppermute | solution.py:389
  59.3 57.9 %collective-permute-start.11 = (bf16[128,384]{1,0:T(8,128)(2,1)S(1)}, bf16[128,384]{1,0:T(8,128)(2,1)S(1)}, u32[]{:S(2)}, u32[]{:S(2)}) collective-permute-start(bf16[128,384]{1,0:T(8,128)(2,1)S(1)} %slice.31.refs_12_), channel_id=1, source_target_pairs={{0,8},{1,9},{2,10},{3,11},{4,12},{5,13},{6,14},{7,15},{8,0},{9,1},... | collective-permute-start | bytes 294920 | tf_op jit(solution)/shard_map/ppermute | solution.py:389
  62.7 1.2 collective-permute-start.7
  62.7 54.4 %collective-permute-start.10 = (bf16[256,384]{1,0:T(8,128)(2,1)S(1)}, bf16[256,384]{1,0:T(8,128)(2,1)S(1)}, u32[]{:S(2)}, u32[]{:S(2)}) collective-permute-start(bf16[256,384]{1,0:T(8,128)(2,1)S(1)} %broadcast_select_fusion), channel_id=1, source_target_pairs={{0,16},{1,9},{2,18},{3,11},{4,20},{5,13},{6,22},{7,15},{8,24},{9,1... | collective-permute-start | bytes 589832 | tf_op jit(solution)/shard_map/ppermute | solution.py:395
  158.5 1.6 collective-permute-start.14
  160.2 7.3 %copy-start = (bf16[768,768]{1,0:T(8,128)(2,1)S(1)}, bf16[768,768]{1,0:T(8,128)(2,1)}, u32[]{:S(2)}) copy-start(bf16[768,768]{1,0:T(8,128)(2,1)} %refs_4_.1) | copy-start | bytes 3538948
  160.2 6.6 %collective-permute-start.16 = (bf16[192,128]{1,0:T(8,128)(2,1)S(1)}, bf16[192,128]{1,0:T(8,128)(2,1)S(1)}, u32[]{:S(2)}, u32[]{:S(2)}) collective-permute-start(bf16[192,128]{1,0:T(8,128)(2,1)S(1)} %get-tuple-element.67), channel_id=1, source_target_pairs={{0,4},{1,5},{2,6},{3,7},{4,0},{5,1},{6,2},{7,3},{8,12},{9,13},{10,... | collective-permute-start | bytes 147464 | tf_op jit(solution)/shard_map/ppermute | solution.py:373
  160.3 6.5 %collective-permute-start.17 = (bf16[192,128]{1,0:T(8,128)(2,1)S(1)}, bf16[192,128]{1,0:T(8,128)(2,1)S(1)}, u32[]{:S(2)}, u32[]{:S(2)}) collective-permute-start(bf16[192,128]{1,0:T(8,128)(2,1)S(1)} %get-tuple-element.68), channel_id=1, source_target_pairs={{0,6},{1,7},{2,4},{3,5},{4,2},{5,3},{6,0},{7,1},{8,14},{9,15},{10,... | collective-permute-start | bytes 147464 | tf_op jit(solution)/shard_map/ppermute | solution.py:373
  162.3 5.2 %collective-permute-start.15 = (bf16[192,128]{1,0:T(8,128)(2,1)S(1)}, bf16[192,128]{1,0:T(8,128)(2,1)S(1)}, u32[]{:S(2)}, u32[]{:S(2)}) collective-permute-start(bf16[192,128]{1,0:T(8,128)(2,1)S(1)} %get-tuple-element.66), channel_id=1, source_target_pairs={{0,2},{1,3},{2,0},{3,1},{4,6},{5,7},{6,4},{7,5},{8,10},{9,11},{10,... | collective-permute-start | bytes 147464 | tf_op jit(solution)/shard_map/ppermute | solution.py:373

commit v4 on v3

--- a/solution.py
+++ b/solution.py
@@ -287,9 +287,7 @@
             scratch_shapes=[pltpu.VMEM((rows_k, width), BF16)] * 2,
             input_output_aliases=aliases,
             compiler_params=params(),
-            cost_estimate=pl.CostEstimate(
-                flops=16 * work * width, bytes_accessed=4 * rows_k * width, transcendentals=work * slots
-            ),
+            cost_estimate=pl.CostEstimate(flops=1, bytes_accessed=1, transcendentals=0),
         )(*args)
     )
     states = []
@@ -378,27 +376,11 @@
     def over_blk(x, t):
         return lax.ppermute(x, "blk", [(i, (i + t) % n_blk) for i in range(n_blk)])
 
-    def along(first, second):
-        return [
-            (b * n_inner + i, (b ^ (second if i % 2 else first)) * n_inner + i)
-            for b in range(n_blk)
-            for i in range(n_inner)
-        ]
-
-    def near(chunk):
-        return [lax.ppermute(chunk, ("blk", "inner"), along(d, d)) for d in (1, 2)]
-
-    def passed(blocks):
-        return jnp.where(lax.axis_index("inner") % 2 == 0, *blocks)
-
-    def far(block):
-        return lax.ppermute(block, ("blk", "inner"), along(2, 1))
+    def plane(chunk, order=(1, 2, 3)):
+        return [lax.ppermute(chunk, "blk", [(b, b ^ d) for b in range(n_blk)]) for d in order]
 
     def after(x, *done):
         return lax.optimization_barrier((x, *done))[0]
-
-    def diagonal(chunk):
-        return lax.ppermute(chunk, ("blk", "inner"), along(3, 3))
 
     pieces = list(pack(q, k, v, valid, rest))
     rows = q.shape[0]
@@ -409,27 +391,24 @@
 
     if n_blk == 4 and rest == 2:
         own0 = pieces[0][:rows]
-        near0 = near(own0)
+        near0 = plane(own0, (3, 2, 1))
         pieces[1], pieces[2] = over_groups(pieces[1], 1), over_groups(pieces[2], 2)
         pieces[3] = over_groups(after(pieces[3], pieces[1], pieces[2]), 3)
         pieces[1], pieces[2] = after((pieces[1], pieces[2]), *near0)
         q_early = gathered_queries(pieces[:3])
-        near0 = after(tuple(near0), *q_early)
         own1 = after(jnp.concatenate([x[:rows] for x in pieces[1:3]], axis=0), *q_early)
-        near1 = near(own1)
-        far0 = far(passed(near0))
-        early = [own0, own1, *near0, far0]
+        near1 = plane(own1, (1, 2, 3))
+        early = [own0, own1, *near0]
         (early_set,), info, unused = attend([(q_early, 0)], early, half, None)
-        near1 = after(tuple(near1), early_set[1])
-        pass1 = passed(near1)
-        far1 = far(pass1)
         last = after(pieces[3], early_set[1])
         own2 = last[:rows]
-        block2 = [*near(own2), diagonal(own2)]
+        near2 = plane(own2, (3, 2, 1))
         q_late = gathered_queries([last])
         met = sum(x.shape[0] for x in early)
-        states, info, unused = attend([(early_set, met), (q_late, 0)], [*early, *near1, own2], half, info)
-        states, info, exports = attend([(x, 0) for x in states], [far1, *block2], half, info, rest - 1)
+        states, info, unused = attend([(early_set, met), (q_late, 0)], [*early, own2], half, info)
+        near1 = after(tuple(near1), states[0][1])
+        states, info, unused = attend([(x, 0) for x in states], list(near1), half, info)
+        states, info, exports = attend([(x, 0) for x in states], near2, half, info, rest - 1)
     else:
         pieces = [pieces[0]] + [over_groups(pieces[s], s) for s in range(1, GROUPS)]
         chunk = jnp.concatenate([x[:rows] for x in pieces], axis=0)

time: 169 us -> 165 us (0.976)
    pallas_call x3 -> x4, Pallas kernels: 132 us -> 130 us  [attend(): pl.pallas_call(functools.partial(attend_kernel, meta, len(kv_list), half,...]
  transfers between devices with their start and end apart: 18 -> 18, of which waited for: 8 -> 7; matrix products, arithmetic and copies ran while one was open for 0% -> 0% of each run, Pallas kernels for 54% -> 64%
where the time goes in v4:
time: 165 us
  Pallas kernels  133 us (81%)
  starting transfers between devices  20.7 us (13%)
  waiting for transfers between devices  10.6 us (6%)
    pallas_call x4, Pallas kernels, attend(): pl.pallas_call(functools.partial(attend_kernel, meta, len(kv_list), half,...  130 us
    ppermute x6, starting transfers between devices, over_groups(): lax.ppermute(x, 'inner', [(i, (i // rest ^ s) * rest + i % rest) for i in...  11 us
    ppermute x9, starting transfers between devices, plane(): lax.ppermute(chunk, 'blk', [(b, b ^ d) for b in range(n_blk)])  9.54 us
    ppermute x9, waiting for transfers between devices, plane(): lax.ppermute(chunk, 'blk', [(b, b ^ d) for b in range(n_blk)])  4.09 us
    ppermute x6, waiting for transfers between devices, over_groups(): lax.ppermute(x, 'inner', [(i, (i // rest ^ s) * rest + i % rest) for i in...  3.79 us
  transfers between devices with their start and end apart: 18, of which 7 were waited for; matrix products, arithmetic and copies ran while one was open for 0% of the time, Pallas kernels for 64%

profile of v4, /device:TPU:0, one launch (start us, length us, event | category | flops | bytes accessed | tf_op | source)
XLA Modules:
  0.0 164.6 jit_solution(5060641290684380713)
XLA Ops:
  0.0 1.6 shard_map.55
  1.6 3.1 %collective-permute-start = (bf16[192,384]{1,0:T(8,128)(2,1)S(1)}, bf16[192,384]{1,0:T(8,128)(2,1)S(1)}, u32[]{:S(2)}, u32[]{:S(2)}) collective-permute-start(bf16[192,384]{1,0:T(8,128)(2,1)S(1)} %get-tuple-element.42), channel_id=1, source_target_pairs={{0,2},{1,3},{2,0},{3,1},{4,6},{5,7},{6,4},{7,5},{8,10},{9,11},{10,... | collective-permute-start | bytes 442376 | tf_op jit(solution)/shard_map/ppermute | solution.py:371
  4.7 2.6 %collective-permute-start.1 = (bf16[192,384]{1,0:T(8,128)(2,1)S(1)}, bf16[192,384]{1,0:T(8,128)(2,1)S(1)}, u32[]{:S(2)}, u32[]{:S(2)}) collective-permute-start(bf16[192,384]{1,0:T(8,128)(2,1)S(1)} %get-tuple-element.43), channel_id=1, source_target_pairs={{0,4},{1,5},{2,6},{3,7},{4,0},{5,1},{6,2},{7,3},{8,12},{9,13},{10,... | collective-permute-start | bytes 442376 | tf_op jit(solution)/shard_map/ppermute | solution.py:371
  7.3 2.5 %collective-permute-start.2 = (bf16[128,384]{1,0:T(8,128)(2,1)S(1)}, bf16[128,384]{1,0:T(8,128)(2,1)S(1)}, u32[]{:S(2)}, u32[]{:S(2)}) collective-permute-start(bf16[128,384]{1,0:T(8,128)(2,1)S(1)} %slice.25.refs_2_.refs_5_), channel_id=1, source_target_pairs={{0,24},{8,16},{16,8},{24,0},{1,25},{9,17},{17,9},{25,1},{2,26},{10... | collective-permute-start | bytes 294920 | tf_op jit(solution)/shard_map/ppermute | solution.py:380
  9.8 0.5 collective-permute-start.3
  10.3 0.5 collective-permute-start.4
  10.9 2.4 %collective-permute-done.2.refs_4_.refs_7_ = bf16[128,384]{1,0:T(8,128)(2,1)S(1)} collective-permute-done((bf16[128,384]{1,0:T(8,128)(2,1)S(1)}, bf16[128,384]{1,0:T(8,128)(2,1)S(1)}, u32[]{:S(2)}, u32[]{:S(2)}) %collective-permute-start.2) | collective-permute-done | bytes 98336 | tf_op jit(solution)/shard_map/ppermute | solution.py:380
  13.2 1.3 collective-permute-done.3.refs_5_.refs_8_
  15.1 1.7 %collective-permute-start.6 = (bf16[192,384]{1,0:T(8,128)(2,1)S(1)}, bf16[192,384]{1,0:T(8,128)(2,1)S(1)}, u32[]{:S(2)}, u32[]{:S(2)}) collective-permute-start(bf16[192,384]{1,0:T(8,128)(2,1)S(1)} %get-tuple-element.51), channel_id=1, source_target_pairs={{0,6},{1,7},{2,4},{3,5},{4,2},{5,3},{6,0},{7,1},{8,14},{9,15},{10,... | collective-permute-start | bytes 442376 | tf_op jit(solution)/shard_map/ppermute | solution.py:371
  16.8 2.5 %collective-permute-start.10 = (bf16[256,384]{1,0:T(8,128)(2,1)S(1)}, bf16[256,384]{1,0:T(8,128)(2,1)S(1)}, u32[]{:S(2)}, u32[]{:S(2)}) collective-permute-start(bf16[256,384]{1,0:T(8,128)(2,1)S(1)} %pad_maximum_fusion.refs_3_.refs_6_), channel_id=1, source_target_pairs={{0,24},{8,16},{16,8},{24,0},{1,25},{9,17},{17,9},{25,1},{2,26},{10... | collective-permute-start | bytes 589832 | tf_op jit(solution)/shard_map/ppermute | solution.py:380
  19.4 0.5 collective-permute-start.8
  19.9 0.5 collective-permute-start.9
  20.4 37.0 %shard_map.56 = (bf16[768,384]{1,0:T(8,128)(2,1)S(1)}, f32[384,768]{1,0:T(8,128)S(1)}, f32[8,768]{1,0:T(8,128)S(1)}, f32[8,128]{1,0:T(8,128)S(1)}) custom-call(bf16[192,384]{1,0:T(8,128)(2,1)S(1)} %pad_maximum_fusion.1.refs_0_, bf16[192,384]{1,0:T(8,128)(2,1)S(1)} %collective-permute-done.5.refs_1_, bf16[128,384]{1,0:T(8,128)(2,1)S(1)} %slice.25.refs_2_.refs_5_, ...), custom_call_target="tpu_custom_call" | custom-call | flops 1 | bytes 1 | tf_op jit(solution)/shard_map/pallas_call | solution.py:282
  57.6 1.1 collective-permute-done.7.refs_4_
  58.7 2.4 %collective-permute-start.13 = (bf16[128,384]{1,0:T(8,128)(2,1)S(1)}, bf16[128,384]{1,0:T(8,128)(2,1)S(1)}, u32[]{:S(2)}, u32[]{:S(2)}) collective-permute-start(bf16[128,384]{1,0:T(8,128)(2,1)S(1)} %slice.31.refs_10_), channel_id=1, source_target_pairs={{0,8},{8,0},{16,24},{24,16},{1,9},{9,1},{17,25},{25,17},{2,10},{10... | collective-permute-start | bytes 294920 | tf_op jit(solution)/shard_map/ppermute | solution.py:380
  61.1 19.3 %shard_map.57 = (f32[384,768]{1,0:T(8,128)S(1)}, f32[8,768]{1,0:T(8,128)S(1)}, bf16[256,384]{1,0:T(8,128)(2,1)S(1)}, f32[384,256]{1,0:T(8,128)S(1)}, f32[8,256]{1,0:T(8,128)S(1)}, /*index=5*/f32[8,128]{1,0:T(8,128)S(1)}) custom-call(bf16[768,384]{1,0:T(8,128)(2,1)S(1)} %get-tuple-element.47.refs_0_, ...), custom_call_target="tpu_custom_call", output_to_operand_aliasing={{0}: (1, {}), {1}: (2, {})} | custom-call | flops 1 | bytes 1 | tf_op jit(solution)/shard_map/pallas_call | solution.py:282
  80.4 48.8 %shard_map.58 = (f32[384,768]{1,0:T(8,128)S(1)}, f32[8,768]{1,0:T(8,128)S(1)}, f32[384,256]{1,0:T(8,128)S(1)}, f32[8,256]{1,0:T(8,128)S(1)}, f32[8,128]{1,0:T(8,128)S(1)}) custom-call(bf16[768,384]{1,0:T(8,128)(2,1)S(1)} %get-tuple-element.47.refs_0_, ...), custom_call_target="tpu_custom_call", output_to_operand_aliasing={{0}: (1, {}), {1}: (2, {}), {2}: (4, {}), {3}: (5, {})} | custom-call | flops 1 | bytes 1 | tf_op jit(solution)/shard_map/pallas_call | solution.py:282
  129.2 25.1 %shard_map.59 = (f32[384,768]{1,0:T(8,128)S(1)}, f32[8,768]{1,0:T(8,128)S(1)}, f32[384,256]{1,0:T(8,128)S(1)}, f32[8,256]{1,0:T(8,128)S(1)}, f32[8,128]{1,0:T(8,128)}, /*index=5*/bf16[288,512]{1,0:T(8,128)(2,1)S(1)}) custom-call(bf16[768,384]{1,0:T(8,128)(2,1)S(1)} %get-tuple-element.47.refs_, ...), custom_call_target="tpu_custom_call", output_to_operand_aliasing={{0}: (1, {}), {1}: (2, {}), {2}: (4, {}), {3}: (5, {})} | custom-call | flops 1 | bytes 1 | tf_op jit(solution)/shard_map/pallas_call | solution.py:282
  154.4 1.6 collective-permute-done.14.refs_4_
  156.4 2.1 %collective-permute-start.17 = (bf16[192,128]{1,0:T(8,128)(2,1)S(1)}, bf16[192,128]{1,0:T(8,128)(2,1)S(1)}, u32[]{:S(2)}, u32[]{:S(2)}) collective-permute-start(bf16[192,128]{1,0:T(8,128)(2,1)S(1)} %get-tuple-element.76), channel_id=1, source_target_pairs={{0,6},{1,7},{2,4},{3,5},{4,2},{5,3},{6,0},{7,1},{8,14},{9,15},{10,... | collective-permute-start | bytes 147464 | tf_op jit(solution)/shard_map/ppermute | solution.py:371
  158.5 1.2 collective-permute-start.15
  159.7 2.9 %collective-permute-done.16.refs_2_ = bf16[192,128]{1,0:T(8,128)(2,1)S(1)} collective-permute-done((bf16[192,128]{1,0:T(8,128)(2,1)S(1)}, bf16[192,128]{1,0:T(8,128)(2,1)S(1)}, u32[]{:S(2)}, u32[]{:S(2)}) %collective-permute-start.16) | collective-permute-done | bytes 49184 | tf_op jit(solution)/shard_map/ppermute | solution.py:371
  162.7 0.8 collective-permute-done.15.refs_1_
  163.5 1.1 shard_map.62
  (32 shorter events, 1.2 us)
Async XLA Ops:
  1.6 13.3 %collective-permute-start = (bf16[192,384]{1,0:T(8,128)(2,1)S(1)}, bf16[192,384]{1,0:T(8,128)(2,1)S(1)}, u32[]{:S(2)}, u32[]{:S(2)}) collective-permute-start(bf16[192,384]{1,0:T(8,128)(2,1)S(1)} %get-tuple-element.42), channel_id=1, source_target_pairs={{0,2},{1,3},{2,0},{3,1},{4,6},{5,7},{6,4},{7,5},{8,10},{9,11},{10,... | collective-permute-start | bytes 442376 | tf_op jit(solution)/shard_map/ppermute | solution.py:371
  4.7 10.2 %collective-permute-start.1 = (bf16[192,384]{1,0:T(8,128)(2,1)S(1)}, bf16[192,384]{1,0:T(8,128)(2,1)S(1)}, u32[]{:S(2)}, u32[]{:S(2)}) collective-permute-start(bf16[192,384]{1,0:T(8,128)(2,1)S(1)} %get-tuple-element.43), channel_id=1, source_target_pairs={{0,4},{1,5},{2,6},{3,7},{4,0},{5,1},{6,2},{7,3},{8,12},{9,13},{10,... | collective-permute-start | bytes 442376 | tf_op jit(solution)/shard_map/ppermute | solution.py:371
  7.3 5.9 %collective-permute-start.2 = (bf16[128,384]{1,0:T(8,128)(2,1)S(1)}, bf16[128,384]{1,0:T(8,128)(2,1)S(1)}, u32[]{:S(2)}, u32[]{:S(2)}) collective-permute-start(bf16[128,384]{1,0:T(8,128)(2,1)S(1)} %slice.25.refs_2_.refs_5_), channel_id=1, source_target_pairs={{0,24},{8,16},{16,8},{24,0},{1,25},{9,17},{17,9},{25,1},{2,26},{10... | collective-permute-start | bytes 294920 | tf_op jit(solution)/shard_map/ppermute | solution.py:380
  9.8 4.7 %collective-permute-start.3 = (bf16[128,384]{1,0:T(8,128)(2,1)S(1)}, bf16[128,384]{1,0:T(8,128)(2,1)S(1)}, u32[]{:S(2)}, u32[]{:S(2)}) collective-permute-start(bf16[128,384]{1,0:T(8,128)(2,1)S(1)} %slice.25.refs_2_.refs_5_), channel_id=1, source_target_pairs={{0,16},{8,24},{16,0},{24,8},{1,17},{9,25},{17,1},{25,9},{2,18},{10... | collective-permute-start | bytes 294920 | tf_op jit(solution)/shard_map/ppermute | solution.py:380
  10.3 4.6 %collective-permute-start.4 = (bf16[128,384]{1,0:T(8,128)(2,1)S(1)}, bf16[128,384]{1,0:T(8,128)(2,1)S(1)}, u32[]{:S(2)}, u32[]{:S(2)}) collective-permute-start(bf16[128,384]{1,0:T(8,128)(2,1)S(1)} %slice.25.refs_2_.refs_5_), channel_id=1, source_target_pairs={{0,8},{8,0},{16,24},{24,16},{1,9},{9,1},{17,25},{25,17},{2,10},{10... | collective-permute-start | bytes 294920 | tf_op jit(solution)/shard_map/ppermute | solution.py:380
  15.0 1.8 %collective-permute-start.5 = (bf16[192,384]{1,0:T(8,128)(2,1)S(1)}, bf16[192,384]{1,0:T(8,128)(2,1)S(1)}, u32[]{:S(2)}, u32[]{:S(2)}) collective-permute-start(bf16[192,384]{1,0:T(8,128)(2,1)S(1)} %pad_maximum_fusion.1.refs_0_), channel_id=1, source_target_pairs={{0,1},{1,0},{2,3},{3,2},{4,5},{5,4},{6,7},{7,6},{8,9},{9,8},{10,11... | collective-permute-start | bytes 442376 | tf_op jit(solution)/shard_map/ppermute | solution.py:374
  15.1 42.3 %collective-permute-start.6 = (bf16[192,384]{1,0:T(8,128)(2,1)S(1)}, bf16[192,384]{1,0:T(8,128)(2,1)S(1)}, u32[]{:S(2)}, u32[]{:S(2)}) collective-permute-start(bf16[192,384]{1,0:T(8,128)(2,1)S(1)} %get-tuple-element.51), channel_id=1, source_target_pairs={{0,6},{1,7},{2,4},{3,5},{4,2},{5,3},{6,0},{7,1},{8,14},{9,15},{10,... | collective-permute-start | bytes 442376 | tf_op jit(solution)/shard_map/ppermute | solution.py:371
  16.8 41.9 %collective-permute-start.10 = (bf16[256,384]{1,0:T(8,128)(2,1)S(1)}, bf16[256,384]{1,0:T(8,128)(2,1)S(1)}, u32[]{:S(2)}, u32[]{:S(2)}) collective-permute-start(bf16[256,384]{1,0:T(8,128)(2,1)S(1)} %pad_maximum_fusion.refs_3_.refs_6_), channel_id=1, source_target_pairs={{0,24},{8,16},{16,8},{24,0},{1,25},{9,17},{17,9},{25,1},{2,26},{10... | collective-permute-start | bytes 589832 | tf_op jit(solution)/shard_map/ppermute | solution.py:380
  19.4 61.0 %collective-permute-start.8 = (bf16[256,384]{1,0:T(8,128)(2,1)S(1)}, bf16[256,384]{1,0:T(8,128)(2,1)S(1)}, u32[]{:S(2)}, u32[]{:S(2)}) collective-permute-start(bf16[256,384]{1,0:T(8,128)(2,1)S(1)} %pad_maximum_fusion.refs_3_.refs_6_), channel_id=1, source_target_pairs={{0,8},{8,0},{16,24},{24,16},{1,9},{9,1},{17,25},{25,17},{2,10},{10... | collective-permute-start | bytes 589832 | tf_op jit(solution)/shard_map/ppermute | solution.py:380
  19.9 60.5 %collective-permute-start.9 = (bf16[256,384]{1,0:T(8,128)(2,1)S(1)}, bf16[256,384]{1,0:T(8,128)(2,1)S(1)}, u32[]{:S(2)}, u32[]{:S(2)}) collective-permute-start(bf16[256,384]{1,0:T(8,128)(2,1)S(1)} %pad_maximum_fusion.refs_3_.refs_6_), channel_id=1, source_target_pairs={{0,16},{8,24},{16,0},{24,8},{1,17},{9,25},{17,1},{25,9},{2,18},{10... | collective-permute-start | bytes 589832 | tf_op jit(solution)/shard_map/ppermute | solution.py:380
  57.4 1.3 collective-permute-start.7
  57.5 71.7 %collective-permute-start.11 = (bf16[128,384]{1,0:T(8,128)(2,1)S(1)}, bf16[128,384]{1,0:T(8,128)(2,1)S(1)}, u32[]{:S(2)}, u32[]{:S(2)}) collective-permute-start(bf16[128,384]{1,0:T(8,128)(2,1)S(1)} %slice.31.refs_10_), channel_id=1, source_target_pairs={{0,24},{8,16},{16,8},{24,0},{1,25},{9,17},{17,9},{25,1},{2,26},{10... | collective-permute-start | bytes 294920 | tf_op jit(solution)/shard_map/ppermute | solution.py:380
  58.7 70.5 %collective-permute-start.12 = (bf16[128,384]{1,0:T(8,128)(2,1)S(1)}, bf16[128,384]{1,0:T(8,128)(2,1)S(1)}, u32[]{:S(2)}, u32[]{:S(2)}) collective-permute-start(bf16[128,384]{1,0:T(8,128)(2,1)S(1)} %slice.31.refs_10_), channel_id=1, source_target_pairs={{0,16},{8,24},{16,0},{24,8},{1,17},{9,25},{17,1},{25,9},{2,18},{10... | collective-permute-start | bytes 294920 | tf_op jit(solution)/shard_map/ppermute | solution.py:380
  58.7 70.5 %collective-permute-start.13 = (bf16[128,384]{1,0:T(8,128)(2,1)S(1)}, bf16[128,384]{1,0:T(8,128)(2,1)S(1)}, u32[]{:S(2)}, u32[]{:S(2)}) collective-permute-start(bf16[128,384]{1,0:T(8,128)(2,1)S(1)} %slice.31.refs_10_), channel_id=1, source_target_pairs={{0,8},{8,0},{16,24},{24,16},{1,9},{9,1},{17,25},{25,17},{2,10},{10... | collective-permute-start | bytes 294920 | tf_op jit(solution)/shard_map/ppermute | solution.py:380
  154.4 1.6 collective-permute-start.14
  156.0 7.5 %copy-start = (bf16[768,768]{1,0:T(8,128)(2,1)S(1)}, bf16[768,768]{1,0:T(8,128)(2,1)}, u32[]{:S(2)}) copy-start(bf16[768,768]{1,0:T(8,128)(2,1)} %refs_4_.1) | copy-start | bytes 3538948
  156.0 6.6 %collective-permute-start.16 = (bf16[192,128]{1,0:T(8,128)(2,1)S(1)}, bf16[192,128]{1,0:T(8,128)(2,1)S(1)}, u32[]{:S(2)}, u32[]{:S(2)}) collective-permute-start(bf16[192,128]{1,0:T(8,128)(2,1)S(1)} %get-tuple-element.75), channel_id=1, source_target_pairs={{0,4},{1,5},{2,6},{3,7},{4,0},{5,1},{6,2},{7,3},{8,12},{9,13},{10,... | collective-permute-start | bytes 147464 | tf_op jit(solution)/shard_map/ppermute | solution.py:371
  156.4 6.3 %collective-permute-start.17 = (bf16[192,128]{1,0:T(8,128)(2,1)S(1)}, bf16[192,128]{1,0:T(8,128)(2,1)S(1)}, u32[]{:S(2)}, u32[]{:S(2)}) collective-permute-start(bf16[192,128]{1,0:T(8,128)(2,1)S(1)} %get-tuple-element.76), channel_id=1, source_target_pairs={{0,6},{1,7},{2,4},{3,5},{4,2},{5,3},{6,0},{7,1},{8,14},{9,15},{10,... | collective-permute-start | bytes 147464 | tf_op jit(solution)/shard_map/ppermute | solution.py:371
  158.5 5.0 %collective-permute-start.15 = (bf16[192,128]{1,0:T(8,128)(2,1)S(1)}, bf16[192,128]{1,0:T(8,128)(2,1)S(1)}, u32[]{:S(2)}, u32[]{:S(2)}) collective-permute-start(bf16[192,128]{1,0:T(8,128)(2,1)S(1)} %get-tuple-element.74), channel_id=1, source_target_pairs={{0,2},{1,3},{2,0},{3,1},{4,6},{5,7},{6,4},{7,5},{8,10},{9,11},{10,... | collective-permute-start | bytes 147464 | tf_op jit(solution)/shard_map/ppermute | solution.py:371

commit v5 on v4

--- a/solution.py
+++ b/solution.py
@@ -151,35 +151,32 @@
 def add_keys(work, ks, vs, safe):
     slots = ks.shape[1] // LANES
     rows_k = ks.shape[0]
-
-    @pl.when(safe)
-    def _():
-        steps = []
-        for first_key, fresh, qs, acc, unused in work:
-            for j in range(slots):
-                for col in range(0, qs.shape[0], MOST_QUERIES):
-                    at = pl.ds(col, min(MOST_QUERIES, qs.shape[0] - col))
-                    for row in range(first_key, rows_k, MOST_KEYS):
-                        ka = pl.ds(row, min(MOST_KEYS, rows_k - row))
-                        steps.append((qs, acc, pl.ds(j * LANES, LANES), at, ka, fresh and row == first_key))
-
-        def scores(step):
-            qs, unused, lanes, at, ka, unused = step
-            return lax.dot_general(ks[ka, lanes], qs[at, lanes], NT, preferred_element_type=F32)
-
-        ahead = scores(steps[0])
-        for i, (qs, acc, lanes, at, ka, zero) in enumerate(steps):
-            p = jnp.exp(ahead).astype(BF16)
-            if i + 1 < len(steps):
-                ahead = scores(steps[i + 1])
-            term = lax.dot_general(vs[ka, lanes], p, TN, preferred_element_type=F32)
-            acc[lanes, at] = term if zero else acc[lanes, at] + term
+    steps = []
+    for first_key, qs, old_acc, old_top, acc, top in work:
+        top[...] = jnp.zeros_like(top) if old_top is None else old_top[...]
+        for j in range(slots):
+            for col in range(0, qs.shape[0], MOST_QUERIES):
+                at = pl.ds(col, min(MOST_QUERIES, qs.shape[0] - col))
+                for row in range(first_key, rows_k, MOST_KEYS):
+                    ka = pl.ds(row, min(MOST_KEYS, rows_k - row))
+                    steps.append((qs, old_acc if row == first_key else acc, acc, pl.ds(j * LANES, LANES), at, ka))
+
+    def scores(step):
+        qs, unused, unused, lanes, at, ka = step
+        return lax.dot_general(ks[ka, lanes], qs[at, lanes], NT, preferred_element_type=F32)
+
+    ahead = scores(steps[0])
+    for i, (qs, base, acc, lanes, at, ka) in enumerate(steps):
+        p = jnp.exp(ahead).astype(BF16)
+        if i + 1 < len(steps):
+            ahead = scores(steps[i + 1])
+        term = lax.dot_general(vs[ka, lanes], p, TN, preferred_element_type=F32)
+        acc[lanes, at] = term if base is None else base[lanes, at] + term
 
     @pl.when(jnp.logical_not(safe))
     def _():
-        for first_key, fresh, qs, acc, top in work:
-            if fresh:
-                acc[...] = jnp.zeros_like(acc)
+        for first_key, qs, old_acc, unused, acc, top in work:
+            acc[...] = jnp.zeros_like(acc) if old_acc is None else old_acc[...]
             add_keys_shifted(first_key, qs, ks, vs, acc, top)
 
 
@@ -234,13 +231,16 @@
     for (n_q, unused), mine, (qs, acc, top) in zip(sets, given, held):
         if n_q:
             spread_queries(mine, half, qs)
-            top[...] = jnp.zeros_like(top)
             own = largest_norm(qs)
             length = own if length is None else jnp.maximum(length, own)
     spread_keys(kv_refs, ks, vs)
     safe = length * largest_norm(ks) * 1.05 <= SAFE * SAFE
     info[...] = jnp.full(info.shape, jnp.where(safe, length, LIMIT), F32)
-    add_keys([(first_key, n_q > 0, *mine) for (n_q, first_key), mine in zip(sets, held)], ks, vs, safe)
+    work = []
+    for (n_q, first_key), mine, (qs, acc, top) in zip(sets, given, held):
+        old_acc, old_top = (None, None) if n_q else mine[1:]
+        work.append((first_key, qs, old_acc, old_top, acc, top))
+    add_keys(work, ks, vs, safe)
     for i, out in enumerate(exports):
         place = 0
         for qs, acc, top in held:
@@ -260,18 +260,15 @@
     slots = width // LANES
     first = info is None
     rows_k = sum(k.shape[0] for k in kv_list)
-    args, meta, out_shape, aliases, work, own_cols = [], [], [], {}, 0, 0
+    args, meta, out_shape, own_cols = [], [], [], 0
     for items, first_key in sets:
         new = items[0].dtype == items[1].dtype
         cols = sum(q.shape[0] for q in items) * 2 if new else items[0].shape[0]
         meta.append((len(items) if new else 0, first_key))
         if new:
             out_shape.append(jax.ShapeDtypeStruct((cols, width), BF16))
-        else:
-            aliases[len(args) + 1], aliases[len(args) + 2] = len(out_shape), len(out_shape) + 1
         out_shape += [jax.ShapeDtypeStruct((width, cols), F32), jax.ShapeDtypeStruct((8, cols), F32)]
         args += items
-        work += cols * (rows_k - first_key)
         own_cols += cols // (n_export + 1)
     args += kv_list
     if not first:
@@ -285,7 +282,6 @@
             in_specs=[VMEM] * len(args),
             out_specs=[VMEM] * len(out_shape),
             scratch_shapes=[pltpu.VMEM((rows_k, width), BF16)] * 2,
-            input_output_aliases=aliases,
             compiler_params=params(),
             cost_estimate=pl.CostEstimate(flops=1, bytes_accessed=1, transcendentals=0),
         )(*args)

time: 165 us -> 171 us (1.036)
  Pallas kernels: 133 us -> 139 us
    pallas_call x4, Pallas kernels: 130 us -> 136 us  [attend(): pl.pallas_call(functools.partial(attend_kernel, meta, len(kv_list), half,...]
where the time goes in v5:
time: 171 us
  Pallas kernels  139 us (81%)
  starting transfers between devices  20.7 us (12%)
  waiting for transfers between devices  10.6 us (6%)
    pallas_call x4, Pallas kernels, attend(): pl.pallas_call(functools.partial(attend_kernel, meta, len(kv_list), half,...  136 us
    ppermute x6, starting transfers between devices, over_groups(): lax.ppermute(x, 'inner', [(i, (i // rest ^ s) * rest + i % rest) for i in...  11 us
    ppermute x9, starting transfers between devices, plane(): lax.ppermute(chunk, 'blk', [(b, b ^ d) for b in range(n_blk)])  9.54 us
    ppermute x9, waiting for transfers between devices, plane(): lax.ppermute(chunk, 'blk', [(b, b ^ d) for b in range(n_blk)])  4.09 us
    ppermute x6, waiting for transfers between devices, over_groups(): lax.ppermute(x, 'inner', [(i, (i // rest ^ s) * rest + i % rest) for i in...  3.78 us
  transfers between devices with their start and end apart: 18, of which 7 were waited for; matrix products, arithmetic and copies ran while one was open for 0% of the time, Pallas kernels for 64%

profile of v5, /device:TPU:0, one launch (start us, length us, event | category | flops | bytes accessed | tf_op | source)
XLA Modules:
  0.0 170.7 jit_solution(10014233619937834618)
XLA Ops:
  0.0 1.6 shard_map.55
  1.6 3.1 %collective-permute-start = (bf16[192,384]{1,0:T(8,128)(2,1)S(1)}, bf16[192,384]{1,0:T(8,128)(2,1)S(1)}, u32[]{:S(2)}, u32[]{:S(2)}) collective-permute-start(bf16[192,384]{1,0:T(8,128)(2,1)S(1)} %get-tuple-element.42), channel_id=1, source_target_pairs={{0,2},{1,3},{2,0},{3,1},{4,6},{5,7},{6,4},{7,5},{8,10},{9,11},{10,... | collective-permute-start | bytes 442376 | tf_op jit(solution)/shard_map/ppermute | solution.py:367
  4.7 2.6 %collective-permute-start.1 = (bf16[192,384]{1,0:T(8,128)(2,1)S(1)}, bf16[192,384]{1,0:T(8,128)(2,1)S(1)}, u32[]{:S(2)}, u32[]{:S(2)}) collective-permute-start(bf16[192,384]{1,0:T(8,128)(2,1)S(1)} %get-tuple-element.43), channel_id=1, source_target_pairs={{0,4},{1,5},{2,6},{3,7},{4,0},{5,1},{6,2},{7,3},{8,12},{9,13},{10,... | collective-permute-start | bytes 442376 | tf_op jit(solution)/shard_map/ppermute | solution.py:367
  7.3 2.5 %collective-permute-start.2 = (bf16[128,384]{1,0:T(8,128)(2,1)S(1)}, bf16[128,384]{1,0:T(8,128)(2,1)S(1)}, u32[]{:S(2)}, u32[]{:S(2)}) collective-permute-start(bf16[128,384]{1,0:T(8,128)(2,1)S(1)} %slice.25.refs_2_.refs_5_), channel_id=1, source_target_pairs={{0,24},{8,16},{16,8},{24,0},{1,25},{9,17},{17,9},{25,1},{2,26},{10... | collective-permute-start | bytes 294920 | tf_op jit(solution)/shard_map/ppermute | solution.py:376
  9.8 0.5 collective-permute-start.3
  10.3 0.5 collective-permute-start.4
  10.9 2.4 %collective-permute-done.2.refs_4_.refs_7_ = bf16[128,384]{1,0:T(8,128)(2,1)S(1)} collective-permute-done((bf16[128,384]{1,0:T(8,128)(2,1)S(1)}, bf16[128,384]{1,0:T(8,128)(2,1)S(1)}, u32[]{:S(2)}, u32[]{:S(2)}) %collective-permute-start.2) | collective-permute-done | bytes 98336 | tf_op jit(solution)/shard_map/ppermute | solution.py:376
  13.2 1.3 collective-permute-done.3.refs_5_.refs_8_
  15.1 1.7 collective-permute-start.6
  16.8 2.5 %collective-permute-start.10 = (bf16[256,384]{1,0:T(8,128)(2,1)S(1)}, bf16[256,384]{1,0:T(8,128)(2,1)S(1)}, u32[]{:S(2)}, u32[]{:S(2)}) collective-permute-start(bf16[256,384]{1,0:T(8,128)(2,1)S(1)} %pad_maximum_fusion.refs_3_.refs_6_), channel_id=1, source_target_pairs={{0,24},{8,16},{16,8},{24,0},{1,25},{9,17},{17,9},{25,1},{2,26},{10... | collective-permute-start | bytes 589832 | tf_op jit(solution)/shard_map/ppermute | solution.py:376
  19.4 0.5 collective-permute-start.8
  19.9 0.5 collective-permute-start.9
  20.4 38.5 %shard_map.56 = (bf16[768,384]{1,0:T(8,128)(2,1)S(1)}, f32[384,768]{1,0:T(8,128)S(1)}, f32[8,768]{1,0:T(8,128)S(1)}, f32[8,128]{1,0:T(8,128)S(1)}) custom-call(bf16[192,384]{1,0:T(8,128)(2,1)S(1)} %pad_maximum_fusion.1.refs_0_, bf16[192,384]{1,0:T(8,128)(2,1)S(1)} %collective-permute-done.5.refs_1_, bf16[128,384]{1,0:T(8,128)(2,1)S(1)} %slice.25.refs_2_.refs_5_, ...), custom_call_target="tpu_custom_call" | custom-call | flops 1 | bytes 1 | tf_op jit(solution)/shard_map/pallas_call | solution.py:279
  59.1 1.1 collective-permute-done.7.refs_4_
  60.2 2.4 %collective-permute-start.13 = (bf16[128,384]{1,0:T(8,128)(2,1)S(1)}, bf16[128,384]{1,0:T(8,128)(2,1)S(1)}, u32[]{:S(2)}, u32[]{:S(2)}) collective-permute-start(bf16[128,384]{1,0:T(8,128)(2,1)S(1)} %slice.31.refs_10_), channel_id=1, source_target_pairs={{0,8},{8,0},{16,24},{24,16},{1,9},{9,1},{17,25},{25,17},{2,10},{10... | collective-permute-start | bytes 294920 | tf_op jit(solution)/shard_map/ppermute | solution.py:376
  62.6 20.4 %shard_map.57 = (f32[384,768]{1,0:T(8,128)S(1)}, f32[8,768]{1,0:T(8,128)S(1)}, bf16[256,384]{1,0:T(8,128)(2,1)S(1)}, f32[384,256]{1,0:T(8,128)S(1)}, f32[8,256]{1,0:T(8,128)S(1)}, /*index=5*/f32[8,128]{1,0:T(8,128)S(1)}) custom-call(bf16[768,384]{1,0:T(8,128)(2,1)S(1)} %get-tuple-element.47.refs_0_, f32[384,768]{1,0:T(8,128)S(1)} %get-tuple-element.48.refs_1_, ...), custom_call_target="tpu_custom_call" | custom-call | flops 1 | bytes 1 | tf_op jit(solution)/shard_map/pallas_call | solution.py:279
  83.0 51.0 %shard_map.58 = (f32[384,768]{1,0:T(8,128)S(1)}, f32[8,768]{1,0:T(8,128)S(1)}, f32[384,256]{1,0:T(8,128)S(1)}, f32[8,256]{1,0:T(8,128)S(1)}, f32[8,128]{1,0:T(8,128)S(1)}) custom-call(bf16[768,384]{1,0:T(8,128)(2,1)S(1)} %get-tuple-element.47.refs_0_, f32[384,768]{1,0:T(8,128)S(1)} %get-tuple-element.54.refs_1_, f32[8,768]{1,0:T(8,128)S(1)} %get-tuple-element.55.refs_2_, ...), custom_call_target="tpu_custom_call" | custom-call | flops 1 | bytes 1 | tf_op jit(solution)/shard_map/pallas_call | solution.py:279
  134.1 26.4 %shard_map.59 = (f32[384,768]{1,0:T(8,128)S(1)}, f32[8,768]{1,0:T(8,128)S(1)}, f32[384,256]{1,0:T(8,128)S(1)}, f32[8,256]{1,0:T(8,128)S(1)}, f32[8,128]{1,0:T(8,128)}, /*index=5*/bf16[288,512]{1,0:T(8,128)(2,1)S(1)}) custom-call(bf16[768,384]{1,0:T(8,128)(2,1)S(1)} %get-tuple-element.47.refs_0_, f32[384,768]{1,0:T(8,128)S(1)} %get-tuple-element.63.refs_1_, ...), custom_call_target="tpu_custom_call" | custom-call | flops 1 | bytes 1 | tf_op jit(solution)/shard_map/pallas_call | solution.py:279
  160.5 1.6 collective-permute-done.14.refs_4_
  162.5 2.1 %collective-permute-start.17 = (bf16[192,128]{1,0:T(8,128)(2,1)S(1)}, bf16[192,128]{1,0:T(8,128)(2,1)S(1)}, u32[]{:S(2)}, u32[]{:S(2)}) collective-permute-start(bf16[192,128]{1,0:T(8,128)(2,1)S(1)} %get-tuple-element.76), channel_id=1, source_target_pairs={{0,6},{1,7},{2,4},{3,5},{4,2},{5,3},{6,0},{7,1},{8,14},{9,15},{10,... | collective-permute-start | bytes 147464 | tf_op jit(solution)/shard_map/ppermute | solution.py:367
  164.6 1.2 collective-permute-start.15
  165.8 2.9 %collective-permute-done.16.refs_2_ = bf16[192,128]{1,0:T(8,128)(2,1)S(1)} collective-permute-done((bf16[192,128]{1,0:T(8,128)(2,1)S(1)}, bf16[192,128]{1,0:T(8,128)(2,1)S(1)}, u32[]{:S(2)}, u32[]{:S(2)}) %collective-permute-start.16) | collective-permute-done | bytes 49184 | tf_op jit(solution)/shard_map/ppermute | solution.py:367
  168.8 0.8 collective-permute-done.15.refs_1_
  169.6 1.1 shard_map.62
  (32 shorter events, 1.2 us)
Async XLA Ops:
  1.6 13.3 %collective-permute-start = (bf16[192,384]{1,0:T(8,128)(2,1)S(1)}, bf16[192,384]{1,0:T(8,128)(2,1)S(1)}, u32[]{:S(2)}, u32[]{:S(2)}) collective-permute-start(bf16[192,384]{1,0:T(8,128)(2,1)S(1)} %get-tuple-element.42), channel_id=1, source_target_pairs={{0,2},{1,3},{2,0},{3,1},{4,6},{5,7},{6,4},{7,5},{8,10},{9,11},{10,... | collective-permute-start | bytes 442376 | tf_op jit(solution)/shard_map/ppermute | solution.py:367
  4.7 10.2 %collective-permute-start.1 = (bf16[192,384]{1,0:T(8,128)(2,1)S(1)}, bf16[192,384]{1,0:T(8,128)(2,1)S(1)}, u32[]{:S(2)}, u32[]{:S(2)}) collective-permute-start(bf16[192,384]{1,0:T(8,128)(2,1)S(1)} %get-tuple-element.43), channel_id=1, source_target_pairs={{0,4},{1,5},{2,6},{3,7},{4,0},{5,1},{6,2},{7,3},{8,12},{9,13},{10,... | collective-permute-start | bytes 442376 | tf_op jit(solution)/shard_map/ppermute | solution.py:367
  7.3 5.9 %collective-permute-start.2 = (bf16[128,384]{1,0:T(8,128)(2,1)S(1)}, bf16[128,384]{1,0:T(8,128)(2,1)S(1)}, u32[]{:S(2)}, u32[]{:S(2)}) collective-permute-start(bf16[128,384]{1,0:T(8,128)(2,1)S(1)} %slice.25.refs_2_.refs_5_), channel_id=1, source_target_pairs={{0,24},{8,16},{16,8},{24,0},{1,25},{9,17},{17,9},{25,1},{2,26},{10... | collective-permute-start | bytes 294920 | tf_op jit(solution)/shard_map/ppermute | solution.py:376
  9.8 4.7 %collective-permute-start.3 = (bf16[128,384]{1,0:T(8,128)(2,1)S(1)}, bf16[128,384]{1,0:T(8,128)(2,1)S(1)}, u32[]{:S(2)}, u32[]{:S(2)}) collective-permute-start(bf16[128,384]{1,0:T(8,128)(2,1)S(1)} %slice.25.refs_2_.refs_5_), channel_id=1, source_target_pairs={{0,16},{8,24},{16,0},{24,8},{1,17},{9,25},{17,1},{25,9},{2,18},{10... | collective-permute-start | bytes 294920 | tf_op jit(solution)/shard_map/ppermute | solution.py:376
  10.3 4.6 %collective-permute-start.4 = (bf16[128,384]{1,0:T(8,128)(2,1)S(1)}, bf16[128,384]{1,0:T(8,128)(2,1)S(1)}, u32[]{:S(2)}, u32[]{:S(2)}) collective-permute-start(bf16[128,384]{1,0:T(8,128)(2,1)S(1)} %slice.25.refs_2_.refs_5_), channel_id=1, source_target_pairs={{0,8},{8,0},{16,24},{24,16},{1,9},{9,1},{17,25},{25,17},{2,10},{10... | collective-permute-start | bytes 294920 | tf_op jit(solution)/shard_map/ppermute | solution.py:376
  15.0 1.8 %collective-permute-start.5 = (bf16[192,384]{1,0:T(8,128)(2,1)S(1)}, bf16[192,384]{1,0:T(8,128)(2,1)S(1)}, u32[]{:S(2)}, u32[]{:S(2)}) collective-permute-start(bf16[192,384]{1,0:T(8,128)(2,1)S(1)} %pad_maximum_fusion.1.refs_0_), channel_id=1, source_target_pairs={{0,1},{1,0},{2,3},{3,2},{4,5},{5,4},{6,7},{7,6},{8,9},{9,8},{10,11... | collective-permute-start | bytes 442376 | tf_op jit(solution)/shard_map/ppermute | solution.py:370
  15.1 43.8 %collective-permute-start.6 = (bf16[192,384]{1,0:T(8,128)(2,1)S(1)}, bf16[192,384]{1,0:T(8,128)(2,1)S(1)}, u32[]{:S(2)}, u32[]{:S(2)}) collective-permute-start(bf16[192,384]{1,0:T(8,128)(2,1)S(1)} %get-tuple-element.51), channel_id=1, source_target_pairs={{0,6},{1,7},{2,4},{3,5},{4,2},{5,3},{6,0},{7,1},{8,14},{9,15},{10,... | collective-permute-start | bytes 442376 | tf_op jit(solution)/shard_map/ppermute | solution.py:367
  16.8 43.4 %collective-permute-start.10 = (bf16[256,384]{1,0:T(8,128)(2,1)S(1)}, bf16[256,384]{1,0:T(8,128)(2,1)S(1)}, u32[]{:S(2)}, u32[]{:S(2)}) collective-permute-start(bf16[256,384]{1,0:T(8,128)(2,1)S(1)} %pad_maximum_fusion.refs_3_.refs_6_), channel_id=1, source_target_pairs={{0,24},{8,16},{16,8},{24,0},{1,25},{9,17},{17,9},{25,1},{2,26},{10... | collective-permute-start | bytes 589832 | tf_op jit(solution)/shard_map/ppermute | solution.py:376
  19.4 63.7 %collective-permute-start.8 = (bf16[256,384]{1,0:T(8,128)(2,1)S(1)}, bf16[256,384]{1,0:T(8,128)(2,1)S(1)}, u32[]{:S(2)}, u32[]{:S(2)}) collective-permute-start(bf16[256,384]{1,0:T(8,128)(2,1)S(1)} %pad_maximum_fusion.refs_3_.refs_6_), channel_id=1, source_target_pairs={{0,8},{8,0},{16,24},{24,16},{1,9},{9,1},{17,25},{25,17},{2,10},{10... | collective-permute-start | bytes 589832 | tf_op jit(solution)/shard_map/ppermute | solution.py:376
  19.9 63.1 %collective-permute-start.9 = (bf16[256,384]{1,0:T(8,128)(2,1)S(1)}, bf16[256,384]{1,0:T(8,128)(2,1)S(1)}, u32[]{:S(2)}, u32[]{:S(2)}) collective-permute-start(bf16[256,384]{1,0:T(8,128)(2,1)S(1)} %pad_maximum_fusion.refs_3_.refs_6_), channel_id=1, source_target_pairs={{0,16},{8,24},{16,0},{24,8},{1,17},{9,25},{17,1},{25,9},{2,18},{10... | collective-permute-start | bytes 589832 | tf_op jit(solution)/shard_map/ppermute | solution.py:376
  58.9 1.3 collective-permute-start.7
  59.0 75.0 %collective-permute-start.11 = (bf16[128,384]{1,0:T(8,128)(2,1)S(1)}, bf16[128,384]{1,0:T(8,128)(2,1)S(1)}, u32[]{:S(2)}, u32[]{:S(2)}) collective-permute-start(bf16[128,384]{1,0:T(8,128)(2,1)S(1)} %slice.31.refs_10_), channel_id=1, source_target_pairs={{0,24},{8,16},{16,8},{24,0},{1,25},{9,17},{17,9},{25,1},{2,26},{10... | collective-permute-start | bytes 294920 | tf_op jit(solution)/shard_map/ppermute | solution.py:376
  60.2 73.8 %collective-permute-start.12 = (bf16[128,384]{1,0:T(8,128)(2,1)S(1)}, bf16[128,384]{1,0:T(8,128)(2,1)S(1)}, u32[]{:S(2)}, u32[]{:S(2)}) collective-permute-start(bf16[128,384]{1,0:T(8,128)(2,1)S(1)} %slice.31.refs_10_), channel_id=1, source_target_pairs={{0,16},{8,24},{16,0},{24,8},{1,17},{9,25},{17,1},{25,9},{2,18},{10... | collective-permute-start | bytes 294920 | tf_op jit(solution)/shard_map/ppermute | solution.py:376
  60.2 73.8 %collective-permute-start.13 = (bf16[128,384]{1,0:T(8,128)(2,1)S(1)}, bf16[128,384]{1,0:T(8,128)(2,1)S(1)}, u32[]{:S(2)}, u32[]{:S(2)}) collective-permute-start(bf16[128,384]{1,0:T(8,128)(2,1)S(1)} %slice.31.refs_10_), channel_id=1, source_target_pairs={{0,8},{8,0},{16,24},{24,16},{1,9},{9,1},{17,25},{25,17},{2,10},{10... | collective-permute-start | bytes 294920 | tf_op jit(solution)/shard_map/ppermute | solution.py:376
  160.5 1.6 collective-permute-start.14
  162.1 7.5 %copy-start = (bf16[768,768]{1,0:T(8,128)(2,1)S(1)}, bf16[768,768]{1,0:T(8,128)(2,1)}, u32[]{:S(2)}) copy-start(bf16[768,768]{1,0:T(8,128)(2,1)} %refs_4_.1) | copy-start | bytes 3538948
  162.1 6.6 %collective-permute-start.16 = (bf16[192,128]{1,0:T(8,128)(2,1)S(1)}, bf16[192,128]{1,0:T(8,128)(2,1)S(1)}, u32[]{:S(2)}, u32[]{:S(2)}) collective-permute-start(bf16[192,128]{1,0:T(8,128)(2,1)S(1)} %get-tuple-element.75), channel_id=1, source_target_pairs={{0,4},{1,5},{2,6},{3,7},{4,0},{5,1},{6,2},{7,3},{8,12},{9,13},{10,... | collective-permute-start | bytes 147464 | tf_op jit(solution)/shard_map/ppermute | solution.py:367
  162.5 6.3 %collective-permute-start.17 = (bf16[192,128]{1,0:T(8,128)(2,1)S(1)}, bf16[192,128]{1,0:T(8,128)(2,1)S(1)}, u32[]{:S(2)}, u32[]{:S(2)}) collective-permute-start(bf16[192,128]{1,0:T(8,128)(2,1)S(1)} %get-tuple-element.76), channel_id=1, source_target_pairs={{0,6},{1,7},{2,4},{3,5},{4,2},{5,3},{6,0},{7,1},{8,14},{9,15},{10,... | collective-permute-start | bytes 147464 | tf_op jit(solution)/shard_map/ppermute | solution.py:367
  164.6 5.0 %collective-permute-start.15 = (bf16[192,128]{1,0:T(8,128)(2,1)S(1)}, bf16[192,128]{1,0:T(8,128)(2,1)S(1)}, u32[]{:S(2)}, u32[]{:S(2)}) collective-permute-start(bf16[192,128]{1,0:T(8,128)(2,1)S(1)} %get-tuple-element.74), channel_id=1, source_target_pairs={{0,2},{1,3},{2,0},{3,1},{4,6},{5,7},{6,4},{7,5},{8,10},{9,11},{10,... | collective-permute-start | bytes 147464 | tf_op jit(solution)/shard_map/ppermute | solution.py:367

commit v6 on v5

--- a/solution.py
+++ b/solution.py
@@ -234,7 +234,7 @@
             own = largest_norm(qs)
             length = own if length is None else jnp.maximum(length, own)
     spread_keys(kv_refs, ks, vs)
-    safe = length * largest_norm(ks) * 1.05 <= SAFE * SAFE
+    safe = jnp.logical_and(length * largest_norm(ks) * 1.05 <= SAFE * SAFE, length < LIMIT)
     info[...] = jnp.full(info.shape, jnp.where(safe, length, LIMIT), F32)
     work = []
     for (n_q, first_key), mine, (qs, acc, top) in zip(sets, given, held):
@@ -247,11 +247,12 @@
             cols = qs.shape[0] // (n_export + 1)
             at, to = pl.ds((i + 1) * cols, cols), pl.ds(place, cols)
             for j in range(qs.shape[1] // LANES):
-                start = j * (HEAD_DIM + 2 * ONES)
+                start = j * (HEAD_DIM + ONES)
                 out[pl.ds(start, HEAD_DIM), to] = acc[pl.ds(j * LANES + HEAD_DIM, HEAD_DIM), at].astype(BF16)
-                out[pl.ds(start + HEAD_DIM, ONES), to] = acc[pl.ds(j * LANES, ONES), at].astype(BF16)
-                shift = jnp.broadcast_to(top[pl.ds(j, 1), at], (ONES, cols))
-                out[pl.ds(start + HEAD_DIM + ONES, ONES), to] = shift.astype(BF16)
+                sums = acc[pl.ds(j * LANES, ONES), at]
+                shift = jnp.broadcast_to(top[pl.ds(j, 1), at], sums.shape)
+                upper = lax.broadcasted_iota(jnp.int32, sums.shape, 0) < ONES // 2
+                out[pl.ds(start + HEAD_DIM, ONES), to] = jnp.where(upper, sums, shift).astype(BF16)
             place += cols
 
 
@@ -274,7 +275,7 @@
     if not first:
         args.append(info)
     out_shape.append(jax.ShapeDtypeStruct((8, LANES), F32))
-    out_shape += [jax.ShapeDtypeStruct((slots * (HEAD_DIM + 2 * ONES), own_cols), BF16)] * n_export
+    out_shape += [jax.ShapeDtypeStruct((slots * (HEAD_DIM + ONES), own_cols), BF16)] * n_export
     out = list(
         pl.pallas_call(
             functools.partial(attend_kernel, meta, len(kv_list), half, first, n_export),
@@ -296,7 +297,7 @@
     held = [refs[2 * i : 2 * i + 2] for i in range(n_sets)]
     imports, outs = refs[2 * n_sets : 2 * n_sets + n_import], list(refs[2 * n_sets + n_import :])
     piece = outs[0].shape[1]
-    step = HEAD_DIM + 2 * ONES
+    step = HEAD_DIM + ONES
     place = 0
     for acc, top in held:
         cols = acc.shape[1] // (n_import + 1)
@@ -311,8 +312,8 @@
                 high = top[pl.ds(j, 1), at]
                 for ref in imports:
                     values = ref[pl.ds(j * step, HEAD_DIM), there].astype(F32)
-                    sums = ref[pl.ds(j * step + HEAD_DIM, ONES), there].astype(F32)[:1]
-                    shift = ref[pl.ds(j * step + HEAD_DIM + ONES, ONES), there].astype(F32)[:1]
+                    both = ref[pl.ds(j * step + HEAD_DIM, ONES), there].astype(F32)
+                    sums, shift = both[:1], both[ONES // 2 : ONES // 2 + 1]
                     new = jnp.maximum(high, shift)
                     mine, theirs = jnp.exp(high - new), jnp.exp(shift - new)
                     total = total * mine + values * theirs
@@ -388,7 +389,7 @@
     if n_blk == 4 and rest == 2:
         own0 = pieces[0][:rows]
         near0 = plane(own0, (3, 2, 1))
-        pieces[1], pieces[2] = over_groups(pieces[1], 1), over_groups(pieces[2], 2)
+        pieces[2], pieces[1] = over_groups(pieces[2], 2), over_groups(pieces[1], 1)
         pieces[3] = over_groups(after(pieces[3], pieces[1], pieces[2]), 3)
         pieces[1], pieces[2] = after((pieces[1], pieces[2]), *near0)
         q_early = gathered_queries(pieces[:3])

time: 171 us -> 171 us (level)
  no operation moved by 1% of the time
where the time goes in v6:
time: 171 us
  Pallas kernels  139 us (81%)
  starting transfers between devices  20.7 us (12%)
  waiting for transfers between devices  10.5 us (6%)
    pallas_call x4, Pallas kernels, attend(): pl.pallas_call(functools.partial(attend_kernel, meta, len(kv_list), half,...  136 us
    ppermute x6, starting transfers between devices, over_groups(): lax.ppermute(x, 'inner', [(i, (i // rest ^ s) * rest + i % rest) for i in...  11 us
    ppermute x9, starting transfers between devices, plane(): lax.ppermute(chunk, 'blk', [(b, b ^ d) for b in range(n_blk)])  9.54 us
    ppermute x9, waiting for transfers between devices, plane(): lax.ppermute(chunk, 'blk', [(b, b ^ d) for b in range(n_blk)])  4.09 us
    ppermute x6, waiting for transfers between devices, over_groups(): lax.ppermute(x, 'inner', [(i, (i // rest ^ s) * rest + i % rest) for i in...  3.78 us
  transfers between devices with their start and end apart: 18, of which 7 were waited for; matrix products, arithmetic and copies ran while one was open for 0% of the time, Pallas kernels for 64%

profile of v6, /device:TPU:0, one launch (start us, length us, event | category | flops | bytes accessed | tf_op | source)
XLA Modules:
  0.0 170.6 jit_solution(8250645304465034012)
XLA Ops:
  0.0 1.6 shard_map.55
  1.6 3.1 %collective-permute-start = (bf16[192,384]{1,0:T(8,128)(2,1)S(1)}, bf16[192,384]{1,0:T(8,128)(2,1)S(1)}, u32[]{:S(2)}, u32[]{:S(2)}) collective-permute-start(bf16[192,384]{1,0:T(8,128)(2,1)S(1)} %get-tuple-element.42), channel_id=1, source_target_pairs={{0,2},{1,3},{2,0},{3,1},{4,6},{5,7},{6,4},{7,5},{8,10},{9,11},{10,... | collective-permute-start | bytes 442376 | tf_op jit(solution)/shard_map/ppermute | solution.py:368
  4.7 2.6 %collective-permute-start.1 = (bf16[192,384]{1,0:T(8,128)(2,1)S(1)}, bf16[192,384]{1,0:T(8,128)(2,1)S(1)}, u32[]{:S(2)}, u32[]{:S(2)}) collective-permute-start(bf16[192,384]{1,0:T(8,128)(2,1)S(1)} %get-tuple-element.43), channel_id=1, source_target_pairs={{0,4},{1,5},{2,6},{3,7},{4,0},{5,1},{6,2},{7,3},{8,12},{9,13},{10,... | collective-permute-start | bytes 442376 | tf_op jit(solution)/shard_map/ppermute | solution.py:368
  7.3 2.5 %collective-permute-start.2 = (bf16[128,384]{1,0:T(8,128)(2,1)S(1)}, bf16[128,384]{1,0:T(8,128)(2,1)S(1)}, u32[]{:S(2)}, u32[]{:S(2)}) collective-permute-start(bf16[128,384]{1,0:T(8,128)(2,1)S(1)} %slice.25.refs_2_.refs_5_), channel_id=1, source_target_pairs={{0,24},{8,16},{16,8},{24,0},{1,25},{9,17},{17,9},{25,1},{2,26},{10... | collective-permute-start | bytes 294920 | tf_op jit(solution)/shard_map/ppermute | solution.py:377
  9.8 0.5 collective-permute-start.3
  10.3 0.5 collective-permute-start.4
  10.9 2.4 %collective-permute-done.2.refs_4_.refs_7_ = bf16[128,384]{1,0:T(8,128)(2,1)S(1)} collective-permute-done((bf16[128,384]{1,0:T(8,128)(2,1)S(1)}, bf16[128,384]{1,0:T(8,128)(2,1)S(1)}, u32[]{:S(2)}, u32[]{:S(2)}) %collective-permute-start.2) | collective-permute-done | bytes 98336 | tf_op jit(solution)/shard_map/ppermute | solution.py:377
  13.2 1.3 collective-permute-done.3.refs_5_.refs_8_
  15.1 1.7 collective-permute-start.6
  16.8 2.5 %collective-permute-start.10 = (bf16[256,384]{1,0:T(8,128)(2,1)S(1)}, bf16[256,384]{1,0:T(8,128)(2,1)S(1)}, u32[]{:S(2)}, u32[]{:S(2)}) collective-permute-start(bf16[256,384]{1,0:T(8,128)(2,1)S(1)} %pad_maximum_fusion.refs_3_.refs_6_), channel_id=1, source_target_pairs={{0,24},{8,16},{16,8},{24,0},{1,25},{9,17},{17,9},{25,1},{2,26},{10... | collective-permute-start | bytes 589832 | tf_op jit(solution)/shard_map/ppermute | solution.py:377
  19.4 0.5 collective-permute-start.8
  19.9 0.5 collective-permute-start.9
  20.4 38.5 %shard_map.56 = (bf16[768,384]{1,0:T(8,128)(2,1)S(1)}, f32[384,768]{1,0:T(8,128)S(1)}, f32[8,768]{1,0:T(8,128)S(1)}, f32[8,128]{1,0:T(8,128)S(1)}) custom-call(bf16[192,384]{1,0:T(8,128)(2,1)S(1)} %pad_maximum_fusion.1.refs_0_, bf16[192,384]{1,0:T(8,128)(2,1)S(1)} %collective-permute-done.5.refs_1_, bf16[128,384]{1,0:T(8,128)(2,1)S(1)} %slice.25.refs_2_.refs_5_, ...), custom_call_target="tpu_custom_call" | custom-call | flops 1 | bytes 1 | tf_op jit(solution)/shard_map/pallas_call | solution.py:280
  59.1 1.1 collective-permute-done.7.refs_4_
  60.2 2.4 %collective-permute-start.13 = (bf16[128,384]{1,0:T(8,128)(2,1)S(1)}, bf16[128,384]{1,0:T(8,128)(2,1)S(1)}, u32[]{:S(2)}, u32[]{:S(2)}) collective-permute-start(bf16[128,384]{1,0:T(8,128)(2,1)S(1)} %slice.31.refs_10_), channel_id=1, source_target_pairs={{0,8},{8,0},{16,24},{24,16},{1,9},{9,1},{17,25},{25,17},{2,10},{10... | collective-permute-start | bytes 294920 | tf_op jit(solution)/shard_map/ppermute | solution.py:377
  62.6 20.4 %shard_map.57 = (f32[384,768]{1,0:T(8,128)S(1)}, f32[8,768]{1,0:T(8,128)S(1)}, bf16[256,384]{1,0:T(8,128)(2,1)S(1)}, f32[384,256]{1,0:T(8,128)S(1)}, f32[8,256]{1,0:T(8,128)S(1)}, /*index=5*/f32[8,128]{1,0:T(8,128)S(1)}) custom-call(bf16[768,384]{1,0:T(8,128)(2,1)S(1)} %get-tuple-element.47.refs_0_, f32[384,768]{1,0:T(8,128)S(1)} %get-tuple-element.48.refs_1_, ...), custom_call_target="tpu_custom_call" | custom-call | flops 1 | bytes 1 | tf_op jit(solution)/shard_map/pallas_call | solution.py:280
  83.0 51.0 %shard_map.58 = (f32[384,768]{1,0:T(8,128)S(1)}, f32[8,768]{1,0:T(8,128)S(1)}, f32[384,256]{1,0:T(8,128)S(1)}, f32[8,256]{1,0:T(8,128)S(1)}, f32[8,128]{1,0:T(8,128)S(1)}) custom-call(bf16[768,384]{1,0:T(8,128)(2,1)S(1)} %get-tuple-element.47.refs_0_, f32[384,768]{1,0:T(8,128)S(1)} %get-tuple-element.54.refs_1_, f32[8,768]{1,0:T(8,128)S(1)} %get-tuple-element.55.refs_2_, ...), custom_call_target="tpu_custom_call" | custom-call | flops 1 | bytes 1 | tf_op jit(solution)/shard_map/pallas_call | solution.py:280
  134.1 26.4 %shard_map.59 = (f32[384,768]{1,0:T(8,128)S(1)}, f32[8,768]{1,0:T(8,128)S(1)}, f32[384,256]{1,0:T(8,128)S(1)}, f32[8,256]{1,0:T(8,128)S(1)}, f32[8,128]{1,0:T(8,128)}, /*index=5*/bf16[240,512]{1,0:T(8,128)(2,1)S(1)}) custom-call(bf16[768,384]{1,0:T(8,128)(2,1)S(1)} %get-tuple-element.47.refs_0_, f32[384,768]{1,0:T(8,128)S(1)} %get-tuple-element.63.refs_1_, ...), custom_call_target="tpu_custom_call" | custom-call | flops 1 | bytes 1 | tf_op jit(solution)/shard_map/pallas_call | solution.py:280
  160.5 1.5 collective-permute-done.14.refs_4_
  162.4 2.0 %collective-permute-start.17 = (bf16[192,128]{1,0:T(8,128)(2,1)S(1)}, bf16[192,128]{1,0:T(8,128)(2,1)S(1)}, u32[]{:S(2)}, u32[]{:S(2)}) collective-permute-start(bf16[192,128]{1,0:T(8,128)(2,1)S(1)} %get-tuple-element.76), channel_id=1, source_target_pairs={{0,6},{1,7},{2,4},{3,5},{4,2},{5,3},{6,0},{7,1},{8,14},{9,15},{10,... | collective-permute-start | bytes 147464 | tf_op jit(solution)/shard_map/ppermute | solution.py:368
  164.5 1.2 collective-permute-start.15
  165.7 2.9 %collective-permute-done.16.refs_2_ = bf16[192,128]{1,0:T(8,128)(2,1)S(1)} collective-permute-done((bf16[192,128]{1,0:T(8,128)(2,1)S(1)}, bf16[192,128]{1,0:T(8,128)(2,1)S(1)}, u32[]{:S(2)}, u32[]{:S(2)}) %collective-permute-start.16) | collective-permute-done | bytes 49184 | tf_op jit(solution)/shard_map/ppermute | solution.py:368
  168.7 0.8 collective-permute-done.15.refs_1_
  169.5 1.1 shard_map.62
  (32 shorter events, 1.2 us)
Async XLA Ops:
  1.6 13.3 %collective-permute-start = (bf16[192,384]{1,0:T(8,128)(2,1)S(1)}, bf16[192,384]{1,0:T(8,128)(2,1)S(1)}, u32[]{:S(2)}, u32[]{:S(2)}) collective-permute-start(bf16[192,384]{1,0:T(8,128)(2,1)S(1)} %get-tuple-element.42), channel_id=1, source_target_pairs={{0,2},{1,3},{2,0},{3,1},{4,6},{5,7},{6,4},{7,5},{8,10},{9,11},{10,... | collective-permute-start | bytes 442376 | tf_op jit(solution)/shard_map/ppermute | solution.py:368
  4.7 10.2 %collective-permute-start.1 = (bf16[192,384]{1,0:T(8,128)(2,1)S(1)}, bf16[192,384]{1,0:T(8,128)(2,1)S(1)}, u32[]{:S(2)}, u32[]{:S(2)}) collective-permute-start(bf16[192,384]{1,0:T(8,128)(2,1)S(1)} %get-tuple-element.43), channel_id=1, source_target_pairs={{0,4},{1,5},{2,6},{3,7},{4,0},{5,1},{6,2},{7,3},{8,12},{9,13},{10,... | collective-permute-start | bytes 442376 | tf_op jit(solution)/shard_map/ppermute | solution.py:368
  7.3 5.9 %collective-permute-start.2 = (bf16[128,384]{1,0:T(8,128)(2,1)S(1)}, bf16[128,384]{1,0:T(8,128)(2,1)S(1)}, u32[]{:S(2)}, u32[]{:S(2)}) collective-permute-start(bf16[128,384]{1,0:T(8,128)(2,1)S(1)} %slice.25.refs_2_.refs_5_), channel_id=1, source_target_pairs={{0,24},{8,16},{16,8},{24,0},{1,25},{9,17},{17,9},{25,1},{2,26},{10... | collective-permute-start | bytes 294920 | tf_op jit(solution)/shard_map/ppermute | solution.py:377
  9.8 4.7 %collective-permute-start.3 = (bf16[128,384]{1,0:T(8,128)(2,1)S(1)}, bf16[128,384]{1,0:T(8,128)(2,1)S(1)}, u32[]{:S(2)}, u32[]{:S(2)}) collective-permute-start(bf16[128,384]{1,0:T(8,128)(2,1)S(1)} %slice.25.refs_2_.refs_5_), channel_id=1, source_target_pairs={{0,16},{8,24},{16,0},{24,8},{1,17},{9,25},{17,1},{25,9},{2,18},{10... | collective-permute-start | bytes 294920 | tf_op jit(solution)/shard_map/ppermute | solution.py:377
  10.3 4.6 %collective-permute-start.4 = (bf16[128,384]{1,0:T(8,128)(2,1)S(1)}, bf16[128,384]{1,0:T(8,128)(2,1)S(1)}, u32[]{:S(2)}, u32[]{:S(2)}) collective-permute-start(bf16[128,384]{1,0:T(8,128)(2,1)S(1)} %slice.25.refs_2_.refs_5_), channel_id=1, source_target_pairs={{0,8},{8,0},{16,24},{24,16},{1,9},{9,1},{17,25},{25,17},{2,10},{10... | collective-permute-start | bytes 294920 | tf_op jit(solution)/shard_map/ppermute | solution.py:377
  15.0 1.8 %collective-permute-start.5 = (bf16[192,384]{1,0:T(8,128)(2,1)S(1)}, bf16[192,384]{1,0:T(8,128)(2,1)S(1)}, u32[]{:S(2)}, u32[]{:S(2)}) collective-permute-start(bf16[192,384]{1,0:T(8,128)(2,1)S(1)} %pad_maximum_fusion.1.refs_0_), channel_id=1, source_target_pairs={{0,1},{1,0},{2,3},{3,2},{4,5},{5,4},{6,7},{7,6},{8,9},{9,8},{10,11... | collective-permute-start | bytes 442376 | tf_op jit(solution)/shard_map/ppermute | solution.py:371
  15.1 43.8 %collective-permute-start.6 = (bf16[192,384]{1,0:T(8,128)(2,1)S(1)}, bf16[192,384]{1,0:T(8,128)(2,1)S(1)}, u32[]{:S(2)}, u32[]{:S(2)}) collective-permute-start(bf16[192,384]{1,0:T(8,128)(2,1)S(1)} %get-tuple-element.51), channel_id=1, source_target_pairs={{0,6},{1,7},{2,4},{3,5},{4,2},{5,3},{6,0},{7,1},{8,14},{9,15},{10,... | collective-permute-start | bytes 442376 | tf_op jit(solution)/shard_map/ppermute | solution.py:368
  16.8 43.4 %collective-permute-start.10 = (bf16[256,384]{1,0:T(8,128)(2,1)S(1)}, bf16[256,384]{1,0:T(8,128)(2,1)S(1)}, u32[]{:S(2)}, u32[]{:S(2)}) collective-permute-start(bf16[256,384]{1,0:T(8,128)(2,1)S(1)} %pad_maximum_fusion.refs_3_.refs_6_), channel_id=1, source_target_pairs={{0,24},{8,16},{16,8},{24,0},{1,25},{9,17},{17,9},{25,1},{2,26},{10... | collective-permute-start | bytes 589832 | tf_op jit(solution)/shard_map/ppermute | solution.py:377
  19.4 63.7 %collective-permute-start.8 = (bf16[256,384]{1,0:T(8,128)(2,1)S(1)}, bf16[256,384]{1,0:T(8,128)(2,1)S(1)}, u32[]{:S(2)}, u32[]{:S(2)}) collective-permute-start(bf16[256,384]{1,0:T(8,128)(2,1)S(1)} %pad_maximum_fusion.refs_3_.refs_6_), channel_id=1, source_target_pairs={{0,8},{8,0},{16,24},{24,16},{1,9},{9,1},{17,25},{25,17},{2,10},{10... | collective-permute-start | bytes 589832 | tf_op jit(solution)/shard_map/ppermute | solution.py:377
  19.9 63.1 %collective-permute-start.9 = (bf16[256,384]{1,0:T(8,128)(2,1)S(1)}, bf16[256,384]{1,0:T(8,128)(2,1)S(1)}, u32[]{:S(2)}, u32[]{:S(2)}) collective-permute-start(bf16[256,384]{1,0:T(8,128)(2,1)S(1)} %pad_maximum_fusion.refs_3_.refs_6_), channel_id=1, source_target_pairs={{0,16},{8,24},{16,0},{24,8},{1,17},{9,25},{17,1},{25,9},{2,18},{10... | collective-permute-start | bytes 589832 | tf_op jit(solution)/shard_map/ppermute | solution.py:377
  58.9 1.3 collective-permute-start.7
  59.0 75.0 %collective-permute-start.11 = (bf16[128,384]{1,0:T(8,128)(2,1)S(1)}, bf16[128,384]{1,0:T(8,128)(2,1)S(1)}, u32[]{:S(2)}, u32[]{:S(2)}) collective-permute-start(bf16[128,384]{1,0:T(8,128)(2,1)S(1)} %slice.31.refs_10_), channel_id=1, source_target_pairs={{0,24},{8,16},{16,8},{24,0},{1,25},{9,17},{17,9},{25,1},{2,26},{10... | collective-permute-start | bytes 294920 | tf_op jit(solution)/shard_map/ppermute | solution.py:377
  60.2 73.8 %collective-permute-start.12 = (bf16[128,384]{1,0:T(8,128)(2,1)S(1)}, bf16[128,384]{1,0:T(8,128)(2,1)S(1)}, u32[]{:S(2)}, u32[]{:S(2)}) collective-permute-start(bf16[128,384]{1,0:T(8,128)(2,1)S(1)} %slice.31.refs_10_), channel_id=1, source_target_pairs={{0,16},{8,24},{16,0},{24,8},{1,17},{9,25},{17,1},{25,9},{2,18},{10... | collective-permute-start | bytes 294920 | tf_op jit(solution)/shard_map/ppermute | solution.py:377
  60.2 73.8 %collective-permute-start.13 = (bf16[128,384]{1,0:T(8,128)(2,1)S(1)}, bf16[128,384]{1,0:T(8,128)(2,1)S(1)}, u32[]{:S(2)}, u32[]{:S(2)}) collective-permute-start(bf16[128,384]{1,0:T(8,128)(2,1)S(1)} %slice.31.refs_10_), channel_id=1, source_target_pairs={{0,8},{8,0},{16,24},{24,16},{1,9},{9,1},{17,25},{25,17},{2,10},{10... | collective-permute-start | bytes 294920 | tf_op jit(solution)/shard_map/ppermute | solution.py:377
  160.5 1.5 collective-permute-start.14
  162.0 7.5 %copy-start = (bf16[768,768]{1,0:T(8,128)(2,1)S(1)}, bf16[768,768]{1,0:T(8,128)(2,1)}, u32[]{:S(2)}) copy-start(bf16[768,768]{1,0:T(8,128)(2,1)} %refs_4_.1) | copy-start | bytes 3538948
  162.1 6.6 %collective-permute-start.16 = (bf16[192,128]{1,0:T(8,128)(2,1)S(1)}, bf16[192,128]{1,0:T(8,128)(2,1)S(1)}, u32[]{:S(2)}, u32[]{:S(2)}) collective-permute-start(bf16[192,128]{1,0:T(8,128)(2,1)S(1)} %get-tuple-element.75), channel_id=1, source_target_pairs={{0,4},{1,5},{2,6},{3,7},{4,0},{5,1},{6,2},{7,3},{8,12},{9,13},{10,... | collective-permute-start | bytes 147464 | tf_op jit(solution)/shard_map/ppermute | solution.py:368
  162.4 6.3 %collective-permute-start.17 = (bf16[192,128]{1,0:T(8,128)(2,1)S(1)}, bf16[192,128]{1,0:T(8,128)(2,1)S(1)}, u32[]{:S(2)}, u32[]{:S(2)}) collective-permute-start(bf16[192,128]{1,0:T(8,128)(2,1)S(1)} %get-tuple-element.76), channel_id=1, source_target_pairs={{0,6},{1,7},{2,4},{3,5},{4,2},{5,3},{6,0},{7,1},{8,14},{9,15},{10,... | collective-permute-start | bytes 147464 | tf_op jit(solution)/shard_map/ppermute | solution.py:368
  164.5 5.0 %collective-permute-start.15 = (bf16[192,128]{1,0:T(8,128)(2,1)S(1)}, bf16[192,128]{1,0:T(8,128)(2,1)S(1)}, u32[]{:S(2)}, u32[]{:S(2)}) collective-permute-start(bf16[192,128]{1,0:T(8,128)(2,1)S(1)} %get-tuple-element.74), channel_id=1, source_target_pairs={{0,2},{1,3},{2,0},{3,1},{4,6},{5,7},{6,4},{7,5},{8,10},{9,11},{10,... | collective-permute-start | bytes 147464 | tf_op jit(solution)/shard_map/ppermute | solution.py:368

commit v7 on v6

--- a/solution.py
+++ b/solution.py
@@ -402,8 +402,8 @@
         near2 = plane(own2, (3, 2, 1))
         q_late = gathered_queries([last])
         met = sum(x.shape[0] for x in early)
-        states, info, unused = attend([(early_set, met), (q_late, 0)], [*early, own2], half, info)
-        near1 = after(tuple(near1), states[0][1])
+        states, info, unused = attend([(early_set, met), (q_late, 0)], [*early, own2, near1[2]], half, info)
+        near1 = after(tuple(near1[:2]), states[0][1])
         states, info, unused = attend([(x, 0) for x in states], list(near1), half, info)
         states, info, exports = attend([(x, 0) for x in states], near2, half, info, rest - 1)
     else:

time: 171 us -> 172 us (level)
  Pallas kernels: 139 us -> 141 us
  transfers between devices with their start and end apart: 18 -> 18, of which waited for: 7 -> 7; matrix products, arithmetic and copies ran while one was open for 0% -> 0% of each run, Pallas kernels for 64% -> 65%
where the time goes in v7:
time: 172 us
  Pallas kernels  141 us (82%)
  starting transfers between devices  20.7 us (12%)
  waiting for transfers between devices  10.5 us (6%)
    pallas_call x4, Pallas kernels, attend(): pl.pallas_call(functools.partial(attend_kernel, meta, len(kv_list), half,...  138 us
    ppermute x6, starting transfers between devices, over_groups(): lax.ppermute(x, 'inner', [(i, (i // rest ^ s) * rest + i % rest) for i in...  11 us
    ppermute x9, starting transfers between devices, plane(): lax.ppermute(chunk, 'blk', [(b, b ^ d) for b in range(n_blk)])  9.54 us
    ppermute x9, waiting for transfers between devices, plane(): lax.ppermute(chunk, 'blk', [(b, b ^ d) for b in range(n_blk)])  4.09 us
    ppermute x6, waiting for transfers between devices, over_groups(): lax.ppermute(x, 'inner', [(i, (i // rest ^ s) * rest + i % rest) for i in...  3.78 us
  transfers between devices with their start and end apart: 18, of which 7 were waited for; matrix products, arithmetic and copies ran while one was open for 0% of the time, Pallas kernels for 65%

profile of v7, /device:TPU:0, one launch (start us, length us, event | category | flops | bytes accessed | tf_op | source)
XLA Modules:
  0.0 172.0 jit_solution(13250887795075008784)
XLA Ops:
  0.0 1.6 shard_map.55
  1.6 3.1 %collective-permute-start = (bf16[192,384]{1,0:T(8,128)(2,1)S(1)}, bf16[192,384]{1,0:T(8,128)(2,1)S(1)}, u32[]{:S(2)}, u32[]{:S(2)}) collective-permute-start(bf16[192,384]{1,0:T(8,128)(2,1)S(1)} %get-tuple-element.41), channel_id=1, source_target_pairs={{0,2},{1,3},{2,0},{3,1},{4,6},{5,7},{6,4},{7,5},{8,10},{9,11},{10,... | collective-permute-start | bytes 442376 | tf_op jit(solution)/shard_map/ppermute | solution.py:368
  4.7 2.6 %collective-permute-start.1 = (bf16[192,384]{1,0:T(8,128)(2,1)S(1)}, bf16[192,384]{1,0:T(8,128)(2,1)S(1)}, u32[]{:S(2)}, u32[]{:S(2)}) collective-permute-start(bf16[192,384]{1,0:T(8,128)(2,1)S(1)} %get-tuple-element.42), channel_id=1, source_target_pairs={{0,4},{1,5},{2,6},{3,7},{4,0},{5,1},{6,2},{7,3},{8,12},{9,13},{10,... | collective-permute-start | bytes 442376 | tf_op jit(solution)/shard_map/ppermute | solution.py:368
  7.3 2.5 %collective-permute-start.2 = (bf16[128,384]{1,0:T(8,128)(2,1)S(1)}, bf16[128,384]{1,0:T(8,128)(2,1)S(1)}, u32[]{:S(2)}, u32[]{:S(2)}) collective-permute-start(bf16[128,384]{1,0:T(8,128)(2,1)S(1)} %slice.25.refs_2_.refs_5_), channel_id=1, source_target_pairs={{0,24},{8,16},{16,8},{24,0},{1,25},{9,17},{17,9},{25,1},{2,26},{10... | collective-permute-start | bytes 294920 | tf_op jit(solution)/shard_map/ppermute | solution.py:377
  9.8 0.5 collective-permute-start.3
  10.3 0.5 collective-permute-start.4
  10.9 2.4 %collective-permute-done.2.refs_4_.refs_7_ = bf16[128,384]{1,0:T(8,128)(2,1)S(1)} collective-permute-done((bf16[128,384]{1,0:T(8,128)(2,1)S(1)}, bf16[128,384]{1,0:T(8,128)(2,1)S(1)}, u32[]{:S(2)}, u32[]{:S(2)}) %collective-permute-start.2) | collective-permute-done | bytes 98336 | tf_op jit(solution)/shard_map/ppermute | solution.py:377
  13.2 1.3 collective-permute-done.3.refs_5_.refs_8_
  15.1 1.7 collective-permute-start.6
  16.8 2.5 %collective-permute-start.8 = (bf16[256,384]{1,0:T(8,128)(2,1)S(1)}, bf16[256,384]{1,0:T(8,128)(2,1)S(1)}, u32[]{:S(2)}, u32[]{:S(2)}) collective-permute-start(bf16[256,384]{1,0:T(8,128)(2,1)S(1)} %pad_maximum_fusion.refs_3_.refs_6_), channel_id=1, source_target_pairs={{0,24},{8,16},{16,8},{24,0},{1,25},{9,17},{17,9},{25,1},{2,26},{10... | collective-permute-start | bytes 589832 | tf_op jit(solution)/shard_map/ppermute | solution.py:377
  19.4 0.5 collective-permute-start.10
  19.9 0.5 collective-permute-start.9
  20.4 38.4 %shard_map.56 = (bf16[768,384]{1,0:T(8,128)(2,1)S(1)}, f32[384,768]{1,0:T(8,128)S(1)}, f32[8,768]{1,0:T(8,128)S(1)}, f32[8,128]{1,0:T(8,128)S(1)}) custom-call(bf16[192,384]{1,0:T(8,128)(2,1)S(1)} %pad_maximum_fusion.1.refs_0_, bf16[192,384]{1,0:T(8,128)(2,1)S(1)} %collective-permute-done.5.refs_1_, bf16[128,384]{1,0:T(8,128)(2,1)S(1)} %slice.25.refs_2_.refs_5_, ...), custom_call_target="tpu_custom_call" | custom-call | flops 1 | bytes 1 | tf_op jit(solution)/shard_map/pallas_call | solution.py:280
  59.0 1.1 collective-permute-done.7.refs_4_
  60.2 2.4 %collective-permute-start.13 = (bf16[128,384]{1,0:T(8,128)(2,1)S(1)}, bf16[128,384]{1,0:T(8,128)(2,1)S(1)}, u32[]{:S(2)}, u32[]{:S(2)}) collective-permute-start(bf16[128,384]{1,0:T(8,128)(2,1)S(1)} %slice.31.refs_10_), channel_id=1, source_target_pairs={{0,8},{8,0},{16,24},{24,16},{1,9},{9,1},{17,25},{25,17},{2,10},{10... | collective-permute-start | bytes 294920 | tf_op jit(solution)/shard_map/ppermute | solution.py:377
  62.5 38.8 %shard_map.57 = (f32[384,768]{1,0:T(8,128)S(1)}, f32[8,768]{1,0:T(8,128)S(1)}, bf16[256,384]{1,0:T(8,128)(2,1)S(1)}, f32[384,256]{1,0:T(8,128)S(1)}, f32[8,256]{1,0:T(8,128)S(1)}, /*index=5*/f32[8,128]{1,0:T(8,128)S(1)}) custom-call(bf16[768,384]{1,0:T(8,128)(2,1)S(1)} %get-tuple-element.46.refs_0_, f32[384,768]{1,0:T(8,128)S(1)} %get-tuple-element.47.refs_1_, ...), custom_call_target="tpu_custom_call" | custom-call | flops 1 | bytes 1 | tf_op jit(solution)/shard_map/pallas_call | solution.py:280
  101.3 34.2 %shard_map.58 = (f32[384,768]{1,0:T(8,128)S(1)}, f32[8,768]{1,0:T(8,128)S(1)}, f32[384,256]{1,0:T(8,128)S(1)}, f32[8,256]{1,0:T(8,128)S(1)}, f32[8,128]{1,0:T(8,128)S(1)}) custom-call(bf16[768,384]{1,0:T(8,128)(2,1)S(1)} %get-tuple-element.46.refs_0_, f32[384,768]{1,0:T(8,128)S(1)} %get-tuple-element.53.refs_1_, f32[8,768]{1,0:T(8,128)S(1)} %get-tuple-element.54.refs_2_, ...), custom_call_target="tpu_custom_call" | custom-call | flops 1 | bytes 1 | tf_op jit(solution)/shard_map/pallas_call | solution.py:280
  135.5 26.4 %shard_map.59 = (f32[384,768]{1,0:T(8,128)S(1)}, f32[8,768]{1,0:T(8,128)S(1)}, f32[384,256]{1,0:T(8,128)S(1)}, f32[8,256]{1,0:T(8,128)S(1)}, f32[8,128]{1,0:T(8,128)}, /*index=5*/bf16[240,512]{1,0:T(8,128)(2,1)S(1)}) custom-call(bf16[768,384]{1,0:T(8,128)(2,1)S(1)} %get-tuple-element.46.refs_0_, f32[384,768]{1,0:T(8,128)S(1)} %get-tuple-element.61.refs_1_, ...), custom_call_target="tpu_custom_call" | custom-call | flops 1 | bytes 1 | tf_op jit(solution)/shard_map/pallas_call | solution.py:280
  161.9 1.5 collective-permute-done.14.refs_4_
  163.8 2.1 %collective-permute-start.17 = (bf16[192,128]{1,0:T(8,128)(2,1)S(1)}, bf16[192,128]{1,0:T(8,128)(2,1)S(1)}, u32[]{:S(2)}, u32[]{:S(2)}) collective-permute-start(bf16[192,128]{1,0:T(8,128)(2,1)S(1)} %get-tuple-element.74), channel_id=1, source_target_pairs={{0,6},{1,7},{2,4},{3,5},{4,2},{5,3},{6,0},{7,1},{8,14},{9,15},{10,... | collective-permute-start | bytes 147464 | tf_op jit(solution)/shard_map/ppermute | solution.py:368
  165.9 1.2 collective-permute-start.15
  167.2 2.9 %collective-permute-done.16.refs_2_ = bf16[192,128]{1,0:T(8,128)(2,1)S(1)} collective-permute-done((bf16[192,128]{1,0:T(8,128)(2,1)S(1)}, bf16[192,128]{1,0:T(8,128)(2,1)S(1)}, u32[]{:S(2)}, u32[]{:S(2)}) %collective-permute-start.16) | collective-permute-done | bytes 49184 | tf_op jit(solution)/shard_map/ppermute | solution.py:368
  170.1 0.8 collective-permute-done.15.refs_1_
  170.9 1.1 shard_map.62
  (32 shorter events, 1.2 us)
Async XLA Ops:
  1.6 13.3 %collective-permute-start = (bf16[192,384]{1,0:T(8,128)(2,1)S(1)}, bf16[192,384]{1,0:T(8,128)(2,1)S(1)}, u32[]{:S(2)}, u32[]{:S(2)}) collective-permute-start(bf16[192,384]{1,0:T(8,128)(2,1)S(1)} %get-tuple-element.41), channel_id=1, source_target_pairs={{0,2},{1,3},{2,0},{3,1},{4,6},{5,7},{6,4},{7,5},{8,10},{9,11},{10,... | collective-permute-start | bytes 442376 | tf_op jit(solution)/shard_map/ppermute | solution.py:368
  4.7 10.2 %collective-permute-start.1 = (bf16[192,384]{1,0:T(8,128)(2,1)S(1)}, bf16[192,384]{1,0:T(8,128)(2,1)S(1)}, u32[]{:S(2)}, u32[]{:S(2)}) collective-permute-start(bf16[192,384]{1,0:T(8,128)(2,1)S(1)} %get-tuple-element.42), channel_id=1, source_target_pairs={{0,4},{1,5},{2,6},{3,7},{4,0},{5,1},{6,2},{7,3},{8,12},{9,13},{10,... | collective-permute-start | bytes 442376 | tf_op jit(solution)/shard_map/ppermute | solution.py:368
  7.3 5.9 %collective-permute-start.2 = (bf16[128,384]{1,0:T(8,128)(2,1)S(1)}, bf16[128,384]{1,0:T(8,128)(2,1)S(1)}, u32[]{:S(2)}, u32[]{:S(2)}) collective-permute-start(bf16[128,384]{1,0:T(8,128)(2,1)S(1)} %slice.25.refs_2_.refs_5_), channel_id=1, source_target_pairs={{0,24},{8,16},{16,8},{24,0},{1,25},{9,17},{17,9},{25,1},{2,26},{10... | collective-permute-start | bytes 294920 | tf_op jit(solution)/shard_map/ppermute | solution.py:377
  9.8 4.7 %collective-permute-start.3 = (bf16[128,384]{1,0:T(8,128)(2,1)S(1)}, bf16[128,384]{1,0:T(8,128)(2,1)S(1)}, u32[]{:S(2)}, u32[]{:S(2)}) collective-permute-start(bf16[128,384]{1,0:T(8,128)(2,1)S(1)} %slice.25.refs_2_.refs_5_), channel_id=1, source_target_pairs={{0,16},{8,24},{16,0},{24,8},{1,17},{9,25},{17,1},{25,9},{2,18},{10... | collective-permute-start | bytes 294920 | tf_op jit(solution)/shard_map/ppermute | solution.py:377
  10.3 4.6 %collective-permute-start.4 = (bf16[128,384]{1,0:T(8,128)(2,1)S(1)}, bf16[128,384]{1,0:T(8,128)(2,1)S(1)}, u32[]{:S(2)}, u32[]{:S(2)}) collective-permute-start(bf16[128,384]{1,0:T(8,128)(2,1)S(1)} %slice.25.refs_2_.refs_5_), channel_id=1, source_target_pairs={{0,8},{8,0},{16,24},{24,16},{1,9},{9,1},{17,25},{25,17},{2,10},{10... | collective-permute-start | bytes 294920 | tf_op jit(solution)/shard_map/ppermute | solution.py:377
  15.0 1.8 %collective-permute-start.5 = (bf16[192,384]{1,0:T(8,128)(2,1)S(1)}, bf16[192,384]{1,0:T(8,128)(2,1)S(1)}, u32[]{:S(2)}, u32[]{:S(2)}) collective-permute-start(bf16[192,384]{1,0:T(8,128)(2,1)S(1)} %pad_maximum_fusion.1.refs_0_), channel_id=1, source_target_pairs={{0,1},{1,0},{2,3},{3,2},{4,5},{5,4},{6,7},{7,6},{8,9},{9,8},{10,11... | collective-permute-start | bytes 442376 | tf_op jit(solution)/shard_map/ppermute | solution.py:371
  15.1 43.7 %collective-permute-start.6 = (bf16[192,384]{1,0:T(8,128)(2,1)S(1)}, bf16[192,384]{1,0:T(8,128)(2,1)S(1)}, u32[]{:S(2)}, u32[]{:S(2)}) collective-permute-start(bf16[192,384]{1,0:T(8,128)(2,1)S(1)} %get-tuple-element.50), channel_id=1, source_target_pairs={{0,6},{1,7},{2,4},{3,5},{4,2},{5,3},{6,0},{7,1},{8,14},{9,15},{10,... | collective-permute-start | bytes 442376 | tf_op jit(solution)/shard_map/ppermute | solution.py:368
  16.8 43.3 %collective-permute-start.8 = (bf16[256,384]{1,0:T(8,128)(2,1)S(1)}, bf16[256,384]{1,0:T(8,128)(2,1)S(1)}, u32[]{:S(2)}, u32[]{:S(2)}) collective-permute-start(bf16[256,384]{1,0:T(8,128)(2,1)S(1)} %pad_maximum_fusion.refs_3_.refs_6_), channel_id=1, source_target_pairs={{0,24},{8,16},{16,8},{24,0},{1,25},{9,17},{17,9},{25,1},{2,26},{10... | collective-permute-start | bytes 589832 | tf_op jit(solution)/shard_map/ppermute | solution.py:377
  19.4 81.9 %collective-permute-start.10 = (bf16[256,384]{1,0:T(8,128)(2,1)S(1)}, bf16[256,384]{1,0:T(8,128)(2,1)S(1)}, u32[]{:S(2)}, u32[]{:S(2)}) collective-permute-start(bf16[256,384]{1,0:T(8,128)(2,1)S(1)} %pad_maximum_fusion.refs_3_.refs_6_), channel_id=1, source_target_pairs={{0,16},{8,24},{16,0},{24,8},{1,17},{9,25},{17,1},{25,9},{2,18},{10... | collective-permute-start | bytes 589832 | tf_op jit(solution)/shard_map/ppermute | solution.py:377
  19.9 81.4 %collective-permute-start.9 = (bf16[256,384]{1,0:T(8,128)(2,1)S(1)}, bf16[256,384]{1,0:T(8,128)(2,1)S(1)}, u32[]{:S(2)}, u32[]{:S(2)}) collective-permute-start(bf16[256,384]{1,0:T(8,128)(2,1)S(1)} %pad_maximum_fusion.refs_3_.refs_6_), channel_id=1, source_target_pairs={{0,8},{8,0},{16,24},{24,16},{1,9},{9,1},{17,25},{25,17},{2,10},{10... | collective-permute-start | bytes 589832 | tf_op jit(solution)/shard_map/ppermute | solution.py:377
  58.9 1.3 collective-permute-start.7
  58.9 76.5 %collective-permute-start.11 = (bf16[128,384]{1,0:T(8,128)(2,1)S(1)}, bf16[128,384]{1,0:T(8,128)(2,1)S(1)}, u32[]{:S(2)}, u32[]{:S(2)}) collective-permute-start(bf16[128,384]{1,0:T(8,128)(2,1)S(1)} %slice.31.refs_10_), channel_id=1, source_target_pairs={{0,24},{8,16},{16,8},{24,0},{1,25},{9,17},{17,9},{25,1},{2,26},{10... | collective-permute-start | bytes 294920 | tf_op jit(solution)/shard_map/ppermute | solution.py:377
  60.1 75.3 %collective-permute-start.12 = (bf16[128,384]{1,0:T(8,128)(2,1)S(1)}, bf16[128,384]{1,0:T(8,128)(2,1)S(1)}, u32[]{:S(2)}, u32[]{:S(2)}) collective-permute-start(bf16[128,384]{1,0:T(8,128)(2,1)S(1)} %slice.31.refs_10_), channel_id=1, source_target_pairs={{0,16},{8,24},{16,0},{24,8},{1,17},{9,25},{17,1},{25,9},{2,18},{10... | collective-permute-start | bytes 294920 | tf_op jit(solution)/shard_map/ppermute | solution.py:377
  60.2 75.4 %collective-permute-start.13 = (bf16[128,384]{1,0:T(8,128)(2,1)S(1)}, bf16[128,384]{1,0:T(8,128)(2,1)S(1)}, u32[]{:S(2)}, u32[]{:S(2)}) collective-permute-start(bf16[128,384]{1,0:T(8,128)(2,1)S(1)} %slice.31.refs_10_), channel_id=1, source_target_pairs={{0,8},{8,0},{16,24},{24,16},{1,9},{9,1},{17,25},{25,17},{2,10},{10... | collective-permute-start | bytes 294920 | tf_op jit(solution)/shard_map/ppermute | solution.py:377
  161.9 1.5 collective-permute-start.14
  163.5 7.5 %copy-start = (bf16[768,768]{1,0:T(8,128)(2,1)S(1)}, bf16[768,768]{1,0:T(8,128)(2,1)}, u32[]{:S(2)}) copy-start(bf16[768,768]{1,0:T(8,128)(2,1)} %refs_4_.1) | copy-start | bytes 3538948
  163.5 6.6 %collective-permute-start.16 = (bf16[192,128]{1,0:T(8,128)(2,1)S(1)}, bf16[192,128]{1,0:T(8,128)(2,1)S(1)}, u32[]{:S(2)}, u32[]{:S(2)}) collective-permute-start(bf16[192,128]{1,0:T(8,128)(2,1)S(1)} %get-tuple-element.73), channel_id=1, source_target_pairs={{0,4},{1,5},{2,6},{3,7},{4,0},{5,1},{6,2},{7,3},{8,12},{9,13},{10,... | collective-permute-start | bytes 147464 | tf_op jit(solution)/shard_map/ppermute | solution.py:368
  163.8 6.3 %collective-permute-start.17 = (bf16[192,128]{1,0:T(8,128)(2,1)S(1)}, bf16[192,128]{1,0:T(8,128)(2,1)S(1)}, u32[]{:S(2)}, u32[]{:S(2)}) collective-permute-start(bf16[192,128]{1,0:T(8,128)(2,1)S(1)} %get-tuple-element.74), channel_id=1, source_target_pairs={{0,6},{1,7},{2,4},{3,5},{4,2},{5,3},{6,0},{7,1},{8,14},{9,15},{10,... | collective-permute-start | bytes 147464 | tf_op jit(solution)/shard_map/ppermute | solution.py:368
  165.9 5.0 %collective-permute-start.15 = (bf16[192,128]{1,0:T(8,128)(2,1)S(1)}, bf16[192,128]{1,0:T(8,128)(2,1)S(1)}, u32[]{:S(2)}, u32[]{:S(2)}) collective-permute-start(bf16[192,128]{1,0:T(8,128)(2,1)S(1)} %get-tuple-element.72), channel_id=1, source_target_pairs={{0,2},{1,3},{2,0},{3,1},{4,6},{5,7},{6,4},{7,5},{8,10},{9,11},{10,... | collective-permute-start | bytes 147464 | tf_op jit(solution)/shard_map/ppermute | solution.py:368

commit v8 on v6

--- a/solution.py
+++ b/solution.py
@@ -338,24 +338,23 @@
 
 
 def project_kernel(rest, *refs):
-    parts, w_ref, out = refs[:GROUPS], refs[GROUPS], refs[GROUPS + 1]
+    parts, w_ref, out, joined = refs[:GROUPS], refs[GROUPS], refs[GROUPS + 1], refs[GROUPS + 2]
     mine = lax.axis_index("inner") // rest
     rows = parts[0].shape[0]
-    total = None
     for s, part in enumerate(parts):
-        g = jnp.bitwise_xor(mine, s)
-        w = w_ref[pl.ds(pl.multiple_of(g * rows, 16), rows), :]
-        term = lax.dot_general(part[...], w, TN, preferred_element_type=F32)
-        total = term if total is None else total + term
-    out[...] = total.astype(BF16)
+        start = pl.multiple_of(jnp.bitwise_xor(mine, s) * rows, 16)
+        joined[pl.ds(start, rows), :] = part[...]
+    out[...] = lax.dot_general(joined[...], w_ref[...], TN, preferred_element_type=F32).astype(BF16)
 
 
 def project(parts, w, rest):
+    rows, cols = parts[0].shape
     return pl.pallas_call(
         functools.partial(project_kernel, rest),
-        out_shape=jax.ShapeDtypeStruct((parts[0].shape[1], w.shape[1]), BF16),
+        out_shape=jax.ShapeDtypeStruct((cols, w.shape[1]), BF16),
         in_specs=[VMEM] * (GROUPS + 1),
         out_specs=VMEM,
+        scratch_shapes=[pltpu.VMEM((GROUPS * rows, cols), BF16)],
         compiler_params=params(),
     )(*parts, w)
 

time: 171 us -> 171 us (level)
  no operation moved by 1% of the time
where the time goes in v8:
time: 171 us
  Pallas kernels  139 us (81%)
  starting transfers between devices  20.7 us (12%)
  waiting for transfers between devices  10.5 us (6%)
    pallas_call x4, Pallas kernels, attend(): pl.pallas_call(functools.partial(attend_kernel, meta, len(kv_list), half,...  136 us
    ppermute x6, starting transfers between devices, over_groups(): lax.ppermute(x, 'inner', [(i, (i // rest ^ s) * rest + i % rest) for i in...  11 us
    ppermute x9, starting transfers between devices, plane(): lax.ppermute(chunk, 'blk', [(b, b ^ d) for b in range(n_blk)])  9.54 us
    ppermute x9, waiting for transfers between devices, plane(): lax.ppermute(chunk, 'blk', [(b, b ^ d) for b in range(n_blk)])  4.09 us
    ppermute x6, waiting for transfers between devices, over_groups(): lax.ppermute(x, 'inner', [(i, (i // rest ^ s) * rest + i % rest) for i in...  3.78 us
  transfers between devices with their start and end apart: 18, of which 7 were waited for; matrix products, arithmetic and copies ran while one was open for 0% of the time, Pallas kernels for 64%

profile of v8, /device:TPU:0, one launch (start us, length us, event | category | flops | bytes accessed | tf_op | source)
XLA Modules:
  0.0 170.6 jit_solution(7521901630724525740)
XLA Ops:
  0.0 1.6 shard_map.55
  1.6 3.1 %collective-permute-start = (bf16[192,384]{1,0:T(8,128)(2,1)S(1)}, bf16[192,384]{1,0:T(8,128)(2,1)S(1)}, u32[]{:S(2)}, u32[]{:S(2)}) collective-permute-start(bf16[192,384]{1,0:T(8,128)(2,1)S(1)} %get-tuple-element.42), channel_id=1, source_target_pairs={{0,2},{1,3},{2,0},{3,1},{4,6},{5,7},{6,4},{7,5},{8,10},{9,11},{10,... | collective-permute-start | bytes 442376 | tf_op jit(solution)/shard_map/ppermute | solution.py:367
  4.7 2.6 %collective-permute-start.1 = (bf16[192,384]{1,0:T(8,128)(2,1)S(1)}, bf16[192,384]{1,0:T(8,128)(2,1)S(1)}, u32[]{:S(2)}, u32[]{:S(2)}) collective-permute-start(bf16[192,384]{1,0:T(8,128)(2,1)S(1)} %get-tuple-element.43), channel_id=1, source_target_pairs={{0,4},{1,5},{2,6},{3,7},{4,0},{5,1},{6,2},{7,3},{8,12},{9,13},{10,... | collective-permute-start | bytes 442376 | tf_op jit(solution)/shard_map/ppermute | solution.py:367
  7.3 2.5 %collective-permute-start.2 = (bf16[128,384]{1,0:T(8,128)(2,1)S(1)}, bf16[128,384]{1,0:T(8,128)(2,1)S(1)}, u32[]{:S(2)}, u32[]{:S(2)}) collective-permute-start(bf16[128,384]{1,0:T(8,128)(2,1)S(1)} %slice.25.refs_2_.refs_5_), channel_id=1, source_target_pairs={{0,24},{8,16},{16,8},{24,0},{1,25},{9,17},{17,9},{25,1},{2,26},{10... | collective-permute-start | bytes 294920 | tf_op jit(solution)/shard_map/ppermute | solution.py:376
  9.8 0.5 collective-permute-start.3
  10.3 0.5 collective-permute-start.4
  10.9 2.4 %collective-permute-done.2.refs_4_.refs_7_ = bf16[128,384]{1,0:T(8,128)(2,1)S(1)} collective-permute-done((bf16[128,384]{1,0:T(8,128)(2,1)S(1)}, bf16[128,384]{1,0:T(8,128)(2,1)S(1)}, u32[]{:S(2)}, u32[]{:S(2)}) %collective-permute-start.2) | collective-permute-done | bytes 98336 | tf_op jit(solution)/shard_map/ppermute | solution.py:376
  13.2 1.3 collective-permute-done.3.refs_5_.refs_8_
  15.1 1.7 collective-permute-start.6
  16.8 2.5 %collective-permute-start.10 = (bf16[256,384]{1,0:T(8,128)(2,1)S(1)}, bf16[256,384]{1,0:T(8,128)(2,1)S(1)}, u32[]{:S(2)}, u32[]{:S(2)}) collective-permute-start(bf16[256,384]{1,0:T(8,128)(2,1)S(1)} %pad_maximum_fusion.refs_3_.refs_6_), channel_id=1, source_target_pairs={{0,24},{8,16},{16,8},{24,0},{1,25},{9,17},{17,9},{25,1},{2,26},{10... | collective-permute-start | bytes 589832 | tf_op jit(solution)/shard_map/ppermute | solution.py:376
  19.4 0.5 collective-permute-start.8
  19.9 0.5 collective-permute-start.9
  20.4 38.5 %shard_map.56 = (bf16[768,384]{1,0:T(8,128)(2,1)S(1)}, f32[384,768]{1,0:T(8,128)S(1)}, f32[8,768]{1,0:T(8,128)S(1)}, f32[8,128]{1,0:T(8,128)S(1)}) custom-call(bf16[192,384]{1,0:T(8,128)(2,1)S(1)} %pad_maximum_fusion.1.refs_0_, bf16[192,384]{1,0:T(8,128)(2,1)S(1)} %collective-permute-done.5.refs_1_, bf16[128,384]{1,0:T(8,128)(2,1)S(1)} %slice.25.refs_2_.refs_5_, ...), custom_call_target="tpu_custom_call" | custom-call | flops 1 | bytes 1 | tf_op jit(solution)/shard_map/pallas_call | solution.py:280
  59.1 1.1 collective-permute-done.7.refs_4_
  60.2 2.4 %collective-permute-start.13 = (bf16[128,384]{1,0:T(8,128)(2,1)S(1)}, bf16[128,384]{1,0:T(8,128)(2,1)S(1)}, u32[]{:S(2)}, u32[]{:S(2)}) collective-permute-start(bf16[128,384]{1,0:T(8,128)(2,1)S(1)} %slice.31.refs_10_), channel_id=1, source_target_pairs={{0,8},{8,0},{16,24},{24,16},{1,9},{9,1},{17,25},{25,17},{2,10},{10... | collective-permute-start | bytes 294920 | tf_op jit(solution)/shard_map/ppermute | solution.py:376
  62.6 20.4 %shard_map.57 = (f32[384,768]{1,0:T(8,128)S(1)}, f32[8,768]{1,0:T(8,128)S(1)}, bf16[256,384]{1,0:T(8,128)(2,1)S(1)}, f32[384,256]{1,0:T(8,128)S(1)}, f32[8,256]{1,0:T(8,128)S(1)}, /*index=5*/f32[8,128]{1,0:T(8,128)S(1)}) custom-call(bf16[768,384]{1,0:T(8,128)(2,1)S(1)} %get-tuple-element.47.refs_0_, f32[384,768]{1,0:T(8,128)S(1)} %get-tuple-element.48.refs_1_, ...), custom_call_target="tpu_custom_call" | custom-call | flops 1 | bytes 1 | tf_op jit(solution)/shard_map/pallas_call | solution.py:280
  83.0 51.0 %shard_map.58 = (f32[384,768]{1,0:T(8,128)S(1)}, f32[8,768]{1,0:T(8,128)S(1)}, f32[384,256]{1,0:T(8,128)S(1)}, f32[8,256]{1,0:T(8,128)S(1)}, f32[8,128]{1,0:T(8,128)S(1)}) custom-call(bf16[768,384]{1,0:T(8,128)(2,1)S(1)} %get-tuple-element.47.refs_0_, f32[384,768]{1,0:T(8,128)S(1)} %get-tuple-element.54.refs_1_, f32[8,768]{1,0:T(8,128)S(1)} %get-tuple-element.55.refs_2_, ...), custom_call_target="tpu_custom_call" | custom-call | flops 1 | bytes 1 | tf_op jit(solution)/shard_map/pallas_call | solution.py:280
  134.1 26.4 %shard_map.59 = (f32[384,768]{1,0:T(8,128)S(1)}, f32[8,768]{1,0:T(8,128)S(1)}, f32[384,256]{1,0:T(8,128)S(1)}, f32[8,256]{1,0:T(8,128)S(1)}, f32[8,128]{1,0:T(8,128)}, /*index=5*/bf16[240,512]{1,0:T(8,128)(2,1)S(1)}) custom-call(bf16[768,384]{1,0:T(8,128)(2,1)S(1)} %get-tuple-element.47.refs_0_, f32[384,768]{1,0:T(8,128)S(1)} %get-tuple-element.63.refs_1_, ...), custom_call_target="tpu_custom_call" | custom-call | flops 1 | bytes 1 | tf_op jit(solution)/shard_map/pallas_call | solution.py:280
  160.5 1.5 collective-permute-done.14.refs_4_
  162.4 2.0 %collective-permute-start.17 = (bf16[192,128]{1,0:T(8,128)(2,1)S(1)}, bf16[192,128]{1,0:T(8,128)(2,1)S(1)}, u32[]{:S(2)}, u32[]{:S(2)}) collective-permute-start(bf16[192,128]{1,0:T(8,128)(2,1)S(1)} %get-tuple-element.76), channel_id=1, source_target_pairs={{0,6},{1,7},{2,4},{3,5},{4,2},{5,3},{6,0},{7,1},{8,14},{9,15},{10,... | collective-permute-start | bytes 147464 | tf_op jit(solution)/shard_map/ppermute | solution.py:367
  164.5 1.2 collective-permute-start.15
  165.7 2.9 %collective-permute-done.16.refs_2_ = bf16[192,128]{1,0:T(8,128)(2,1)S(1)} collective-permute-done((bf16[192,128]{1,0:T(8,128)(2,1)S(1)}, bf16[192,128]{1,0:T(8,128)(2,1)S(1)}, u32[]{:S(2)}, u32[]{:S(2)}) %collective-permute-start.16) | collective-permute-done | bytes 49184 | tf_op jit(solution)/shard_map/ppermute | solution.py:367
  168.7 0.8 collective-permute-done.15.refs_1_
  169.5 1.1 shard_map.62
  (32 shorter events, 1.2 us)
Async XLA Ops:
  1.6 13.3 %collective-permute-start = (bf16[192,384]{1,0:T(8,128)(2,1)S(1)}, bf16[192,384]{1,0:T(8,128)(2,1)S(1)}, u32[]{:S(2)}, u32[]{:S(2)}) collective-permute-start(bf16[192,384]{1,0:T(8,128)(2,1)S(1)} %get-tuple-element.42), channel_id=1, source_target_pairs={{0,2},{1,3},{2,0},{3,1},{4,6},{5,7},{6,4},{7,5},{8,10},{9,11},{10,... | collective-permute-start | bytes 442376 | tf_op jit(solution)/shard_map/ppermute | solution.py:367
  4.7 10.2 %collective-permute-start.1 = (bf16[192,384]{1,0:T(8,128)(2,1)S(1)}, bf16[192,384]{1,0:T(8,128)(2,1)S(1)}, u32[]{:S(2)}, u32[]{:S(2)}) collective-permute-start(bf16[192,384]{1,0:T(8,128)(2,1)S(1)} %get-tuple-element.43), channel_id=1, source_target_pairs={{0,4},{1,5},{2,6},{3,7},{4,0},{5,1},{6,2},{7,3},{8,12},{9,13},{10,... | collective-permute-start | bytes 442376 | tf_op jit(solution)/shard_map/ppermute | solution.py:367
  7.3 5.9 %collective-permute-start.2 = (bf16[128,384]{1,0:T(8,128)(2,1)S(1)}, bf16[128,384]{1,0:T(8,128)(2,1)S(1)}, u32[]{:S(2)}, u32[]{:S(2)}) collective-permute-start(bf16[128,384]{1,0:T(8,128)(2,1)S(1)} %slice.25.refs_2_.refs_5_), channel_id=1, source_target_pairs={{0,24},{8,16},{16,8},{24,0},{1,25},{9,17},{17,9},{25,1},{2,26},{10... | collective-permute-start | bytes 294920 | tf_op jit(solution)/shard_map/ppermute | solution.py:376
  9.8 4.7 %collective-permute-start.3 = (bf16[128,384]{1,0:T(8,128)(2,1)S(1)}, bf16[128,384]{1,0:T(8,128)(2,1)S(1)}, u32[]{:S(2)}, u32[]{:S(2)}) collective-permute-start(bf16[128,384]{1,0:T(8,128)(2,1)S(1)} %slice.25.refs_2_.refs_5_), channel_id=1, source_target_pairs={{0,16},{8,24},{16,0},{24,8},{1,17},{9,25},{17,1},{25,9},{2,18},{10... | collective-permute-start | bytes 294920 | tf_op jit(solution)/shard_map/ppermute | solution.py:376
  10.3 4.6 %collective-permute-start.4 = (bf16[128,384]{1,0:T(8,128)(2,1)S(1)}, bf16[128,384]{1,0:T(8,128)(2,1)S(1)}, u32[]{:S(2)}, u32[]{:S(2)}) collective-permute-start(bf16[128,384]{1,0:T(8,128)(2,1)S(1)} %slice.25.refs_2_.refs_5_), channel_id=1, source_target_pairs={{0,8},{8,0},{16,24},{24,16},{1,9},{9,1},{17,25},{25,17},{2,10},{10... | collective-permute-start | bytes 294920 | tf_op jit(solution)/shard_map/ppermute | solution.py:376
  15.0 1.8 %collective-permute-start.5 = (bf16[192,384]{1,0:T(8,128)(2,1)S(1)}, bf16[192,384]{1,0:T(8,128)(2,1)S(1)}, u32[]{:S(2)}, u32[]{:S(2)}) collective-permute-start(bf16[192,384]{1,0:T(8,128)(2,1)S(1)} %pad_maximum_fusion.1.refs_0_), channel_id=1, source_target_pairs={{0,1},{1,0},{2,3},{3,2},{4,5},{5,4},{6,7},{7,6},{8,9},{9,8},{10,11... | collective-permute-start | bytes 442376 | tf_op jit(solution)/shard_map/ppermute | solution.py:370
  15.1 43.8 %collective-permute-start.6 = (bf16[192,384]{1,0:T(8,128)(2,1)S(1)}, bf16[192,384]{1,0:T(8,128)(2,1)S(1)}, u32[]{:S(2)}, u32[]{:S(2)}) collective-permute-start(bf16[192,384]{1,0:T(8,128)(2,1)S(1)} %get-tuple-element.51), channel_id=1, source_target_pairs={{0,6},{1,7},{2,4},{3,5},{4,2},{5,3},{6,0},{7,1},{8,14},{9,15},{10,... | collective-permute-start | bytes 442376 | tf_op jit(solution)/shard_map/ppermute | solution.py:367
  16.8 43.4 %collective-permute-start.10 = (bf16[256,384]{1,0:T(8,128)(2,1)S(1)}, bf16[256,384]{1,0:T(8,128)(2,1)S(1)}, u32[]{:S(2)}, u32[]{:S(2)}) collective-permute-start(bf16[256,384]{1,0:T(8,128)(2,1)S(1)} %pad_maximum_fusion.refs_3_.refs_6_), channel_id=1, source_target_pairs={{0,24},{8,16},{16,8},{24,0},{1,25},{9,17},{17,9},{25,1},{2,26},{10... | collective-permute-start | bytes 589832 | tf_op jit(solution)/shard_map/ppermute | solution.py:376
  19.4 63.7 %collective-permute-start.8 = (bf16[256,384]{1,0:T(8,128)(2,1)S(1)}, bf16[256,384]{1,0:T(8,128)(2,1)S(1)}, u32[]{:S(2)}, u32[]{:S(2)}) collective-permute-start(bf16[256,384]{1,0:T(8,128)(2,1)S(1)} %pad_maximum_fusion.refs_3_.refs_6_), channel_id=1, source_target_pairs={{0,8},{8,0},{16,24},{24,16},{1,9},{9,1},{17,25},{25,17},{2,10},{10... | collective-permute-start | bytes 589832 | tf_op jit(solution)/shard_map/ppermute | solution.py:376
  19.9 63.1 %collective-permute-start.9 = (bf16[256,384]{1,0:T(8,128)(2,1)S(1)}, bf16[256,384]{1,0:T(8,128)(2,1)S(1)}, u32[]{:S(2)}, u32[]{:S(2)}) collective-permute-start(bf16[256,384]{1,0:T(8,128)(2,1)S(1)} %pad_maximum_fusion.refs_3_.refs_6_), channel_id=1, source_target_pairs={{0,16},{8,24},{16,0},{24,8},{1,17},{9,25},{17,1},{25,9},{2,18},{10... | collective-permute-start | bytes 589832 | tf_op jit(solution)/shard_map/ppermute | solution.py:376
  58.9 1.3 collective-permute-start.7
  59.0 75.0 %collective-permute-start.11 = (bf16[128,384]{1,0:T(8,128)(2,1)S(1)}, bf16[128,384]{1,0:T(8,128)(2,1)S(1)}, u32[]{:S(2)}, u32[]{:S(2)}) collective-permute-start(bf16[128,384]{1,0:T(8,128)(2,1)S(1)} %slice.31.refs_10_), channel_id=1, source_target_pairs={{0,24},{8,16},{16,8},{24,0},{1,25},{9,17},{17,9},{25,1},{2,26},{10... | collective-permute-start | bytes 294920 | tf_op jit(solution)/shard_map/ppermute | solution.py:376
  60.2 73.8 %collective-permute-start.12 = (bf16[128,384]{1,0:T(8,128)(2,1)S(1)}, bf16[128,384]{1,0:T(8,128)(2,1)S(1)}, u32[]{:S(2)}, u32[]{:S(2)}) collective-permute-start(bf16[128,384]{1,0:T(8,128)(2,1)S(1)} %slice.31.refs_10_), channel_id=1, source_target_pairs={{0,16},{8,24},{16,0},{24,8},{1,17},{9,25},{17,1},{25,9},{2,18},{10... | collective-permute-start | bytes 294920 | tf_op jit(solution)/shard_map/ppermute | solution.py:376
  60.2 73.8 %collective-permute-start.13 = (bf16[128,384]{1,0:T(8,128)(2,1)S(1)}, bf16[128,384]{1,0:T(8,128)(2,1)S(1)}, u32[]{:S(2)}, u32[]{:S(2)}) collective-permute-start(bf16[128,384]{1,0:T(8,128)(2,1)S(1)} %slice.31.refs_10_), channel_id=1, source_target_pairs={{0,8},{8,0},{16,24},{24,16},{1,9},{9,1},{17,25},{25,17},{2,10},{10... | collective-permute-start | bytes 294920 | tf_op jit(solution)/shard_map/ppermute | solution.py:376
  160.5 1.5 collective-permute-start.14
  162.0 7.5 %copy-start = (bf16[768,768]{1,0:T(8,128)(2,1)S(1)}, bf16[768,768]{1,0:T(8,128)(2,1)}, u32[]{:S(2)}) copy-start(bf16[768,768]{1,0:T(8,128)(2,1)} %refs_4_.1) | copy-start | bytes 3538948
  162.1 6.6 %collective-permute-start.16 = (bf16[192,128]{1,0:T(8,128)(2,1)S(1)}, bf16[192,128]{1,0:T(8,128)(2,1)S(1)}, u32[]{:S(2)}, u32[]{:S(2)}) collective-permute-start(bf16[192,128]{1,0:T(8,128)(2,1)S(1)} %get-tuple-element.75), channel_id=1, source_target_pairs={{0,4},{1,5},{2,6},{3,7},{4,0},{5,1},{6,2},{7,3},{8,12},{9,13},{10,... | collective-permute-start | bytes 147464 | tf_op jit(solution)/shard_map/ppermute | solution.py:367
  162.4 6.3 %collective-permute-start.17 = (bf16[192,128]{1,0:T(8,128)(2,1)S(1)}, bf16[192,128]{1,0:T(8,128)(2,1)S(1)}, u32[]{:S(2)}, u32[]{:S(2)}) collective-permute-start(bf16[192,128]{1,0:T(8,128)(2,1)S(1)} %get-tuple-element.76), channel_id=1, source_target_pairs={{0,6},{1,7},{2,4},{3,5},{4,2},{5,3},{6,0},{7,1},{8,14},{9,15},{10,... | collective-permute-start | bytes 147464 | tf_op jit(solution)/shard_map/ppermute | solution.py:367
  164.5 5.0 %collective-permute-start.15 = (bf16[192,128]{1,0:T(8,128)(2,1)S(1)}, bf16[192,128]{1,0:T(8,128)(2,1)S(1)}, u32[]{:S(2)}, u32[]{:S(2)}) collective-permute-start(bf16[192,128]{1,0:T(8,128)(2,1)S(1)} %get-tuple-element.74), channel_id=1, source_target_pairs={{0,2},{1,3},{2,0},{3,1},{4,6},{5,7},{6,4},{7,5},{8,10},{9,11},{10,... | collective-permute-start | bytes 147464 | tf_op jit(solution)/shard_map/ppermute | solution.py:367
